TPU v7x, 32 devices: a whole 2x2x4 slice. The times are simulated.
32 devices in a mesh: groups: 2 (over y), ep: 4 (over z), tp: 4 (over x, core).
Axes of the slice: x: 2, y: 2, z: 4, core: 2. Of those that a mesh axis runs over, the one named last changes fastest.
Arguments:
- tokens: bfloat16 [2, 512, 4096], P(None, ('groups', 'ep')), parts along dimension 1, may hold values from -6 to 6
- expert_ids: int32 [2, 512, 2], P(None, ('groups', 'ep')), parts along dimension 1, may hold values from 0 to 1, all different within a row
- gate_weights: float32 [2, 512, 2], P(None, ('groups', 'ep')), parts along dimension 1, may hold values from 0.05 to 1
- replica_pick: int32 [2, 512, 2], P(None, ('groups', 'ep')), parts along dimension 1, may hold values from 0 to 3
- placement: int32 [2, 4], replicated, may hold values from 0 to 1, as said below
- slot_limit: int32 [4], replicated, may hold values from 20 to 40, as said below
- expert_weights: bfloat16 [4, 3, 1536, 4096], P('ep', None, 'tp'), as said below
Outputs:
- layer_out: bfloat16 [2, 512, 4096], P(None, ('groups', 'ep'), 'tp'), parts along dimension 1
There are 2 independent parts, one for each index of `groups`. A program takes and returns all parts, laid end to end along the dimension named above; an argument that names none is the same for every part. Nothing has to cross between parts.
Inputs may be any that keep to these rules, and one draw needn't show every extreme that they name: `expert_ids`: each row names 2 different experts, and every expert is named somewhere. `placement`: row 0 is the old and row 1 the new slot-to-expert table. In each table every expert is held by one or more slots, and exactly 2 slots hold another expert in row 1 than in row 0. `slot_limit`: some slot has capacity exactly 40. `expert_weights`: slots that hold the same expert in the old table hold equal weights.
All inputs are finite; a program needn't handle non-finite values.
Results may differ from a plain program's by a relative error of at most 0.015.
Values may be sent and summed in bfloat16 or wider, within the bound.
No kernel may reach another device: no remote copies, remote signals or barrier semaphores. Data moves between devices by JAX's collectives and lax.ppermute only.
A program may use at most 128 MiB of HBM per device.

v0:
```python
import jax
import jax.numpy as jnp
from jax import lax
from jax.sharding import PartitionSpec as P


def broadcast(shard, axis, root):
    mine = lax.axis_index(axis) == root
    return lax.psum(jnp.where(mine, shard, jnp.zeros_like(shard)), axis)


def slot_choice(slot_table, chosen_ids, pick_values, slot_count):
    slot_range = jnp.arange(slot_count, dtype=jnp.int32)
    holders = (slot_table[None, None, :] == chosen_ids[:, :, None]).astype(jnp.int32)
    holder_count = jnp.sum(holders, axis=2)
    earlier = jnp.cumsum(holders, axis=2) - holders
    wanted = pick_values % holder_count
    matched = holders * (earlier == wanted[:, :, None]).astype(jnp.int32)
    return jnp.sum(matched * slot_range[None, None, :], axis=2)


def placements(slot_table, limits, chosen_ids, pick_values, block_rows, capacity):
    slot_count = slot_table.shape[0]
    chosen = slot_choice(slot_table, chosen_ids, pick_values, slot_count)
    row_count, top_count = chosen.shape
    blocked = chosen.reshape(row_count // block_rows, block_rows * top_count)
    onehot = (blocked[:, :, None] == jnp.arange(slot_count, dtype=jnp.int32)[None, None, :]).astype(
        jnp.int32
    )
    ranked = jnp.sum(onehot * (jnp.cumsum(onehot, axis=1) - onehot), axis=2)
    allowed = jnp.sum(onehot * limits[None, None, :], axis=2)
    located = jnp.where(ranked < allowed, blocked * capacity + ranked, slot_count * capacity)
    return located.reshape(row_count, top_count)


def feed_forward(inputs, weights):
    gate_proj = jnp.dot(inputs, weights[0].T, preferred_element_type=jnp.float32)
    upward = jnp.dot(inputs, weights[1].T, preferred_element_type=jnp.float32)
    hidden = (jax.nn.silu(gate_proj) * upward).astype(jnp.bfloat16)
    return jnp.dot(hidden, weights[2], preferred_element_type=jnp.float32)


def per_device(
    tokens, expert_ids, gate_weights, replica_pick, placement, slot_limit, expert_weights
):
    tok_rows = tokens.shape[1]
    model_width = tokens.shape[2]
    top_count = expert_ids.shape[2]
    slot_count = placement.shape[1]
    capacity = tok_rows * top_count * 5 // (4 * slot_count)
    column_count = model_width // lax.axis_size("tp")
    column_start = lax.axis_index("tp") * column_count
    own_weights = expert_weights[0]
    slot_range = jnp.arange(slot_count, dtype=jnp.int32)

    def run_span(span_id, weights):
        span_rows = tokens[span_id]
        located = placements(
            placement[span_id],
            slot_limit,
            expert_ids[span_id],
            replica_pick[span_id],
            tok_rows,
            capacity,
        )
        token_index = jnp.arange(tok_rows, dtype=jnp.int32)
        token_source = jnp.full((slot_count * capacity + 1,), tok_rows, jnp.int32)
        spread = jnp.broadcast_to(token_index[:, None], located.shape).reshape(-1)
        token_source = token_source.at[located.reshape(-1)].set(spread)[:-1]
        narrow = lax.dynamic_slice_in_dim(span_rows, column_start, column_count, 1)
        padded_rows = jnp.concatenate([narrow, jnp.zeros((1, column_count), jnp.bfloat16)])
        outgoing = padded_rows[token_source].reshape(slot_count, capacity, column_count)
        received = lax.all_to_all(outgoing, "ep", split_axis=0, concat_axis=0, tiled=True)
        received = lax.all_gather(received, "tp", axis=2, tiled=True)
        source_count = received.shape[0]
        item_count = received.shape[1]
        partial_out = feed_forward(
            received.reshape(source_count * item_count, model_width), weights
        )
        summed = lax.psum_scatter(
            partial_out.reshape(source_count, item_count, model_width).astype(jnp.bfloat16),
            "tp",
            scatter_dimension=2,
            tiled=True,
        )
        came_back = lax.all_to_all(summed, "ep", split_axis=0, concat_axis=0, tiled=True)
        flat_back = jnp.concatenate(
            [
                came_back.reshape(slot_count * capacity, column_count),
                jnp.zeros((1, column_count), jnp.bfloat16),
            ]
        )
        combined = jnp.zeros((tok_rows, column_count), jnp.float32)
        span_gates = gate_weights[span_id]
        for member in range(top_count):
            combined = combined + span_gates[:, member, None] * flat_back[
                located[:, member]
            ].astype(jnp.float32)
        return combined.astype(jnp.bfloat16)

    first_out = run_span(0, own_weights)
    old_table = placement[0]
    new_table = placement[1]
    changed = (old_table != new_table).astype(jnp.int32)
    running = jnp.cumsum(changed)
    own_slot = lax.axis_index("ep")
    result = own_weights
    for moving in range(max(2, lax.axis_size("ep") // 8)):
        target = jnp.sum(slot_range * changed * (running == moving + 1).astype(jnp.int32))
        wanted = jnp.sum(new_table * (slot_range == target).astype(jnp.int32))
        source = jnp.min(jnp.where(old_table == wanted, slot_range, slot_count))
        arrived = broadcast(own_weights, "ep", source)
        result = jnp.where(own_slot == target, arrived, result)
    second_out = run_span(1, result)
    return jnp.stack([first_out, second_out])


def solution(mesh):
    placed = (
        P(None, ("groups", "ep"), None),
        P(None, ("groups", "ep"), None),
        P(None, ("groups", "ep"), None),
        P(None, ("groups", "ep"), None),
        P(),
        P(),
        P("ep", None, "tp", None),
    )
    return jax.shard_map(
        per_device,
        mesh=mesh,
        in_specs=placed,
        out_specs=P(None, ("groups", "ep"), "tp"),
        check_vma=False,
    )
```

profile of v0, /device:TPU:0, one launch (start us, length us, event | category | flops | bytes accessed | tf_op | source)
XLA Modules:
  0.0 759.3 jit_solution(10539277624889024180)
XLA Ops:
  7.4 0.7 slice_bitcast_fusion.12
  8.1 0.8 slice_bitcast_fusion.19
  8.8 0.1 convert_reduce_fusion.1
  9.0 0.1 convert_reduce_fusion
  9.2 0.8 and_select_fusion.1
  10.0 0.1 fusion.27
  10.1 0.1 copy.16
  10.2 0.1 eq.183
  10.3 0.1 fusion.24
  10.4 0.2 reduce_window_sum.42
  10.6 0.1 fusion.30
  10.7 0.1 copy.21
  10.8 0.1 eq.195
  11.0 0.1 fusion.23
  11.1 0.2 reduce_window_sum.44
  11.2 0.9 select_reduce_fusion.3
  12.1 0.1 reduce_sum.130
  12.2 0.1 copy.18
  12.3 0.1 reduce_sum.131
  12.5 0.1 copy.19
  12.5 0.1 copy.17
  12.6 0.2 mul.186
  12.8 0.1 reduce_sum.142
  12.9 0.1 copy.23
  13.0 0.1 reduce_sum.143
  13.2 0.1 copy.24
  13.2 0.1 copy.22
  13.3 0.2 mul.201
  13.5 0.1 reshape.755
  13.7 1.3 fusion.48
  15.0 1.0 scatter_custom_fusion
  16.0 1.7 gather_fusion
  17.7 6.3 all-to-all-start
  24.0 0.2 reduce-window.9
  24.2 10.1 %all-to-all-done = bf16[4,40,1024]{2,1,0:T(8,128)(2,1)S(1)} async-done(((bf16[4,40,1024]{2,1,0:T(8,128)(2,1)}), bf16[4,40,1024]{2,1,0:T(8,128)(2,1)S(1)}, u32[]{:S(2)}, u32[]{:S(2)}) %all-to-all-start) | async-done | bytes 327712 | tf_op jit(solution)/shard_map/all_to_all | solution.py:73
  34.3 0.7 copy-done
  35.1 0.7 fusion.37
  35.8 1.2 fusion.34
  37.1 1.9 fusion.35
  38.9 1.2 fusion.33
  41.4 10.6 %bitcast_select_fusion.1 = (bf16[3,384,4096]{2,1,0:T(8,128)(2,1)}, bf16[3,384,4096]{2,1,0:T(8,128)(2,1)}) fusion(bf16[1,3,384,4096]{3,2,1,0:T(8,128)(2,1)} %param.13, pred[]{:T(512)S(6)} %eq.214, pred[]{:T(512)S(6)} %eq.206), kind=kLoop, calls=%fused_computation.9 | loop fusion | flops 9437184 | bytes 28311554 | tf_op jit(solution)/shard_map/jit(_where)/select_n | solution.py:9
  52.1 1.0 scatter_custom_fusion.1
  53.1 0.9 gather_fusion.3
  54.0 24.3 %all_to_all.20 = bf16[4,40,1024]{2,1,0:T(8,128)(2,1)} all-to-all(bf16[4,40,1024]{2,1,0:T(8,128)(2,1)S(1)} %bitcast.151), channel_id=1, replica_groups=mesh['groups'=2,'ep'=4,'tp'=4] {'ep'}, dimensions={0} | all-to-all | bytes 655360 | tf_op jit(solution)/shard_map/all_to_all | solution.py:73
  79.8 3.6 fusion.6
  83.3 3.1 fusion.16
  86.5 3.8 convolution_convert_fusion.1
  90.4 597.3 %all-reduce.7.cloned.1.call-done = (bf16[3,384,4096]{2,1,0:T(8,128)(2,1)}, bf16[3,384,4096]{2,1,0:T(8,128)(2,1)}) async-done(((bf16[3,384,4096]{2,1,0:T(8,128)(2,1)}, bf16[3,384,4096]{2,1,0:T(8,128)(2,1)}), (bf16[3,384,4096]{2,1,0:T(8,128)(2,1)}, bf16[3,384,4096]{2,1,0:T(8,128)(2,1)})) %all-reduce.7.cloned.1.call-update) | async-done | bytes 18874384 | tf_op jit(solution)/shard_map/psum | solution.py:9
  687.6 9.2 %fusion = bf16[3,384,4096]{2,1,0:T(8,128)(2,1)} fusion(bf16[3,384,4096]{2,1,0:T(8,128)(2,1)} %get-tuple-element.13, bf16[3,384,4096]{2,1,0:T(8,128)(2,1)} %get-tuple-element.14, bf16[1,3,384,4096]{3,2,1,0:T(8,128)(2,1)} %param.13, pred[]{:T(512)S(6)} %eq.209, pred[]{:T(512)S(6)} %eq.201), kind=kLoop, calls=%fused_computation.11 | loop fusion | flops 9437184 | bytes 37748736 | tf_op jit(solution)/shard_map/jit(_where)/select_n | solution.py:113
  696.8 3.5 fusion.2
  700.4 3.0 fusion.15
  703.4 3.8 convolution_convert_fusion
  707.3 4.7 all-to-all-start.1
  712.1 10.2 %all-to-all-done.1 = bf16[4,40,1024]{2,1,0:T(8,128)(2,1)S(1)} async-done(((bf16[4,40,1024]{2,1,0:T(8,128)(2,1)}), bf16[4,40,1024]{2,1,0:T(8,128)(2,1)S(1)}, u32[]{:S(2)}, u32[]{:S(2)}) %all-to-all-start.1) | async-done | bytes 327712 | tf_op jit(solution)/shard_map/all_to_all | solution.py:86
  722.3 12.7 %reduce-scatter.5.cloned.1.call-done = bf16[4,40,1024]{2,1,0:T(8,128)(2,1)} async-done(((bf16[4,40,4096]{2,1,0:T(8,128)(2,1)}), bf16[4,40,1024]{2,1,0:T(8,128)(2,1)}) %reduce-scatter.5.cloned.1.call-update) | async-done | bytes 327696 | tf_op jit(solution)/shard_map/reduce_scatter | solution.py:80
  735.0 4.6 all-to-all-start.3
  739.6 0.7 gather_fusion.1
  740.3 0.7 gather_fusion.2
  741.0 0.1 fusion.22
  741.1 8.7 %all-to-all-done.3 = bf16[4,40,1024]{2,1,0:T(8,128)(2,1)S(1)} async-done(((bf16[4,40,1024]{2,1,0:T(8,128)(2,1)}), bf16[4,40,1024]{2,1,0:T(8,128)(2,1)S(1)}, u32[]{:S(2)}, u32[]{:S(2)}) %all-to-all-start.3) | async-done | bytes 327712 | tf_op jit(solution)/shard_map/all_to_all | solution.py:86
  749.9 0.7 gather_fusion.4
  750.6 0.7 gather_fusion.5
  751.3 0.1 fusion.20
  751.4 0.7 pad_maximum_fusion
  (48 shorter events, 0.7 us)
Async XLA Ops:
  13.7 10.3 %copy-start.1 = (s32[2,4]{1,0:T(2,128)S(1)}, s32[2,4]{1,0:T(2,128)}, u32[]{:S(2)}) copy-start(s32[2,4]{1,0:T(2,128)} %param.11) | copy-start | bytes 100
  17.7 16.6 %all-to-all-start = ((bf16[4,40,1024]{2,1,0:T(8,128)(2,1)}), bf16[4,40,1024]{2,1,0:T(8,128)(2,1)S(1)}, u32[]{:S(2)}, u32[]{:S(2)}) async-start(bf16[4,40,1024]{2,1,0:T(8,128)(2,1)} %bitcast.9), calls=%async_computation | async-start | bytes 655360 | tf_op jit(solution)/shard_map/all_to_all | solution.py:73
  24.0 55.7 %all-gather.3.cloned.1.call-start = ((), (), s32[]{:S(2)}) async-start(), calls=%async_computation.6 | async-start | bytes 1638400 | tf_op jit(solution)/shard_map/all_gather | solution.py:74
  34.3 0.7 copy-start
  35.1 652.6 %all-reduce.7.cloned.1.call-start = ((), (), s32[]{:S(2)}) async-start(), calls=%async_computation.10 | async-start | bytes 37748736 | tf_op jit(solution)/shard_map/psum | solution.py:9
  52.0 644.8 %all-gather.5.cloned.1.call-start = ((), (), s32[]{:S(2)}) async-start(), calls=%async_computation.8 | async-start | bytes 1638400 | tf_op jit(solution)/shard_map/all_gather | solution.py:74
  78.4 628.9 %reduce-scatter.3.cloned.1.call-start = ((), (), s32[]{:S(2)}) async-start(), calls=%async_computation.7 | async-start | bytes 1638400 | tf_op jit(solution)/shard_map/reduce_scatter | solution.py:80
  79.7 3.6 copy-start.3
  90.3 644.7 %reduce-scatter.5.cloned.1.call-start = ((), (), s32[]{:S(2)}) async-start(), calls=%async_computation.9 | async-start | bytes 1638400 | tf_op jit(solution)/shard_map/reduce_scatter | solution.py:80
  696.8 3.5 copy-start.4
  703.4 8.7 %copy-start.2 = (f32[2,64,2]{1,2,0:T(2,128)S(1)}, f32[2,64,2]{1,2,0:T(2,128)}, u32[]{:S(2)}) copy-start(f32[2,64,2]{1,2,0:T(2,128)} %param.9) | copy-start | bytes 3076
  707.3 15.0 %all-to-all-start.1 = ((bf16[4,40,1024]{2,1,0:T(8,128)(2,1)}), bf16[4,40,1024]{2,1,0:T(8,128)(2,1)S(1)}, u32[]{:S(2)}, u32[]{:S(2)}) async-start(bf16[4,40,1024]{2,1,0:T(8,128)(2,1)} %reduce-scatter.3.cloned.1.call-done), calls=%async_computation.2 | async-start | bytes 655360 | tf_op jit(solution)/shard_map/all_to_all | solution.py:86
  735.0 14.9 %all-to-all-start.3 = ((bf16[4,40,1024]{2,1,0:T(8,128)(2,1)}), bf16[4,40,1024]{2,1,0:T(8,128)(2,1)S(1)}, u32[]{:S(2)}, u32[]{:S(2)}) async-start(bf16[4,40,1024]{2,1,0:T(8,128)(2,1)} %reduce-scatter.5.cloned.1.call-done), calls=%async_computation.5 | async-start | bytes 655360 | tf_op jit(solution)/shard_map/all_to_all | solution.py:86
Sparse Core Ops, SparseCore 0:
  35.2 17.2 all-gather.2
  78.5 17.1 all-gather.4
  98.2 26.5 reduce-scatter.2
  707.4 27.5 reduce-scatter.4
Sparse Core Ops, SparseCore 1:
  52.1 635.5 all-reduce.6
where the time goes:
time: 760 us; the launch traced here: 759 us
  waiting for transfers between devices  639 us (84%)
  other arithmetic  28.8 us (4%)
  blocking collectives  24.3 us (3%)
  matrix products  20.8 us (3%)
  between operations  17.4 us (2%)
  starting transfers between devices  15.8 us (2%)
  local copies, waits for them, and re-layouts  12.9 us (2%)
    psum x1, waiting for transfers between devices, broadcast(): return lax.psum(jnp.where(mine, shard, jnp.zeros_like(shard)), axis)  597 us
    all_to_all x1, blocking collectives, run_span(): lax.all_to_all(outgoing, 'ep', split_axis=0, concat_axis=0, tiled=True)  24.3 us
    all_to_all x2, waiting for transfers between devices, run_span(): lax.all_to_all(summed, 'ep', split_axis=0, concat_axis=0, tiled=True)  18.9 us
  transfers between devices with their start and end apart: 8, of which 5 were waited for; matrix products, arithmetic and copies ran while one was open for 7% of the time, Pallas kernels for 0%

commit v1 on v0

v1 whole, which is shorter than its diff:
```python
import functools

import jax
import jax.numpy as jnp
from jax import lax
from jax.experimental import pallas as pl
from jax.experimental.pallas import tpu as pltpu
from jax.sharding import PartitionSpec as P

VMEM_LIMIT = 32 * 1024 * 1024
CONTRACT_LAST = (((1,), (1,)), ((), ()))


def routes(placement, limits, chosen_ids, pick_values, gates):
    spans, rows, top = chosen_ids.shape
    slots = placement.shape[1]
    slot_range = jnp.arange(slots, dtype=jnp.int32)
    same = placement[:, :, None] == placement[:, None, :]
    before = slot_range[None, :] < slot_range[:, None]
    turn = jnp.sum((same & before).astype(jnp.int32), axis=2)
    flat_ids = chosen_ids.reshape(spans, rows * top)
    holders = flat_ids[:, :, None] == placement[:, None, :]
    count = jnp.sum(holders.astype(jnp.int32), axis=2)
    wanted = pick_values.reshape(spans, rows * top) % count
    onehot = holders & (turn[:, None, :] == wanted[:, :, None])
    slot = jnp.sum(jnp.where(onehot, slot_range, 0), axis=2)
    limit = jnp.sum(jnp.where(onehot, limits, 0), axis=2)
    order = jnp.arange(rows * top, dtype=jnp.int32)
    ahead = (slot[:, :, None] == slot[:, None, :]) & (order[None, :] < order[:, None])
    rank = jnp.sum(ahead.astype(jnp.int32), axis=2)
    kept = rank < limit
    shape = (spans, rows, top)
    return (
        slot.reshape(shape),
        rank.reshape(shape),
        jnp.where(kept.reshape(shape), gates, 0.0),
        kept.reshape(shape),
    )


def in_vmem(count):
    return [pl.BlockSpec(memory_space=pltpu.VMEM)] * count


def with_core(count):
    return [pl.BlockSpec(memory_space=pltpu.SMEM)] + in_vmem(count)


def params():
    return pltpu.CompilerParams(vmem_limit_bytes=VMEM_LIMIT)


def cost(rows, width, units):
    return pl.CostEstimate(
        flops=2 * rows * width * units, bytes_accessed=2 * rows * width, transcendentals=0
    )


def in_hbm():
    return pl.BlockSpec(memory_space=pltpu.HBM)


def take_kernel(span, core_ref, from_ref, out_ref, sems):
    chips = core_ref.shape[0]
    part = out_ref.shape[1] // chips
    copies = []
    for chip in range(chips):
        at = pl.multiple_of((2 * chip + core_ref[chip]) * part, part)
        to = out_ref.at[:, chip * part : (chip + 1) * part]
        copies.append(pltpu.make_async_copy(from_ref.at[span, :, pl.ds(at, part)], to, sems.at[chip]))
        copies[-1].start()
    for copy in copies:
        copy.wait()


def take(core, tokens, span):
    chips = core.shape[0]
    rows, width = tokens.shape[1:]
    return pl.pallas_call(
        functools.partial(take_kernel, span),
        out_shape=jax.ShapeDtypeStruct((rows, width // 2), jnp.bfloat16),
        in_specs=[pl.BlockSpec(memory_space=pltpu.SMEM), in_hbm()],
        out_specs=in_vmem(1)[0],
        scratch_shapes=[pltpu.SemaphoreType.DMA((chips,))],
        compiler_params=params(),
        cost_estimate=cost(rows, width, 1),
    )(core, tokens)


def pack_kernel(core_ref, choose_ref, rows_ref, own_ref, *out_refs):
    chips = core_ref.shape[0]
    count = own_ref.shape[0]
    part = own_ref.shape[1] // (2 * chips)
    first = core_ref[0] == 0
    choose = choose_ref[...]
    for chip in range(chips):
        of = 2 * chip * part
        low = jnp.dot(
            choose, rows_ref[:, of : of + part], preferred_element_type=jnp.float32
        )
        high = jnp.dot(
            choose, rows_ref[:, of + part : of + 2 * part], preferred_element_type=jnp.float32
        )
        own_ref[:, of : of + part] = low[:count].astype(jnp.bfloat16)
        own_ref[:, of + part : of + 2 * part] = high[:count].astype(jnp.bfloat16)
        sent = jnp.where(first, low, high)
        for index, out_ref in enumerate(out_refs):
            at = (index + 1) * count
            out_ref[:, chip * part : (chip + 1) * part] = sent[at : at + count].astype(jnp.bfloat16)


def pack(core, choose, rows, slots):
    count = choose.shape[0] // slots
    width = rows.shape[1]
    outs = [jax.ShapeDtypeStruct((count, width), jnp.bfloat16)]
    outs += [jax.ShapeDtypeStruct((count, width // 2), jnp.bfloat16)] * (slots - 1)
    own, *others = pl.pallas_call(
        pack_kernel,
        out_shape=outs,
        in_specs=with_core(2),
        out_specs=in_vmem(slots),
        compiler_params=params(),
        cost_estimate=cost(choose.shape[0], choose.shape[1], width),
    )(core, choose, rows)
    return own, others


def load_kernel(columns_ref, from_ref, up_ref, down_ref, sent_ref, sems):
    parts = up_ref.shape[0]
    chips = down_ref.shape[0]
    part = up_ref.shape[3]
    copies = []
    for chip in range(chips):
        for side, to_ref in enumerate((sent_ref, down_ref)):
            at = pl.multiple_of(columns_ref[2 * side, chip] * part, part)
            copies.append(
                pltpu.make_async_copy(
                    from_ref.at[0, 2, :, pl.ds(at, part)], to_ref.at[chip], sems.at[2 * chip + side]
                )
            )
    for index in range(parts):
        copies.append(
            pltpu.make_async_copy(
                from_ref.at[0, 0:2, :, index * part : (index + 1) * part],
                up_ref.at[index],
                sems.at[parts + index],
            )
        )
    for copy in copies:
        copy.start()
    for copy in copies:
        copy.wait()


def load(columns, weights):
    chips = columns.shape[1]
    units, width = weights.shape[2:]
    part = width // (2 * chips)
    return pl.pallas_call(
        load_kernel,
        out_shape=[
            pltpu.VMEM((2 * chips, 2, units, part), jnp.bfloat16),
            pltpu.VMEM((chips, units, part), jnp.bfloat16),
            jax.ShapeDtypeStruct((chips, units, part), jnp.bfloat16),
        ],
        in_specs=[pl.BlockSpec(memory_space=pltpu.SMEM), in_hbm()],
        out_specs=in_vmem(3),
        scratch_shapes=[pltpu.SemaphoreType.DMA((4 * chips,))],
        compiler_params=params(),
        cost_estimate=cost(3 * units, width, 1),
    )(columns, weights)


def up_kernel(core_ref, own_ref, *refs):
    *piece_refs, weight_ref, hidden_ref, rows_ref = refs
    chips = core_ref.shape[0]
    count = len(piece_refs) // 2
    part = own_ref.shape[1] // (2 * chips)
    first = core_ref[0] == 0
    gate = upward = 0.0
    for index in range(2 * chips):
        chip, core = index // 2, index % 2
        column = slice(index * part, (index + 1) * part)
        of = slice(chip * part, (chip + 1) * part)
        values = [own_ref[:, column]]
        for piece in range(count):
            own, other = piece_refs[piece][:, of], piece_refs[count + piece][:, of]
            values.append(
                jnp.where(first, own, other) if core == 0 else jnp.where(first, other, own)
            )
        if all(value.shape[0] % 16 == 0 for value in values):
            at = 0
            for value in values:
                rows_ref[at : at + value.shape[0]] = value
                at += value.shape[0]
        else:
            joined = jnp.concatenate([value.astype(jnp.float32) for value in values])
            rows_ref[...] = joined.astype(jnp.bfloat16)
        rows = rows_ref[...]
        gate += lax.dot_general(
            rows, weight_ref[index, 0], CONTRACT_LAST, preferred_element_type=jnp.float32
        )
        upward += lax.dot_general(
            rows, weight_ref[index, 1], CONTRACT_LAST, preferred_element_type=jnp.float32
        )
    hidden_ref[...] = (gate / (1.0 + jnp.exp(-gate)) * upward).astype(jnp.bfloat16)


def up(core, own, own_pieces, other_pieces, weights):
    total, width = own.shape[0] + sum(piece.shape[0] for piece in own_pieces), own.shape[1]
    units, part = weights.shape[2:]
    return pl.pallas_call(
        up_kernel,
        out_shape=jax.ShapeDtypeStruct((total, units), jnp.bfloat16),
        in_specs=with_core(2 * len(own_pieces) + 2),
        out_specs=in_vmem(1)[0],
        scratch_shapes=[pltpu.VMEM((total, part), jnp.bfloat16)],
        compiler_params=params(),
        cost_estimate=cost(total, width, 2 * units),
    )(core, own, *own_pieces, *other_pieces, weights)


def down_kernel(columns_ref, hidden_ref, other_hidden_ref, weight_ref, other_ref, *out_refs):
    hidden, other_hidden = hidden_ref[...], other_hidden_ref[...]
    for shift, out_ref in enumerate(out_refs):
        total = jnp.dot(hidden, weight_ref[shift], preferred_element_type=jnp.float32)
        total += jnp.dot(
            other_hidden, other_ref[columns_ref[1, shift]], preferred_element_type=jnp.float32
        )
        out_ref[...] = total.astype(jnp.bfloat16)


def down(columns, hidden, other_hidden, weights, other_weights):
    chips, units, part = other_weights.shape
    rows = hidden.shape[0]
    return pl.pallas_call(
        down_kernel,
        out_shape=[jax.ShapeDtypeStruct((rows, part), jnp.bfloat16)] * chips,
        in_specs=with_core(4),
        out_specs=in_vmem(chips),
        compiler_params=params(),
        cost_estimate=cost(rows, 2 * units, chips * part),
    )(columns, hidden, other_hidden, weights, other_weights)


def unpack_kernel(weight_ref, *refs):
    *piece_refs, out_ref = refs
    rows = jnp.concatenate([ref[...].astype(jnp.float32) for ref in piece_refs])
    rows = rows.astype(jnp.bfloat16)
    weight = weight_ref[...]
    high = weight.astype(jnp.bfloat16)
    low = (weight - high.astype(jnp.float32)).astype(jnp.bfloat16)
    total = jnp.dot(high, rows, preferred_element_type=jnp.float32)
    total += jnp.dot(low, rows, preferred_element_type=jnp.float32)
    out_ref[...] = total.astype(jnp.bfloat16)


def unpack(weight, pieces):
    rows, part = weight.shape[0], pieces[0].shape[1]
    return pl.pallas_call(
        unpack_kernel,
        out_shape=jax.ShapeDtypeStruct((rows, part), jnp.bfloat16),
        in_specs=in_vmem(1 + len(pieces)),
        out_specs=in_vmem(1)[0],
        compiler_params=params(),
        cost_estimate=cost(rows, weight.shape[1], part),
    )(weight, *pieces)


def per_device(
    tokens, expert_ids, gate_weights, replica_pick, placement, slot_limit, expert_weights
):
    spans, rows, width = tokens.shape
    top = expert_ids.shape[2]
    ep = lax.axis_size("ep")
    tp = lax.axis_size("tp")
    chips = tp // 2
    part = width // tp
    capacity = rows * top * 5 // (4 * ep)
    few = ep <= 8
    own_slot = lax.axis_index("ep")
    own_chip = lax.axis_index("tp") // 2
    own_core = lax.axis_index("tp") % 2
    slot_range = jnp.arange(ep, dtype=jnp.int32)
    chip_range = jnp.arange(chips, dtype=jnp.int32)
    core = jnp.full((chips,), own_core, jnp.int32)
    chip_order = (own_chip + chip_range) % chips
    columns = jnp.stack(
        [chip_range * 2 + 1 - own_core, chip_order, chip_order * 2 + own_core]
    )

    def along_ep(value, shift):
        return lax.ppermute(value, "ep", [(i, (i + shift) % ep) for i in range(ep)])

    def along_chips(value, shift):
        pairs = [
            (x * 2 + c, (x + shift) % chips * 2 + c) for x in range(chips) for c in range(2)
        ]
        return lax.ppermute(value, "tp", pairs)

    def along_cores(value):
        return lax.ppermute(value, "tp", [(i, i ^ 1) for i in range(tp)])

    def exchange(pieces, back):
        sign = -1 if back else 1
        if few:
            return [along_ep(piece, sign * (at + 1)) for at, piece in enumerate(pieces)]
        stacked = jnp.stack([pieces[0]] + pieces)
        placed = stacked[sign * (slot_range - own_slot) % ep]
        came = lax.all_to_all(placed, "ep", 0, 0, tiled=True)
        return list(came[(own_slot - sign * slot_range[1:]) % ep])

    weights = pltpu.with_memory_space_constraint(expert_weights, pltpu.HBM)
    arrived = {}
    for span in range(1, spans):
        sent = take(core, pltpu.with_memory_space_constraint(tokens, pltpu.HBM), span)
        arrived[span] = (tokens[span], exchange([sent] * (ep - 1), False))

    slot, rank, kept_gates, kept = routes(
        placement, slot_limit, expert_ids, replica_pick, gate_weights
    )
    place = (slot[0] - own_slot) % ep * capacity + rank[0]
    place = jnp.where(kept[0], place, ep * capacity)
    hits = place[:, :, None] == jnp.arange(ep * capacity, dtype=jnp.int32)
    choose = jnp.any(hits, axis=1).astype(jnp.bfloat16).T
    up_weights, down_weights, for_other = load(columns, weights)
    other_down = along_cores(for_other)
    own, others = pack(core, choose, tokens[0], ep)
    others, other_down = lax.optimization_barrier((others, other_down))
    arrived[0] = (own, exchange(others, False))

    def finish(span, after):
        own, pieces = arrived[span]
        if after is not None:
            own, after = lax.optimization_barrier((own, after))
        hidden = up(core, own, pieces, [along_cores(piece) for piece in pieces], up_weights)
        sums = down(columns, hidden, along_cores(hidden), down_weights, other_down)
        came = [along_chips(sums[shift], shift) for shift in range(1, chips)]
        totals = []
        count = own.shape[0]
        for piece in range(ep):
            at = slice(piece * count, (piece + 1) * count)
            total = sums[0][at].astype(jnp.float32)
            for value in came:
                total = total + value[at].astype(jnp.float32)
            totals.append(total.astype(jnp.bfloat16))
        return [totals[0]] + exchange(totals[1:], True), hidden

    returned = {}
    hidden = None
    for span in list(range(1, spans)) + [0]:
        returned[span], hidden = finish(span, hidden)

    old_table = placement[0]
    outs = []
    for span in range(spans):
        if span == 0:
            weight = jnp.sum(jnp.where(hits, kept_gates[0][:, :, None], 0.0), axis=1)
            outs.append(unpack(weight, returned[0]))
            continue
        serves = placement[span][:, None] == old_table[None, :]
        serving = jnp.min(jnp.where(serves, slot_range, ep), axis=1)
        served = jnp.sum(
            jnp.where(slot[span][:, :, None] == slot_range, (serving - own_slot) % ep, 0), axis=2
        )
        combined = jnp.zeros((rows, part), jnp.float32)
        for at in range(ep):
            share = jnp.sum(jnp.where(served == at, kept_gates[span], 0.0), axis=1)[:, None]
            value = share * returned[span][at].astype(jnp.float32)
            combined = combined + jnp.where(share != 0, value, 0.0)
        outs.append(combined.astype(jnp.bfloat16))
    return jnp.stack(outs)


def solution(mesh):
    placed = (
        P(None, ("groups", "ep"), None),
        P(None, ("groups", "ep"), None),
        P(None, ("groups", "ep"), None),
        P(None, ("groups", "ep"), None),
        P(),
        P(),
        P("ep", None, "tp", None),
    )
    return jax.shard_map(
        per_device,
        mesh=mesh,
        in_specs=placed,
        out_specs=P(None, ("groups", "ep"), "tp"),
        check_vma=False,
    )
```

time: 760 us -> 94.4 us (0.12)
  waiting for transfers between devices: 639 us -> 17.1 us
  blocking collectives: 24.3 us -> 0 us
  other arithmetic: 28.8 us -> 6.25 us
  matrix products: 20.8 us -> 0 us
  Pallas kernels: 0 us -> 19.4 us
  starting transfers between devices: 15.8 us -> 34.8 us
  between operations: 17.4 us -> 0.42 us
    psum x1 -> x0, waiting for transfers between devices: 597 us -> none  [broadcast(): return lax.psum(jnp.where(mine, shard, jnp.zeros_like(shard)), axis)]
    ppermute x0 -> x23, starting transfers between devices: none -> 34.8 us  [the longest x12 29.7 us: along_ep(): return lax.ppermute(value, 'ep', [(i, (i + shift) % ep) for i in range(ep)])]
    all_to_all x3 -> x0, waiting for transfers between devices: 29 us -> none  [the longest x2 18.9 us: run_span(): lax.all_to_all(summed, 'ep', split_axis=0, concat_axis=0, tiled=True)]
    all_to_all x1 -> x0, blocking collectives: 24.3 us -> none  [run_span(): lax.all_to_all(outgoing, 'ep', split_axis=0, concat_axis=0, tiled=True)]
    dot_general x6 -> x0, matrix products: 20.8 us -> none  [the longest x2 7.64 us: feed_forward(): return jnp.dot(hidden, weights[2], preferred_element_type=jnp.float32)]
    select_n x9 -> x5, other arithmetic: 20.7 us -> 0.17 us  [the longest x1 0.13 us: routes(): wanted = pick_values.reshape(spans, rows * top) % count]
    pallas_call x0 -> x8, Pallas kernels: none -> 19.4 us  [the longest x2 7.05 us: up(): pl.pallas_call(up_kernel, out_shape=jax.ShapeDtypeStruct((total, units),...]
    ppermute x0 -> x23, waiting for transfers between devices: none -> 17.1 us  [the longest x12 12.9 us: along_ep(): return lax.ppermute(value, 'ep', [(i, (i + shift) % ep) for i in range(ep)])]
  transfers between devices with their start and end apart: 8 -> 23, of which waited for: 5 -> 8; matrix products, arithmetic and copies ran while one was open for 7% -> 11% of each run, Pallas kernels for 0% -> 19%
where the time goes in v1:
time: 94.4 us; the launch traced here: 93.9 us
  starting transfers between devices  34.8 us (37%)
  Pallas kernels  19.4 us (21%)
  waiting for transfers between devices  17.1 us (18%)
  local copies, waits for them, and re-layouts  15.9 us (17%)
  other arithmetic  6.25 us (7%)
    ppermute x12, starting transfers between devices, along_ep(): return lax.ppermute(value, 'ep', [(i, (i + shift) % ep) for i in range(ep)])  29.7 us
    ppermute x12, waiting for transfers between devices, along_ep(): return lax.ppermute(value, 'ep', [(i, (i + shift) % ep) for i in range(ep)])  12.9 us
    unnamed x39, local copies, waits for them, and re-layouts  11.4 us
    pallas_call x2, Pallas kernels, up(): pl.pallas_call(up_kernel, out_shape=jax.ShapeDtypeStruct((total, units),...  7.05 us
    pallas_call x1, Pallas kernels, load(): pl.pallas_call(load_kernel, out_shape=[pltpu.VMEM((2 * chips, 2, units, p...  5.56 us
    pallas_call x2, Pallas kernels, down(): pl.pallas_call(down_kernel, out_shape=[jax.ShapeDtypeStruct((rows, part),...  4.04 us
    ppermute x2, starting transfers between devices, along_chips(): return lax.ppermute(value, 'tp', pairs)  3.04 us
    ppermute x9, waiting for transfers between devices, along_cores(): return lax.ppermute(value, 'tp', [(i, i ^ 1) for i in range(tp)])  2.42 us
  transfers between devices with their start and end apart: 23, of which 8 were waited for; matrix products, arithmetic and copies ran while one was open for 11% of the time, Pallas kernels for 19%

profile of v1, /device:TPU:0, one launch (start us, length us, event | category | flops | bytes accessed | tf_op | source)
XLA Modules:
  0.0 93.9 jit_solution(16683553376364460617)
XLA Ops:
  0.0 1.5 %shard_map.74 = bf16[64,2048]{1,0:T(8,128)(2,1)S(1)} custom-call(s32[2]{0:T(128)S(1)} %sub.44.core_ref, bf16[2,64,4096]{2,1,0:T(8,128)(2,1)} %from_ref.2), custom_call_target="tpu_custom_call" | custom-call | flops 524288 | bytes 524288 | tf_op jit(solution)/shard_map/pallas_call | solution.py:79
  1.5 3.1 %collective-permute-start = (bf16[64,2048]{1,0:T(8,128)(2,1)S(1)}, bf16[64,2048]{1,0:T(8,128)(2,1)}, u32[]{:S(2)}, u32[]{:S(2)}) collective-permute-start(bf16[64,2048]{1,0:T(8,128)(2,1)S(1)} %shard_map.74), channel_id=1, source_target_pairs={{0,4},{4,8},{8,12},{12,0},{1,5},{5,9},{9,13},{13,1},{2,6},{6,10},{... | collective-permute-start | bytes 786440 | tf_op jit(solution)/shard_map/ppermute | solution.py:293
  4.6 2.6 %collective-permute-start.1 = (bf16[64,2048]{1,0:T(8,128)(2,1)S(1)}, bf16[64,2048]{1,0:T(8,128)(2,1)}, u32[]{:S(2)}, u32[]{:S(2)}) collective-permute-start(bf16[64,2048]{1,0:T(8,128)(2,1)S(1)} %shard_map.74), channel_id=1, source_target_pairs={{0,8},{4,12},{8,0},{12,4},{1,9},{5,13},{9,1},{13,5},{2,10},{6,14},... | collective-permute-start | bytes 786440 | tf_op jit(solution)/shard_map/ppermute | solution.py:293
  7.2 1.3 %collective-permute-start.2 = (bf16[64,2048]{1,0:T(8,128)(2,1)S(1)}, bf16[64,2048]{1,0:T(8,128)(2,1)}, u32[]{:S(2)}, u32[]{:S(2)}) collective-permute-start(bf16[64,2048]{1,0:T(8,128)(2,1)S(1)} %shard_map.74), channel_id=1, source_target_pairs={{0,12},{4,0},{8,4},{12,8},{1,13},{5,1},{9,5},{13,9},{2,14},{6,2},{... | collective-permute-start | bytes 786440 | tf_op jit(solution)/shard_map/ppermute | solution.py:293
  8.7 5.6 %shard_map.75 = (bf16[4,2,384,1024]{3,2,1,0:T(8,128)(2,1)S(1)}, bf16[2,384,1024]{2,1,0:T(8,128)(2,1)S(1)}, bf16[2,384,1024]{2,1,0:T(8,128)(2,1)}) custom-call(s32[3,2]{1,0:T(4,128)S(1)} %pad_add_fusion.columns_ref, bf16[1,3,384,4096]{3,2,1,0:T(8,128)(2,1)} %from_ref.3), custom_call_target="tpu_custom_call" | custom-call | flops 9437184 | bytes 9437184 | tf_op jit(solution)/shard_map/pallas_call | solution.py:159
  14.2 2.6 %copy-done = bf16[4,2,384,1024]{3,2,1,0:T(8,128)(2,1)} copy-done((bf16[4,2,384,1024]{3,2,1,0:T(8,128)(2,1)}, bf16[4,2,384,1024]{3,2,1,0:T(8,128)(2,1)S(1)}, u32[]{:S(2)}) %copy-start) | copy-done | bytes 6291480
  16.9 0.1 copy.35
  17.0 0.1 eq.135
  17.2 0.1 copy.36
  17.3 0.1 reshape.176
  17.5 0.2 convert_reduce_fusion.1
  17.7 0.1 and_select_fusion.3
  18.0 0.2 convert_reduce_fusion
  18.2 0.2 lt.91
  18.4 0.5 slice_bitcast_fusion.3
  18.9 0.1 sub.40
  19.1 0.1 squeeze.20
  19.3 0.2 squeeze.19
  19.6 0.1 copy.42
  19.7 0.8 select_reduce_fusion.4
  20.6 2.4 %slice_bitcast_fusion.1 = (bf16[64,4096]{1,0:T(8,128)(2,1)}, bf16[64,4096]{1,0:T(8,128)(2,1)}) fusion(bf16[2,64,4096]{2,1,0:T(8,128)(2,1)} %from_ref.2), kind=kLoop, calls=%fused_computation.1 | loop fusion | bytes 2097152 | tf_op jit(solution)/shard_map/squeeze | solution.py:328
  23.0 0.1 eq.152
  23.3 0.1 fusion
  23.5 0.6 collective-permute-start.3
  24.0 0.4 collective-permute-done.1.refs_1_
  24.4 0.5 collective-permute-start.5
  24.9 0.6 fusion.5
  25.5 0.1 copy.44
  25.6 1.0 %copy-done.4 = bf16[64,4096]{1,0:T(8,128)(2,1)S(1)} copy-done((bf16[64,4096]{1,0:T(8,128)(2,1)S(1)}, bf16[64,4096]{1,0:T(8,128)(2,1)}, u32[]{:S(2)}) %copy-start.4) | copy-done | bytes 524312
  26.7 1.0 %shard_map.73 = (bf16[40,4096]{1,0:T(8,128)(2,1)S(1)}, bf16[40,2048]{1,0:T(8,128)(2,1)S(1)}, bf16[40,2048]{1,0:T(8,128)(2,1)S(1)}, bf16[40,2048]{1,0:T(8,128)(2,1)S(1)}) custom-call(s32[2]{0:T(128)S(1)} %sub.44.core_ref, bf16[160,64]{1,0:T(8,128)(2,1)S(1)} %bitcast.19, bf16[64,4096]{1,0:T(8,128)(2,1)S(1)} %copy-done.4), custom_call_target="tpu_custom_call" | custom-call | flops 83886080 | bytes 20480 | tf_op jit(solution)/shard_map/pallas_call | solution.py:117
  27.7 0.6 broadcast_compare_fusion
  28.3 2.8 %copy-done.1 = bf16[4,2,384,1024]{3,2,1,0:T(8,128)(2,1)S(1)} copy-done((bf16[4,2,384,1024]{3,2,1,0:T(8,128)(2,1)S(1)}, bf16[4,2,384,1024]{3,2,1,0:T(8,128)(2,1)}, u32[]{:S(2)}) %copy-start.1) | copy-done | bytes 6291480
  31.1 1.0 %copy-done.3 = bf16[64,4096]{1,0:T(8,128)(2,1)S(1)} copy-done((bf16[64,4096]{1,0:T(8,128)(2,1)S(1)}, bf16[64,4096]{1,0:T(8,128)(2,1)}, u32[]{:S(2)}) %copy-start.3) | copy-done | bytes 524312
  32.2 3.7 %shard_map.76.hidden_ref = bf16[256,384]{1,0:T(8,128)(2,1)S(1)} custom-call(s32[2]{0:T(128)S(1)} %sub.44.core_ref, bf16[64,4096]{1,0:T(8,128)(2,1)S(1)} %copy-done.3, bf16[64,2048]{1,0:T(8,128)(2,1)} %collective-permute-done.refs_0_, bf16[64,2048]{1,0:T(8,128)(2,1)} %collective-permute-done.1.refs_1_, bf16[64,2048]{1,0:T(8,128)(2,1)} %collective-permute-done.2.refs_2_, ...), custom_call_target="tpu_custom_call" | custom-call | flops 1610612736 | bytes 2097152 | tf_op jit(solution)/shard_map/pallas_call | solution.py:212
  36.0 6.1 %collective-permute-start.7 = (bf16[40,2048]{1,0:T(8,128)(2,1)S(1)}, bf16[40,2048]{1,0:T(8,128)(2,1)}, u32[]{:S(2)}, u32[]{:S(2)}) collective-permute-start(bf16[40,2048]{1,0:T(8,128)(2,1)S(1)} %get-tuple-element.28), channel_id=1, source_target_pairs={{0,4},{4,8},{8,12},{12,0},{1,5},{5,9},{9,13},{13,1},{2,6},{6,10},{... | collective-permute-start | bytes 491528 | tf_op jit(solution)/shard_map/ppermute | solution.py:293
  42.0 1.6 %collective-permute-start.8 = (bf16[40,2048]{1,0:T(8,128)(2,1)S(1)}, bf16[40,2048]{1,0:T(8,128)(2,1)}, u32[]{:S(2)}, u32[]{:S(2)}) collective-permute-start(bf16[40,2048]{1,0:T(8,128)(2,1)S(1)} %get-tuple-element.29), channel_id=1, source_target_pairs={{0,8},{4,12},{8,0},{12,4},{1,9},{5,13},{9,1},{13,5},{2,10},{6,14},... | collective-permute-start | bytes 491528 | tf_op jit(solution)/shard_map/ppermute | solution.py:293
  43.7 0.7 collective-permute-start.9
  44.4 2.6 %shard_map.80 = (bf16[256,1024]{1,0:T(8,128)(2,1)S(1)}, bf16[256,1024]{1,0:T(8,128)(2,1)}) custom-call(s32[3,2]{1,0:T(4,128)S(1)} %pad_add_fusion.columns_ref, bf16[256,384]{1,0:T(8,128)(2,1)S(1)} %shard_map.76.hidden_ref, bf16[256,384]{1,0:T(8,128)(2,1)S(1)} %collective-permute-done.18.other_hidden_ref, ...), custom_call_target="tpu_custom_call" | custom-call | flops 805306368 | bytes 393216 | tf_op jit(solution)/shard_map/pallas_call | solution.py:236
  47.1 0.8 copy-done.5
  47.9 1.5 %collective-permute-start.19 = (bf16[256,1024]{1,0:T(8,128)(2,1)}, bf16[256,1024]{1,0:T(8,128)(2,1)}, u32[]{:S(2)}, u32[]{:S(2)}) collective-permute-start(bf16[256,1024]{1,0:T(8,128)(2,1)} %get-tuple-element.36), channel_id=1, source_target_pairs={{0,2},{1,3},{2,0},{3,1},{4,6},{5,7},{6,4},{7,5},{8,10},{9,11},{10,... | collective-permute-start | bytes 1572872 | tf_op jit(solution)/shard_map/ppermute | solution.py:299
  49.3 5.8 %collective-permute-done.8.refs_1_ = bf16[40,2048]{1,0:T(8,128)(2,1)} collective-permute-done((bf16[40,2048]{1,0:T(8,128)(2,1)S(1)}, bf16[40,2048]{1,0:T(8,128)(2,1)}, u32[]{:S(2)}, u32[]{:S(2)}) %collective-permute-start.8) | collective-permute-done | bytes 163872 | tf_op jit(solution)/shard_map/ppermute | solution.py:293
  55.2 0.5 collective-permute-start.12
  55.8 1.1 %collective-permute-done.11.refs_4_ = bf16[40,2048]{1,0:T(8,128)(2,1)} collective-permute-done((bf16[40,2048]{1,0:T(8,128)(2,1)}, bf16[40,2048]{1,0:T(8,128)(2,1)}, u32[]{:S(2)}, u32[]{:S(2)}) %collective-permute-start.11) | collective-permute-done | bytes 163872 | tf_op jit(solution)/shard_map/ppermute | solution.py:302
  56.9 0.2 collective-permute-done.12.refs_5_
  57.1 2.8 %copy-done.2 = bf16[4,2,384,1024]{3,2,1,0:T(8,128)(2,1)S(1)} copy-done((bf16[4,2,384,1024]{3,2,1,0:T(8,128)(2,1)S(1)}, bf16[4,2,384,1024]{3,2,1,0:T(8,128)(2,1)}, u32[]{:S(2)}) %copy-start.2) | copy-done | bytes 6291480
  59.9 3.3 %shard_map.77.hidden_ref = bf16[160,384]{1,0:T(8,128)(2,1)S(1)} custom-call(s32[2]{0:T(128)S(1)} %sub.44.core_ref, bf16[40,4096]{1,0:T(8,128)(2,1)S(1)} %get-tuple-element.23.own_ref, bf16[40,2048]{1,0:T(8,128)(2,1)} %collective-permute-done.7.refs_0_, bf16[40,2048]{1,0:T(8,128)(2,1)} %collective-permute-done.8.refs_1_, ...), custom_call_target="tpu_custom_call" | custom-call | flops 1006632960 | bytes 1310720 | tf_op jit(solution)/shard_map/pallas_call | solution.py:212
  63.3 0.3 collective-permute-start.13
  63.6 1.0 %collective-permute-done.13.other_hidden_ref = bf16[160,384]{1,0:T(8,128)(2,1)S(1)} collective-permute-done((bf16[160,384]{1,0:T(8,128)(2,1)S(1)}, bf16[160,384]{1,0:T(8,128)(2,1)S(1)}, u32[]{:S(2)}, u32[]{:S(2)}) %collective-permute-start.13) | collective-permute-done | bytes 122912 | tf_op jit(solution)/shard_map/ppermute | solution.py:302
  64.7 1.4 %shard_map.78 = (bf16[160,1024]{1,0:T(8,128)(2,1)S(1)}, bf16[160,1024]{1,0:T(8,128)(2,1)S(1)}) custom-call(s32[3,2]{1,0:T(4,128)S(1)} %pad_add_fusion.columns_ref, bf16[160,384]{1,0:T(8,128)(2,1)S(1)} %shard_map.77.hidden_ref, bf16[160,384]{1,0:T(8,128)(2,1)S(1)} %collective-permute-done.13.other_hidden_ref, ...), custom_call_target="tpu_custom_call" | custom-call | flops 503316480 | bytes 245760 | tf_op jit(solution)/shard_map/pallas_call | solution.py:236
  66.1 1.6 %collective-permute-start.14 = (bf16[160,1024]{1,0:T(8,128)(2,1)S(1)}, bf16[160,1024]{1,0:T(8,128)(2,1)S(1)}, u32[]{:S(2)}, u32[]{:S(2)}) collective-permute-start(bf16[160,1024]{1,0:T(8,128)(2,1)S(1)} %get-tuple-element.34), channel_id=1, source_target_pairs={{0,2},{1,3},{2,0},{3,1},{4,6},{5,7},{6,4},{7,5},{8,10},{9,11},{10,... | collective-permute-start | bytes 983048 | tf_op jit(solution)/shard_map/ppermute | solution.py:299
  67.7 0.1 select_reduce_fusion.weight_ref
  67.8 1.2 %add_convert_fusion.3 = (bf16[64,1024]{1,0:T(8,128)(2,1)S(1)}, bf16[64,1024]{1,0:T(8,128)(2,1)S(1)}, bf16[64,1024]{1,0:T(8,128)(2,1)S(1)}) fusion(bf16[256,1024]{1,0:T(8,128)(2,1)} %collective-permute-done.19, bf16[256,1024]{1,0:T(8,128)(2,1)S(1)} %copy-done.6), kind=kLoop, calls=%fused_computation.6 | loop fusion | flops 786432 | bytes 1179648 | tf_op jit(solution)/shard_map/convert_element_type | solution.py:346
  69.0 4.4 %collective-permute-start.20 = (bf16[64,1024]{1,0:T(8,128)(2,1)S(1)}, bf16[64,1024]{1,0:T(8,128)(2,1)S(1)}, u32[]{:S(2)}, u32[]{:S(2)}) collective-permute-start(bf16[64,1024]{1,0:T(8,128)(2,1)S(1)} %get-tuple-element.45), channel_id=1, source_target_pairs={{0,12},{4,0},{8,4},{12,8},{1,13},{5,1},{9,5},{13,9},{2,14},{6,2},{... | collective-permute-start | bytes 393224 | tf_op jit(solution)/shard_map/ppermute | solution.py:293
  73.3 0.9 collective-permute-start.21
  74.2 1.8 %collective-permute-done.14 = bf16[160,1024]{1,0:T(8,128)(2,1)S(1)} collective-permute-done((bf16[160,1024]{1,0:T(8,128)(2,1)S(1)}, bf16[160,1024]{1,0:T(8,128)(2,1)S(1)}, u32[]{:S(2)}, u32[]{:S(2)}) %collective-permute-start.14) | collective-permute-done | bytes 327712 | tf_op jit(solution)/shard_map/ppermute | solution.py:299
  76.1 0.1 add_convert_fusion.5
  76.2 4.4 %collective-permute-start.15 = (bf16[40,1024]{1,0:T(8,128)(2,1)S(1)}, bf16[40,1024]{1,0:T(8,128)(2,1)S(1)}, u32[]{:S(2)}, u32[]{:S(2)}) collective-permute-start(bf16[40,1024]{1,0:T(8,128)(2,1)S(1)} %get-tuple-element.52), channel_id=1, source_target_pairs={{0,12},{4,0},{8,4},{12,8},{1,13},{5,1},{9,5},{13,9},{2,14},{6,2},{... | collective-permute-start | bytes 245768 | tf_op jit(solution)/shard_map/ppermute | solution.py:293
  80.5 0.8 collective-permute-start.16
  81.3 3.9 %collective-permute-start.17 = (bf16[40,1024]{1,0:T(8,128)(2,1)S(1)}, bf16[40,1024]{1,0:T(8,128)(2,1)S(1)}, u32[]{:S(2)}, u32[]{:S(2)}) collective-permute-start(bf16[40,1024]{1,0:T(8,128)(2,1)S(1)} %get-tuple-element.50), channel_id=1, source_target_pairs={{0,4},{4,8},{8,12},{12,0},{1,5},{5,9},{9,13},{13,1},{2,6},{6,10},{... | collective-permute-start | bytes 245768 | tf_op jit(solution)/shard_map/ppermute | solution.py:293
  85.2 5.3 %collective-permute-done.21 = bf16[64,1024]{1,0:T(8,128)(2,1)S(1)} collective-permute-done((bf16[64,1024]{1,0:T(8,128)(2,1)S(1)}, bf16[64,1024]{1,0:T(8,128)(2,1)S(1)}, u32[]{:S(2)}, u32[]{:S(2)}) %collective-permute-start.21) | collective-permute-done | bytes 131104 | tf_op jit(solution)/shard_map/ppermute | solution.py:293
  90.5 1.1 %fusion.1 = bf16[1,64,1024]{2,1,0:T(8,128)(2,1)S(1)} fusion(bf16[64,1024]{1,0:T(8,128)(2,1)S(1)} %collective-permute-done.22, f32[64]{0:T(128)S(1)} %copy-done.11, pred[64]{0:T(512)(128)(4,1)S(1)} %broadcast_compare_fusion, bf16[64,1024]{1,0:T(8,128)(2,1)S(1)} %collective-permute-done.21, f32[64]{0:T(128)S(1)} %copy-done.12, ...), kind=kLoop, calls=%fused_computation.16 | loop fusion | flops 1310720 | bytes 787712 | tf_op jit(solution)/shard_map/stack | solution.py:372
  91.6 1.3 %collective-permute-done.16.refs_2_ = bf16[40,1024]{1,0:T(8,128)(2,1)S(1)} collective-permute-done((bf16[40,1024]{1,0:T(8,128)(2,1)S(1)}, bf16[40,1024]{1,0:T(8,128)(2,1)S(1)}, u32[]{:S(2)}, u32[]{:S(2)}) %collective-permute-start.16) | collective-permute-done | bytes 81952 | tf_op jit(solution)/shard_map/ppermute | solution.py:293
  93.0 0.2 shard_map.79
  93.2 0.7 pad_maximum_fusion
  (77 shorter events, 1.1 us)
Async XLA Ops:
  1.5 21.9 %collective-permute-start = (bf16[64,2048]{1,0:T(8,128)(2,1)S(1)}, bf16[64,2048]{1,0:T(8,128)(2,1)}, u32[]{:S(2)}, u32[]{:S(2)}) collective-permute-start(bf16[64,2048]{1,0:T(8,128)(2,1)S(1)} %shard_map.74), channel_id=1, source_target_pairs={{0,4},{4,8},{8,12},{12,0},{1,5},{5,9},{9,13},{13,1},{2,6},{6,10},{... | collective-permute-start | bytes 786440 | tf_op jit(solution)/shard_map/ppermute | solution.py:293
  4.6 19.8 %collective-permute-start.1 = (bf16[64,2048]{1,0:T(8,128)(2,1)S(1)}, bf16[64,2048]{1,0:T(8,128)(2,1)}, u32[]{:S(2)}, u32[]{:S(2)}) collective-permute-start(bf16[64,2048]{1,0:T(8,128)(2,1)S(1)} %shard_map.74), channel_id=1, source_target_pairs={{0,8},{4,12},{8,0},{12,4},{1,9},{5,13},{9,1},{13,5},{2,10},{6,14},... | collective-permute-start | bytes 786440 | tf_op jit(solution)/shard_map/ppermute | solution.py:293
  7.2 17.2 %collective-permute-start.2 = (bf16[64,2048]{1,0:T(8,128)(2,1)S(1)}, bf16[64,2048]{1,0:T(8,128)(2,1)}, u32[]{:S(2)}, u32[]{:S(2)}) collective-permute-start(bf16[64,2048]{1,0:T(8,128)(2,1)S(1)} %shard_map.74), channel_id=1, source_target_pairs={{0,12},{4,0},{8,4},{12,8},{1,13},{5,1},{9,5},{13,9},{2,14},{6,2},{... | collective-permute-start | bytes 786440 | tf_op jit(solution)/shard_map/ppermute | solution.py:293
  8.6 8.3 %copy-start.14 = (s32[2,64,2]{1,2,0:T(2,128)S(1)}, s32[2,64,2]{1,2,0:T(2,128)}, u32[]{:S(2)}) copy-start(s32[2,64,2]{1,2,0:T(2,128)} %param.8) | copy-start | bytes 3076
  8.6 8.6 %copy-start.15 = (s32[2,64,2]{1,2,0:T(2,128)S(1)}, s32[2,64,2]{1,2,0:T(2,128)}, u32[]{:S(2)}) copy-start(s32[2,64,2]{1,2,0:T(2,128)} %param.10) | copy-start | bytes 3076
  8.6 8.8 %copy-start.7 = (s32[2,4]{1,0:T(2,128)S(1)}, s32[2,4]{1,0:T(2,128)}, u32[]{:S(2)}) copy-start(s32[2,4]{1,0:T(2,128)} %param.11) | copy-start | bytes 100
  8.6 9.2 %copy-start.17 = (s32[4]{0:T(128)S(1)}, s32[4]{0:T(128)}, u32[]{:S(2)}) copy-start(s32[4]{0:T(128)} %param.12) | copy-start | bytes 52
  8.6 10.9 %copy-start.16 = (f32[2,64,2]{1,2,0:T(2,128)S(1)}, f32[2,64,2]{1,2,0:T(2,128)}, u32[]{:S(2)}) copy-start(f32[2,64,2]{1,2,0:T(2,128)} %param.9) | copy-start | bytes 3076
  14.2 2.6 %copy-start = (bf16[4,2,384,1024]{3,2,1,0:T(8,128)(2,1)}, bf16[4,2,384,1024]{3,2,1,0:T(8,128)(2,1)S(1)}, u32[]{:S(2)}) copy-start(bf16[4,2,384,1024]{3,2,1,0:T(8,128)(2,1)S(1)} %get-tuple-element.22.refs_6_) | copy-start | bytes 18874372
  16.9 19.1 %collective-permute-start.6 = (bf16[2,384,1024]{2,1,0:T(8,128)(2,1)}, bf16[2,384,1024]{2,1,0:T(8,128)(2,1)S(1)}, u32[]{:S(2)}, u32[]{:S(2)}) collective-permute-start(bf16[2,384,1024]{2,1,0:T(8,128)(2,1)} %get-tuple-element.27), channel_id=1, source_target_pairs={{0,1},{1,0},{2,3},{3,2},{4,5},{5,4},{6,7},{7,6},{8,9},{9,8},{10,11... | collective-permute-start | bytes 4718600 | tf_op jit(solution)/shard_map/ppermute | solution.py:302
  20.6 4.9 %copy-start.8 = (s32[64,2]{0,1:T(2,128)}, s32[64,2]{0,1:T(2,128)S(1)}, u32[]{:S(2)}) copy-start(s32[64,2]{0,1:T(2,128)S(1)} %fusion.10) | copy-start | bytes 1540
  23.5 4.8 %collective-permute-start.3 = (bf16[64,2048]{1,0:T(8,128)(2,1)}, bf16[64,2048]{1,0:T(8,128)(2,1)}, u32[]{:S(2)}, u32[]{:S(2)}) collective-permute-start(bf16[64,2048]{1,0:T(8,128)(2,1)} %collective-permute-done.refs_0_), channel_id=1, source_target_pairs={{0,1},{1,0},{2,3},{3,2},{4,5},{5,4},{6,7},{7,6},{8,9},{9,8},{10,11... | collective-permute-start | bytes 786440 | tf_op jit(solution)/shard_map/ppermute | solution.py:302
  24.4 3.9 %collective-permute-start.4 = (bf16[64,2048]{1,0:T(8,128)(2,1)}, bf16[64,2048]{1,0:T(8,128)(2,1)}, u32[]{:S(2)}, u32[]{:S(2)}) collective-permute-start(bf16[64,2048]{1,0:T(8,128)(2,1)} %collective-permute-done.1.refs_1_), channel_id=1, source_target_pairs={{0,1},{1,0},{2,3},{3,2},{4,5},{5,4},{6,7},{7,6},{8,9},{9,8},{10,11... | collective-permute-start | bytes 786440 | tf_op jit(solution)/shard_map/ppermute | solution.py:302
  24.4 3.9 %collective-permute-start.5 = (bf16[64,2048]{1,0:T(8,128)(2,1)}, bf16[64,2048]{1,0:T(8,128)(2,1)}, u32[]{:S(2)}, u32[]{:S(2)}) collective-permute-start(bf16[64,2048]{1,0:T(8,128)(2,1)} %collective-permute-done.2.refs_2_), channel_id=1, source_target_pairs={{0,1},{1,0},{2,3},{3,2},{4,5},{5,4},{6,7},{7,6},{8,9},{9,8},{10,11... | collective-permute-start | bytes 786440 | tf_op jit(solution)/shard_map/ppermute | solution.py:302
  25.6 1.1 %copy-start.4 = (bf16[64,4096]{1,0:T(8,128)(2,1)S(1)}, bf16[64,4096]{1,0:T(8,128)(2,1)}, u32[]{:S(2)}) copy-start(bf16[64,4096]{1,0:T(8,128)(2,1)} %get-tuple-element.48.rows_ref) | copy-start | bytes 1572868
  28.3 2.8 %copy-start.1 = (bf16[4,2,384,1024]{3,2,1,0:T(8,128)(2,1)S(1)}, bf16[4,2,384,1024]{3,2,1,0:T(8,128)(2,1)}, u32[]{:S(2)}) copy-start(bf16[4,2,384,1024]{3,2,1,0:T(8,128)(2,1)} %copy-done) | copy-start | bytes 18874372
  31.1 1.0 %copy-start.3 = (bf16[64,4096]{1,0:T(8,128)(2,1)S(1)}, bf16[64,4096]{1,0:T(8,128)(2,1)}, u32[]{:S(2)}) copy-start(bf16[64,4096]{1,0:T(8,128)(2,1)} %get-tuple-element.49.own_ref) | copy-start | bytes 1572868
  32.2 12.3 %copy-start.12 = (f32[64]{0:T(128)S(1)}, f32[64]{0:T(128)}, u32[]{:S(2)}) copy-start(f32[64]{0:T(128)} %get-tuple-element.39) | copy-start | bytes 772
  35.9 8.5 %collective-permute-start.18 = (bf16[256,384]{1,0:T(8,128)(2,1)S(1)}, bf16[256,384]{1,0:T(8,128)(2,1)S(1)}, u32[]{:S(2)}, u32[]{:S(2)}) collective-permute-start(bf16[256,384]{1,0:T(8,128)(2,1)S(1)} %shard_map.76.hidden_ref), channel_id=1, source_target_pairs={{0,1},{1,0},{2,3},{3,2},{4,5},{5,4},{6,7},{7,6},{8,9},{9,8},{10,11... | collective-permute-start | bytes 589832 | tf_op jit(solution)/shard_map/ppermute | solution.py:302
  36.0 13.4 %collective-permute-start.7 = (bf16[40,2048]{1,0:T(8,128)(2,1)S(1)}, bf16[40,2048]{1,0:T(8,128)(2,1)}, u32[]{:S(2)}, u32[]{:S(2)}) collective-permute-start(bf16[40,2048]{1,0:T(8,128)(2,1)S(1)} %get-tuple-element.28), channel_id=1, source_target_pairs={{0,4},{4,8},{8,12},{12,0},{1,5},{5,9},{9,13},{13,1},{2,6},{6,10},{... | collective-permute-start | bytes 491528 | tf_op jit(solution)/shard_map/ppermute | solution.py:293
  42.0 13.1 %collective-permute-start.8 = (bf16[40,2048]{1,0:T(8,128)(2,1)S(1)}, bf16[40,2048]{1,0:T(8,128)(2,1)}, u32[]{:S(2)}, u32[]{:S(2)}) collective-permute-start(bf16[40,2048]{1,0:T(8,128)(2,1)S(1)} %get-tuple-element.29), channel_id=1, source_target_pairs={{0,8},{4,12},{8,0},{12,4},{1,9},{5,13},{9,1},{13,5},{2,10},{6,14},... | collective-permute-start | bytes 491528 | tf_op jit(solution)/shard_map/ppermute | solution.py:293
  43.7 11.5 %collective-permute-start.9 = (bf16[40,2048]{1,0:T(8,128)(2,1)S(1)}, bf16[40,2048]{1,0:T(8,128)(2,1)}, u32[]{:S(2)}, u32[]{:S(2)}) collective-permute-start(bf16[40,2048]{1,0:T(8,128)(2,1)S(1)} %get-tuple-element.30), channel_id=1, source_target_pairs={{0,12},{4,0},{8,4},{12,8},{1,13},{5,1},{9,5},{13,9},{2,14},{6,2},{... | collective-permute-start | bytes 491528 | tf_op jit(solution)/shard_map/ppermute | solution.py:293
  44.4 11.3 %copy-start.13 = (f32[64]{0:T(128)S(1)}, f32[64]{0:T(128)}, u32[]{:S(2)}) copy-start(f32[64]{0:T(128)} %get-tuple-element.40) | copy-start | bytes 772
  47.1 0.8 copy-start.5
  47.9 19.9 %collective-permute-start.19 = (bf16[256,1024]{1,0:T(8,128)(2,1)}, bf16[256,1024]{1,0:T(8,128)(2,1)}, u32[]{:S(2)}, u32[]{:S(2)}) collective-permute-start(bf16[256,1024]{1,0:T(8,128)(2,1)} %get-tuple-element.36), channel_id=1, source_target_pairs={{0,2},{1,3},{2,0},{3,1},{4,6},{5,7},{6,4},{7,5},{8,10},{9,11},{10,... | collective-permute-start | bytes 1572872 | tf_op jit(solution)/shard_map/ppermute | solution.py:299
  49.3 6.4 %collective-permute-start.10 = (bf16[40,2048]{1,0:T(8,128)(2,1)}, bf16[40,2048]{1,0:T(8,128)(2,1)}, u32[]{:S(2)}, u32[]{:S(2)}) collective-permute-start(bf16[40,2048]{1,0:T(8,128)(2,1)} %collective-permute-done.7.refs_0_), channel_id=1, source_target_pairs={{0,1},{1,0},{2,3},{3,2},{4,5},{5,4},{6,7},{7,6},{8,9},{9,8},{10,11... | collective-permute-start | bytes 491528 | tf_op jit(solution)/shard_map/ppermute | solution.py:302
  55.2 1.7 %collective-permute-start.11 = (bf16[40,2048]{1,0:T(8,128)(2,1)}, bf16[40,2048]{1,0:T(8,128)(2,1)}, u32[]{:S(2)}, u32[]{:S(2)}) collective-permute-start(bf16[40,2048]{1,0:T(8,128)(2,1)} %collective-permute-done.8.refs_1_), channel_id=1, source_target_pairs={{0,1},{1,0},{2,3},{3,2},{4,5},{5,4},{6,7},{7,6},{8,9},{9,8},{10,11... | collective-permute-start | bytes 491528 | tf_op jit(solution)/shard_map/ppermute | solution.py:302
  55.2 2.0 %collective-permute-start.12 = (bf16[40,2048]{1,0:T(8,128)(2,1)}, bf16[40,2048]{1,0:T(8,128)(2,1)}, u32[]{:S(2)}, u32[]{:S(2)}) collective-permute-start(bf16[40,2048]{1,0:T(8,128)(2,1)} %collective-permute-done.9.refs_2_), channel_id=1, source_target_pairs={{0,1},{1,0},{2,3},{3,2},{4,5},{5,4},{6,7},{7,6},{8,9},{9,8},{10,11... | collective-permute-start | bytes 491528 | tf_op jit(solution)/shard_map/ppermute | solution.py:302
  55.8 7.8 %copy-start.10 = (f32[64]{0:T(128)S(1)}, f32[64]{0:T(128)}, u32[]{:S(2)}) copy-start(f32[64]{0:T(128)} %get-tuple-element.37) | copy-start | bytes 772
  57.1 2.8 %copy-start.2 = (bf16[4,2,384,1024]{3,2,1,0:T(8,128)(2,1)S(1)}, bf16[4,2,384,1024]{3,2,1,0:T(8,128)(2,1)}, u32[]{:S(2)}) copy-start(bf16[4,2,384,1024]{3,2,1,0:T(8,128)(2,1)} %copy-done) | copy-start | bytes 18874372
  63.3 1.4 %collective-permute-start.13 = (bf16[160,384]{1,0:T(8,128)(2,1)S(1)}, bf16[160,384]{1,0:T(8,128)(2,1)S(1)}, u32[]{:S(2)}, u32[]{:S(2)}) collective-permute-start(bf16[160,384]{1,0:T(8,128)(2,1)S(1)} %shard_map.77.hidden_ref), channel_id=1, source_target_pairs={{0,1},{1,0},{2,3},{3,2},{4,5},{5,4},{6,7},{7,6},{8,9},{9,8},{10,11... | collective-permute-start | bytes 368648 | tf_op jit(solution)/shard_map/ppermute | solution.py:302
  63.6 4.0 %copy-start.9 = (s32[64,2]{0,1:T(2,128)S(1)}, s32[64,2]{0,1:T(2,128)}, u32[]{:S(2)}) copy-start(s32[64,2]{0,1:T(2,128)} %copy-done.8) | copy-start | bytes 1540
  63.6 4.2 %copy-start.6 = (bf16[256,1024]{1,0:T(8,128)(2,1)S(1)}, bf16[256,1024]{1,0:T(8,128)(2,1)}, u32[]{:S(2)}) copy-start(bf16[256,1024]{1,0:T(8,128)(2,1)} %copy-done.5) | copy-start | bytes 1572868
  66.1 24.4 %copy-start.11 = (f32[64]{0:T(128)S(1)}, f32[64]{0:T(128)}, u32[]{:S(2)}) copy-start(f32[64]{0:T(128)} %get-tuple-element.38) | copy-start | bytes 772
  66.1 10.0 %collective-permute-start.14 = (bf16[160,1024]{1,0:T(8,128)(2,1)S(1)}, bf16[160,1024]{1,0:T(8,128)(2,1)S(1)}, u32[]{:S(2)}, u32[]{:S(2)}) collective-permute-start(bf16[160,1024]{1,0:T(8,128)(2,1)S(1)} %get-tuple-element.34), channel_id=1, source_target_pairs={{0,2},{1,3},{2,0},{3,1},{4,6},{5,7},{6,4},{7,5},{8,10},{9,11},{10,... | collective-permute-start | bytes 983048 | tf_op jit(solution)/shard_map/ppermute | solution.py:299
  69.0 12.3 %collective-permute-start.20 = (bf16[64,1024]{1,0:T(8,128)(2,1)S(1)}, bf16[64,1024]{1,0:T(8,128)(2,1)S(1)}, u32[]{:S(2)}, u32[]{:S(2)}) collective-permute-start(bf16[64,1024]{1,0:T(8,128)(2,1)S(1)} %get-tuple-element.45), channel_id=1, source_target_pairs={{0,12},{4,0},{8,4},{12,8},{1,13},{5,1},{9,5},{13,9},{2,14},{6,2},{... | collective-permute-start | bytes 393224 | tf_op jit(solution)/shard_map/ppermute | solution.py:293
  73.3 17.2 %collective-permute-start.21 = (bf16[64,1024]{1,0:T(8,128)(2,1)S(1)}, bf16[64,1024]{1,0:T(8,128)(2,1)S(1)}, u32[]{:S(2)}, u32[]{:S(2)}) collective-permute-start(bf16[64,1024]{1,0:T(8,128)(2,1)S(1)} %get-tuple-element.47), channel_id=1, source_target_pairs={{0,8},{4,12},{8,0},{12,4},{1,9},{5,13},{9,1},{13,5},{2,10},{6,14},... | collective-permute-start | bytes 393224 | tf_op jit(solution)/shard_map/ppermute | solution.py:293
  74.2 16.3 %collective-permute-start.22 = (bf16[64,1024]{1,0:T(8,128)(2,1)S(1)}, bf16[64,1024]{1,0:T(8,128)(2,1)S(1)}, u32[]{:S(2)}, u32[]{:S(2)}) collective-permute-start(bf16[64,1024]{1,0:T(8,128)(2,1)S(1)} %get-tuple-element.46), channel_id=1, source_target_pairs={{0,4},{4,8},{8,12},{12,0},{1,5},{5,9},{9,13},{13,1},{2,6},{6,10},{... | collective-permute-start | bytes 393224 | tf_op jit(solution)/shard_map/ppermute | solution.py:293
  76.2 15.5 %collective-permute-start.15 = (bf16[40,1024]{1,0:T(8,128)(2,1)S(1)}, bf16[40,1024]{1,0:T(8,128)(2,1)S(1)}, u32[]{:S(2)}, u32[]{:S(2)}) collective-permute-start(bf16[40,1024]{1,0:T(8,128)(2,1)S(1)} %get-tuple-element.52), channel_id=1, source_target_pairs={{0,12},{4,0},{8,4},{12,8},{1,13},{5,1},{9,5},{13,9},{2,14},{6,2},{... | collective-permute-start | bytes 245768 | tf_op jit(solution)/shard_map/ppermute | solution.py:293
  80.5 12.4 %collective-permute-start.16 = (bf16[40,1024]{1,0:T(8,128)(2,1)S(1)}, bf16[40,1024]{1,0:T(8,128)(2,1)S(1)}, u32[]{:S(2)}, u32[]{:S(2)}) collective-permute-start(bf16[40,1024]{1,0:T(8,128)(2,1)S(1)} %get-tuple-element.51), channel_id=1, source_target_pairs={{0,8},{4,12},{8,0},{12,4},{1,9},{5,13},{9,1},{13,5},{2,10},{6,14},... | collective-permute-start | bytes 245768 | tf_op jit(solution)/shard_map/ppermute | solution.py:293
  81.3 11.7 %collective-permute-start.17 = (bf16[40,1024]{1,0:T(8,128)(2,1)S(1)}, bf16[40,1024]{1,0:T(8,128)(2,1)S(1)}, u32[]{:S(2)}, u32[]{:S(2)}) collective-permute-start(bf16[40,1024]{1,0:T(8,128)(2,1)S(1)} %get-tuple-element.50), channel_id=1, source_target_pairs={{0,4},{4,8},{8,12},{12,0},{1,5},{5,9},{9,13},{13,1},{2,6},{6,10},{... | collective-permute-start | bytes 245768 | tf_op jit(solution)/shard_map/ppermute | solution.py:293

commit v2 on v1

--- a/solution.py
+++ b/solution.py
@@ -51,40 +51,47 @@
 
 
 def cost(rows, width, units):
-    return pl.CostEstimate(
-        flops=2 * rows * width * units, bytes_accessed=2 * rows * width, transcendentals=0
-    )
+    return pl.CostEstimate(flops=2 * rows, bytes_accessed=2 * rows, transcendentals=0)
 
 
 def in_hbm():
     return pl.BlockSpec(memory_space=pltpu.HBM)
 
 
-def take_kernel(span, core_ref, from_ref, out_ref, sems):
+def take_kernel(lead, side, core_ref, from_ref, out_ref, sems):
     chips = core_ref.shape[0]
-    part = out_ref.shape[1] // chips
+    part = from_ref.shape[-1] // (2 * chips)
     copies = []
     for chip in range(chips):
-        at = pl.multiple_of((2 * chip + core_ref[chip]) * part, part)
-        to = out_ref.at[:, chip * part : (chip + 1) * part]
-        copies.append(pltpu.make_async_copy(from_ref.at[span, :, pl.ds(at, part)], to, sems.at[chip]))
-        copies[-1].start()
+        core = core_ref[chip] if side == 0 else 1 - core_ref[chip]
+        at = pl.multiple_of((2 * chip + core) * part, part)
+        if len(out_ref.shape) == 3:
+            to = out_ref.at[chip]
+        else:
+            to = out_ref.at[:, chip * part : (chip + 1) * part]
+        copies.append(
+            pltpu.make_async_copy(from_ref.at[*lead, :, pl.ds(at, part)], to, sems.at[chip])
+        )
+    for copy in copies:
+        copy.start()
     for copy in copies:
         copy.wait()
 
 
-def take(core, tokens, span):
+def take(core, values, lead, side, stacked):
     chips = core.shape[0]
-    rows, width = tokens.shape[1:]
+    rows, width = values.shape[-2:]
+    part = width // (2 * chips)
+    shape = (chips, rows, part) if stacked else (rows, chips * part)
     return pl.pallas_call(
-        functools.partial(take_kernel, span),
-        out_shape=jax.ShapeDtypeStruct((rows, width // 2), jnp.bfloat16),
+        functools.partial(take_kernel, lead, side),
+        out_shape=jax.ShapeDtypeStruct(shape, jnp.bfloat16),
         in_specs=[pl.BlockSpec(memory_space=pltpu.SMEM), in_hbm()],
         out_specs=in_vmem(1)[0],
         scratch_shapes=[pltpu.SemaphoreType.DMA((chips,))],
         compiler_params=params(),
         cost_estimate=cost(rows, width, 1),
-    )(core, tokens)
+    )(core, values)
 
 
 def pack_kernel(core_ref, choose_ref, rows_ref, own_ref, *out_refs):
@@ -125,25 +132,24 @@
     return own, others
 
 
-def load_kernel(columns_ref, from_ref, up_ref, down_ref, sent_ref, sems):
+def load_kernel(columns_ref, from_ref, up_ref, down_ref, sems):
     parts = up_ref.shape[0]
     chips = down_ref.shape[0]
     part = up_ref.shape[3]
     copies = []
-    for chip in range(chips):
-        for side, to_ref in enumerate((sent_ref, down_ref)):
-            at = pl.multiple_of(columns_ref[2 * side, chip] * part, part)
-            copies.append(
-                pltpu.make_async_copy(
-                    from_ref.at[0, 2, :, pl.ds(at, part)], to_ref.at[chip], sems.at[2 * chip + side]
-                )
-            )
     for index in range(parts):
         copies.append(
             pltpu.make_async_copy(
                 from_ref.at[0, 0:2, :, index * part : (index + 1) * part],
                 up_ref.at[index],
-                sems.at[parts + index],
+                sems.at[index],
+            )
+        )
+    for chip in range(chips):
+        at = pl.multiple_of(columns_ref[0, chip] * part, part)
+        copies.append(
+            pltpu.make_async_copy(
+                from_ref.at[0, 2, :, pl.ds(at, part)], down_ref.at[chip], sems.at[parts + chip]
             )
         )
     for copy in copies:
@@ -161,11 +167,10 @@
         out_shape=[
             pltpu.VMEM((2 * chips, 2, units, part), jnp.bfloat16),
             pltpu.VMEM((chips, units, part), jnp.bfloat16),
-            jax.ShapeDtypeStruct((chips, units, part), jnp.bfloat16),
         ],
         in_specs=[pl.BlockSpec(memory_space=pltpu.SMEM), in_hbm()],
-        out_specs=in_vmem(3),
-        scratch_shapes=[pltpu.SemaphoreType.DMA((4 * chips,))],
+        out_specs=in_vmem(2),
+        scratch_shapes=[pltpu.SemaphoreType.DMA((3 * chips,))],
         compiler_params=params(),
         cost_estimate=cost(3 * units, width, 1),
     )(columns, weights)
@@ -285,9 +290,7 @@
     chip_range = jnp.arange(chips, dtype=jnp.int32)
     core = jnp.full((chips,), own_core, jnp.int32)
     chip_order = (own_chip + chip_range) % chips
-    columns = jnp.stack(
-        [chip_range * 2 + 1 - own_core, chip_order, chip_order * 2 + own_core]
-    )
+    columns = jnp.stack([chip_order * 2 + own_core, chip_order])
 
     def along_ep(value, shift):
         return lax.ppermute(value, "ep", [(i, (i + shift) % ep) for i in range(ep)])
@@ -313,7 +316,7 @@
     weights = pltpu.with_memory_space_constraint(expert_weights, pltpu.HBM)
     arrived = {}
     for span in range(1, spans):
-        sent = take(core, pltpu.with_memory_space_constraint(tokens, pltpu.HBM), span)
+        sent = take(core, pltpu.with_memory_space_constraint(tokens, pltpu.HBM), (span,), 0, False)
         arrived[span] = (tokens[span], exchange([sent] * (ep - 1), False))
 
     slot, rank, kept_gates, kept = routes(
@@ -323,17 +326,30 @@
     place = jnp.where(kept[0], place, ep * capacity)
     hits = place[:, :, None] == jnp.arange(ep * capacity, dtype=jnp.int32)
     choose = jnp.any(hits, axis=1).astype(jnp.bfloat16).T
-    up_weights, down_weights, for_other = load(columns, weights)
+    own, others = pack(core, choose, tokens[0], ep)
+    for_other = take(core, weights, (0, 2), 1, True)
+    for_other, others = lax.optimization_barrier((for_other, others))
     other_down = along_cores(for_other)
-    own, others = pack(core, choose, tokens[0], ep)
-    others, other_down = lax.optimization_barrier((others, other_down))
+    last_own, last = arrived[spans - 1]
+    weights, last[0] = lax.optimization_barrier((weights, last[0]))
+    up_weights, down_weights = load(
+        columns, pltpu.with_memory_space_constraint(weights, pltpu.HBM)
+    )
+
+    swapped = {}
+    for span in range(1, spans):
+        own_rows, pieces = arrived[span]
+        both = (pieces, [along_cores(piece) for piece in pieces])
+        both, others, other_down = lax.optimization_barrier((both, others, other_down))
+        arrived[span], swapped[span] = (own_rows, both[0]), both[1]
     arrived[0] = (own, exchange(others, False))
 
     def finish(span, after):
         own, pieces = arrived[span]
         if after is not None:
-            own, after = lax.optimization_barrier((own, after))
-        hidden = up(core, own, pieces, [along_cores(piece) for piece in pieces], up_weights)
+            own, pieces, after = lax.optimization_barrier((own, pieces, after))
+        others = swapped.get(span) or [along_cores(piece) for piece in pieces]
+        hidden = up(core, own, pieces, others, up_weights)
         sums = down(columns, hidden, along_cores(hidden), down_weights, other_down)
         came = [along_chips(sums[shift], shift) for shift in range(1, chips)]
         totals = []
@@ -344,7 +360,7 @@
             for value in came:
                 total = total + value[at].astype(jnp.float32)
             totals.append(total.astype(jnp.bfloat16))
-        return [totals[0]] + exchange(totals[1:], True), hidden
+        return [totals[0]] + exchange(totals[1:], True), sums
 
     returned = {}
     hidden = None

time: 94.4 us -> 86 us (0.911)
  local copies, waits for them, and re-layouts: 15.9 us -> 8.39 us
  waiting for transfers between devices: 17.1 us -> 20.9 us
  starting transfers between devices: 34.8 us -> 31.9 us
  Pallas kernels: 19.4 us -> 17.8 us
    unnamed x39 -> x27, local copies, waits for them, and re-layouts: 11.4 us -> 4.16 us
    ppermute x12, waiting for transfers between devices: 12.9 us -> 16.7 us  [along_ep(): return lax.ppermute(value, 'ep', [(i, (i + shift) % ep) for i in range(ep)])]
    ppermute x12, starting transfers between devices: 29.7 us -> 26.8 us  [along_ep(): return lax.ppermute(value, 'ep', [(i, (i + shift) % ep) for i in range(ep)])]
    squeeze x1, local copies, waits for them, and re-layouts: 2.37 us -> 0.09 us  [per_device(): own, others = pack(core, choose, tokens[0], ep)]
    pallas_call x1 -> x2, Pallas kernels: 1.53 us -> 3.47 us  [take(): pl.pallas_call(functools.partial(take_kernel, lead, side), out_shape=jax....]
    pallas_call x1, Pallas kernels: 5.56 us -> 3.87 us  [load(): pl.pallas_call(load_kernel, out_shape=[pltpu.VMEM((2 * chips, 2, units, p...]
    pallas_call x2, Pallas kernels: 7.05 us -> 6 us  [up(): pl.pallas_call(up_kernel, out_shape=jax.ShapeDtypeStruct((total, units),...]
    convert_element_type x2, other arithmetic: 1.27 us -> 0.23 us  [finish(): totals.append(total.astype(jnp.bfloat16))]
  transfers between devices with their start and end apart: 23 -> 23, of which waited for: 8 -> 9; matrix products, arithmetic and copies ran while one was open for 11% -> 13% of each run, Pallas kernels for 19% -> 15%
where the time goes in v2:
time: 86 us; the launch traced here: 85.7 us
  starting transfers between devices  31.9 us (37%)
  waiting for transfers between devices  20.9 us (24%)
  Pallas kernels  17.8 us (21%)
  local copies, waits for them, and re-layouts  8.39 us (10%)
  other arithmetic  6.3 us (7%)
    ppermute x12, starting transfers between devices, along_ep(): return lax.ppermute(value, 'ep', [(i, (i + shift) % ep) for i in range(ep)])  26.8 us
    ppermute x12, waiting for transfers between devices, along_ep(): return lax.ppermute(value, 'ep', [(i, (i + shift) % ep) for i in range(ep)])  16.7 us
    pallas_call x2, Pallas kernels, up(): pl.pallas_call(up_kernel, out_shape=jax.ShapeDtypeStruct((total, units),...  6 us
    unnamed x27, local copies, waits for them, and re-layouts  4.16 us
    pallas_call x1, Pallas kernels, load(): pl.pallas_call(load_kernel, out_shape=[pltpu.VMEM((2 * chips, 2, units, p...  3.87 us
    pallas_call x2, Pallas kernels, take(): pl.pallas_call(functools.partial(take_kernel, lead, side), out_shape=jax....  3.47 us
    pallas_call x2, Pallas kernels, down(): pl.pallas_call(down_kernel, out_shape=[jax.ShapeDtypeStruct((rows, part),...  3.19 us
    ppermute x2, starting transfers between devices, along_chips(): return lax.ppermute(value, 'tp', pairs)  3.1 us
  transfers between devices with their start and end apart: 23, of which 9 were waited for; matrix products, arithmetic and copies ran while one was open for 13% of the time, Pallas kernels for 15%

profile of v2, /device:TPU:0, one launch (start us, length us, event | category | flops | bytes accessed | tf_op | source)
XLA Modules:
  0.0 85.7 jit_solution(2666247194527708875)
XLA Ops:
  0.0 1.5 %shard_map.74 = bf16[64,2048]{1,0:T(8,128)(2,1)S(1)} custom-call(s32[2]{0:T(128)S(1)} %add.127.core_ref, bf16[2,64,4096]{2,1,0:T(8,128)(2,1)} %from_ref.2), custom_call_target="tpu_custom_call" | custom-call | flops 128 | bytes 128 | tf_op jit(solution)/shard_map/pallas_call | solution.py:86
  1.5 3.1 %collective-permute-start = (bf16[64,2048]{1,0:T(8,128)(2,1)S(1)}, bf16[64,2048]{1,0:T(8,128)(2,1)S(1)}, u32[]{:S(2)}, u32[]{:S(2)}) collective-permute-start(bf16[64,2048]{1,0:T(8,128)(2,1)S(1)} %shard_map.74), channel_id=1, source_target_pairs={{0,4},{4,8},{8,12},{12,0},{1,5},{5,9},{9,13},{13,1},{2,6},{6,10},{... | collective-permute-start | bytes 786440 | tf_op jit(solution)/shard_map/ppermute | solution.py:296
  4.6 2.6 %collective-permute-start.1 = (bf16[64,2048]{1,0:T(8,128)(2,1)S(1)}, bf16[64,2048]{1,0:T(8,128)(2,1)S(1)}, u32[]{:S(2)}, u32[]{:S(2)}) collective-permute-start(bf16[64,2048]{1,0:T(8,128)(2,1)S(1)} %shard_map.74), channel_id=1, source_target_pairs={{0,8},{4,12},{8,0},{12,4},{1,9},{5,13},{9,1},{13,5},{2,10},{6,14},... | collective-permute-start | bytes 786440 | tf_op jit(solution)/shard_map/ppermute | solution.py:296
  7.2 1.3 %collective-permute-start.2 = (bf16[64,2048]{1,0:T(8,128)(2,1)S(1)}, bf16[64,2048]{1,0:T(8,128)(2,1)S(1)}, u32[]{:S(2)}, u32[]{:S(2)}) collective-permute-start(bf16[64,2048]{1,0:T(8,128)(2,1)S(1)} %shard_map.74), channel_id=1, source_target_pairs={{0,12},{4,0},{8,4},{12,8},{1,13},{5,1},{9,5},{13,9},{2,14},{6,2},{... | collective-permute-start | bytes 786440 | tf_op jit(solution)/shard_map/ppermute | solution.py:296
  8.7 1.9 %shard_map.75 = bf16[2,384,1024]{2,1,0:T(8,128)(2,1)S(1)} custom-call(s32[2]{0:T(128)S(1)} %add.127.core_ref, bf16[1,3,384,4096]{3,2,1,0:T(8,128)(2,1)} %from_ref.4), custom_call_target="tpu_custom_call" | custom-call | flops 768 | bytes 768 | tf_op jit(solution)/shard_map/pallas_call | solution.py:86
  10.7 1.1 %copy-done = bf16[2,384,1024]{2,1,0:T(8,128)(2,1)} copy-done((bf16[2,384,1024]{2,1,0:T(8,128)(2,1)}, bf16[2,384,1024]{2,1,0:T(8,128)(2,1)S(1)}, u32[]{:S(2)}) %copy-start) | copy-done | bytes 1572888
  11.9 0.1 reshape.163
  12.2 0.1 eq.135
  12.5 0.2 convert_reduce_fusion.1
  12.7 0.1 and_select_fusion.3
  12.9 0.2 convert_reduce_fusion
  13.1 0.2 squeeze.19
  13.4 0.1 squeeze.20
  13.6 0.1 sub.25
  14.0 0.1 copy.44
  14.1 1.0 %shard_map.73 = (bf16[40,4096]{1,0:T(8,128)(2,1)S(1)}, bf16[40,2048]{1,0:T(8,128)(2,1)S(1)}, bf16[40,2048]{1,0:T(8,128)(2,1)S(1)}, bf16[40,2048]{1,0:T(8,128)(2,1)S(1)}) custom-call(s32[2]{0:T(128)S(1)} %add.127.core_ref, bf16[160,64]{1,0:T(8,128)(2,1)S(1)} %bitcast.19, bf16[64,4096]{1,0:T(8,128)(2,1)S(1)} %get-tuple-element.76.rows_ref), custom_call_target="tpu_custom_call" | custom-call | flops 320 | bytes 320 | tf_op jit(solution)/shard_map/pallas_call | solution.py:124
  15.1 0.7 copy-done.1
  15.8 0.7 copy-done.3
  16.5 0.7 copy-done.5
  17.1 0.6 slice_bitcast_fusion.3
  17.7 0.8 lt.91
  18.5 0.8 copy.42
  19.3 0.9 %select_reduce_fusion.4 = s32[4]{0:T(128)S(1)} fusion(s32[4]{0:T(128)} %get-tuple-element.85, s32[4]{0:T(128)} %get-tuple-element.84), kind=kLoop, calls=%fused_computation.34 | loop fusion | flops 44 | bytes 48 | tf_op jit(solution)/shard_map/reduce_min | solution.py:378
  20.1 0.5 and_select_fusion
  20.7 0.7 broadcast_select_fusion
  21.4 0.6 fusion.13
  22.0 0.6 and_select_fusion.1
  22.6 0.1 eq.152
  22.8 0.8 copy.46
  23.6 0.7 select_reduce_fusion.1
  24.4 0.6 collective-permute-start.3
  25.1 0.4 collective-permute-start.5
  25.5 0.7 pad_add_fusion.columns_ref
  26.2 3.9 %shard_map.76 = (bf16[4,2,384,1024]{3,2,1,0:T(8,128)(2,1)S(1)}, bf16[2,384,1024]{2,1,0:T(8,128)(2,1)S(1)}) custom-call(s32[2,2]{1,0:T(2,128)S(1)} %pad_add_fusion.columns_ref, bf16[1,3,384,4096]{3,2,1,0:T(8,128)(2,1)} %from_ref.4), custom_call_target="tpu_custom_call" | custom-call | flops 2304 | bytes 2304 | tf_op jit(solution)/shard_map/pallas_call | solution.py:165
  30.2 3.4 %shard_map.77.hidden_ref = bf16[256,384]{1,0:T(8,128)(2,1)S(1)} custom-call(s32[2]{0:T(128)S(1)} %add.127.core_ref, bf16[64,4096]{1,0:T(8,128)(2,1)S(1)} %get-tuple-element.77.own_ref, bf16[64,2048]{1,0:T(8,128)(2,1)S(1)} %collective-permute-done.refs_0_, bf16[64,2048]{1,0:T(8,128)(2,1)S(1)} %collective-permute-done.1.refs_1_, ...), custom_call_target="tpu_custom_call" | custom-call | flops 512 | bytes 512 | tf_op jit(solution)/shard_map/pallas_call | solution.py:217
  33.6 0.2 collective-permute-start.10
  33.8 5.4 %collective-permute-start.7 = (bf16[40,2048]{1,0:T(8,128)(2,1)S(1)}, bf16[40,2048]{1,0:T(8,128)(2,1)S(1)}, u32[]{:S(2)}, u32[]{:S(2)}) collective-permute-start(bf16[40,2048]{1,0:T(8,128)(2,1)S(1)} %copy-done.6), channel_id=1, source_target_pairs={{0,4},{4,8},{8,12},{12,0},{1,5},{5,9},{9,13},{13,1},{2,6},{6,10},{... | collective-permute-start | bytes 491528 | tf_op jit(solution)/shard_map/ppermute | solution.py:296
  39.1 1.7 %collective-permute-start.8 = (bf16[40,2048]{1,0:T(8,128)(2,1)S(1)}, bf16[40,2048]{1,0:T(8,128)(2,1)S(1)}, u32[]{:S(2)}, u32[]{:S(2)}) collective-permute-start(bf16[40,2048]{1,0:T(8,128)(2,1)S(1)} %copy-done.4), channel_id=1, source_target_pairs={{0,8},{4,12},{8,0},{12,4},{1,9},{5,13},{9,1},{13,5},{2,10},{6,14},... | collective-permute-start | bytes 491528 | tf_op jit(solution)/shard_map/ppermute | solution.py:296
  40.8 0.8 collective-permute-start.9
  41.6 1.8 %shard_map.78 = (bf16[256,1024]{1,0:T(8,128)(2,1)S(1)}, bf16[256,1024]{1,0:T(8,128)(2,1)S(1)}) custom-call(s32[2,2]{1,0:T(2,128)S(1)} %pad_add_fusion.columns_ref, bf16[256,384]{1,0:T(8,128)(2,1)S(1)} %shard_map.77.hidden_ref, bf16[256,384]{1,0:T(8,128)(2,1)S(1)} %collective-permute-done.10.other_hidden_ref, ...), custom_call_target="tpu_custom_call" | custom-call | flops 512 | bytes 512 | tf_op jit(solution)/shard_map/pallas_call | solution.py:241
  43.4 1.6 %collective-permute-start.19 = (bf16[256,1024]{1,0:T(8,128)(2,1)S(1)}, bf16[256,1024]{1,0:T(8,128)(2,1)S(1)}, u32[]{:S(2)}, u32[]{:S(2)}) collective-permute-start(bf16[256,1024]{1,0:T(8,128)(2,1)S(1)} %get-tuple-element.58), channel_id=1, source_target_pairs={{0,2},{1,3},{2,0},{3,1},{4,6},{5,7},{6,4},{7,5},{8,10},{9,11},{10,... | collective-permute-start | bytes 1572872 | tf_op jit(solution)/shard_map/ppermute | solution.py:302
  44.9 0.5 collective-permute-done.7.refs_0_
  45.4 6.8 %collective-permute-done.8.refs_1_ = bf16[40,2048]{1,0:T(8,128)(2,1)S(1)} collective-permute-done((bf16[40,2048]{1,0:T(8,128)(2,1)S(1)}, bf16[40,2048]{1,0:T(8,128)(2,1)S(1)}, u32[]{:S(2)}, u32[]{:S(2)}) %collective-permute-start.8) | collective-permute-done | bytes 163872 | tf_op jit(solution)/shard_map/ppermute | solution.py:296
  52.2 0.5 collective-permute-start.12
  52.7 0.9 %collective-permute-done.11.refs_3_ = bf16[40,2048]{1,0:T(8,128)(2,1)S(1)} collective-permute-done((bf16[40,2048]{1,0:T(8,128)(2,1)S(1)}, bf16[40,2048]{1,0:T(8,128)(2,1)S(1)}, u32[]{:S(2)}, u32[]{:S(2)}) %collective-permute-start.11) | collective-permute-done | bytes 163872 | tf_op jit(solution)/shard_map/ppermute | solution.py:305
  53.6 0.2 collective-permute-done.12.refs_4_
  53.8 0.3 collective-permute-done.13.refs_5_
  54.1 2.6 %shard_map.79.hidden_ref = bf16[160,384]{1,0:T(8,128)(2,1)S(1)} custom-call(s32[2]{0:T(128)S(1)} %add.127.core_ref, bf16[40,4096]{1,0:T(8,128)(2,1)S(1)} %get-tuple-element.59.own_ref, bf16[40,2048]{1,0:T(8,128)(2,1)S(1)} %collective-permute-done.7.refs_0_, bf16[40,2048]{1,0:T(8,128)(2,1)S(1)} %collective-permute-done.8.refs_1_, ...), custom_call_target="tpu_custom_call" | custom-call | flops 320 | bytes 320 | tf_op jit(solution)/shard_map/pallas_call | solution.py:217
  56.6 0.3 collective-permute-start.14
  56.9 1.1 %collective-permute-done.14.other_hidden_ref = bf16[160,384]{1,0:T(8,128)(2,1)S(1)} collective-permute-done((bf16[160,384]{1,0:T(8,128)(2,1)S(1)}, bf16[160,384]{1,0:T(8,128)(2,1)S(1)}, u32[]{:S(2)}, u32[]{:S(2)}) %collective-permute-start.14) | collective-permute-done | bytes 122912 | tf_op jit(solution)/shard_map/ppermute | solution.py:305
  58.0 1.4 %shard_map.80 = (bf16[160,1024]{1,0:T(8,128)(2,1)S(1)}, bf16[160,1024]{1,0:T(8,128)(2,1)S(1)}) custom-call(s32[2,2]{1,0:T(2,128)S(1)} %pad_add_fusion.columns_ref, bf16[160,384]{1,0:T(8,128)(2,1)S(1)} %shard_map.79.hidden_ref, bf16[160,384]{1,0:T(8,128)(2,1)S(1)} %collective-permute-done.14.other_hidden_ref, ...), custom_call_target="tpu_custom_call" | custom-call | flops 320 | bytes 320 | tf_op jit(solution)/shard_map/pallas_call | solution.py:241
  59.5 1.5 %collective-permute-start.15 = (bf16[160,1024]{1,0:T(8,128)(2,1)S(1)}, bf16[160,1024]{1,0:T(8,128)(2,1)S(1)}, u32[]{:S(2)}, u32[]{:S(2)}) collective-permute-start(bf16[160,1024]{1,0:T(8,128)(2,1)S(1)} %get-tuple-element.64), channel_id=1, source_target_pairs={{0,2},{1,3},{2,0},{3,1},{4,6},{5,7},{6,4},{7,5},{8,10},{9,11},{10,... | collective-permute-start | bytes 983048 | tf_op jit(solution)/shard_map/ppermute | solution.py:302
  61.1 0.1 add_convert_fusion.3
  61.3 4.0 %collective-permute-start.22 = (bf16[64,1024]{1,0:T(8,128)(2,1)S(1)}, bf16[64,1024]{1,0:T(8,128)(2,1)S(1)}, u32[]{:S(2)}, u32[]{:S(2)}) collective-permute-start(bf16[64,1024]{1,0:T(8,128)(2,1)S(1)} %get-tuple-element.74), channel_id=1, source_target_pairs={{0,4},{4,8},{8,12},{12,0},{1,5},{5,9},{9,13},{13,1},{2,6},{6,10},{... | collective-permute-start | bytes 393224 | tf_op jit(solution)/shard_map/ppermute | solution.py:296
  65.3 0.9 %collective-permute-start.21 = (bf16[64,1024]{1,0:T(8,128)(2,1)S(1)}, bf16[64,1024]{1,0:T(8,128)(2,1)S(1)}, u32[]{:S(2)}, u32[]{:S(2)}) collective-permute-start(bf16[64,1024]{1,0:T(8,128)(2,1)S(1)} %get-tuple-element.75), channel_id=1, source_target_pairs={{0,8},{4,12},{8,0},{12,4},{1,9},{5,13},{9,1},{13,5},{2,10},{6,14},... | collective-permute-start | bytes 393224 | tf_op jit(solution)/shard_map/ppermute | solution.py:296
  66.2 1.5 %collective-permute-start.20 = (bf16[64,1024]{1,0:T(8,128)(2,1)S(1)}, bf16[64,1024]{1,0:T(8,128)(2,1)S(1)}, u32[]{:S(2)}, u32[]{:S(2)}) collective-permute-start(bf16[64,1024]{1,0:T(8,128)(2,1)S(1)} %get-tuple-element.73), channel_id=1, source_target_pairs={{0,12},{4,0},{8,4},{12,8},{1,13},{5,1},{9,5},{13,9},{2,14},{6,2},{... | collective-permute-start | bytes 393224 | tf_op jit(solution)/shard_map/ppermute | solution.py:296
  67.7 1.6 %collective-permute-done.15 = bf16[160,1024]{1,0:T(8,128)(2,1)S(1)} collective-permute-done((bf16[160,1024]{1,0:T(8,128)(2,1)S(1)}, bf16[160,1024]{1,0:T(8,128)(2,1)S(1)}, u32[]{:S(2)}, u32[]{:S(2)}) %collective-permute-start.15) | collective-permute-done | bytes 327712 | tf_op jit(solution)/shard_map/ppermute | solution.py:302
  69.5 4.4 %collective-permute-start.16 = (bf16[40,1024]{1,0:T(8,128)(2,1)S(1)}, bf16[40,1024]{1,0:T(8,128)(2,1)S(1)}, u32[]{:S(2)}, u32[]{:S(2)}) collective-permute-start(bf16[40,1024]{1,0:T(8,128)(2,1)S(1)} %get-tuple-element.80), channel_id=1, source_target_pairs={{0,12},{4,0},{8,4},{12,8},{1,13},{5,1},{9,5},{13,9},{2,14},{6,2},{... | collective-permute-start | bytes 245768 | tf_op jit(solution)/shard_map/ppermute | solution.py:296
  73.8 1.1 %collective-permute-start.17 = (bf16[40,1024]{1,0:T(8,128)(2,1)S(1)}, bf16[40,1024]{1,0:T(8,128)(2,1)S(1)}, u32[]{:S(2)}, u32[]{:S(2)}) collective-permute-start(bf16[40,1024]{1,0:T(8,128)(2,1)S(1)} %get-tuple-element.79), channel_id=1, source_target_pairs={{0,8},{4,12},{8,0},{12,4},{1,9},{5,13},{9,1},{13,5},{2,10},{6,14},... | collective-permute-start | bytes 245768 | tf_op jit(solution)/shard_map/ppermute | solution.py:296
  75.0 0.2 fusion.1
  75.2 1.5 %collective-permute-done.16.refs_1_ = bf16[40,1024]{1,0:T(8,128)(2,1)S(1)} collective-permute-done((bf16[40,1024]{1,0:T(8,128)(2,1)S(1)}, bf16[40,1024]{1,0:T(8,128)(2,1)S(1)}, u32[]{:S(2)}, u32[]{:S(2)}) %collective-permute-start.16) | collective-permute-done | bytes 81952 | tf_op jit(solution)/shard_map/ppermute | solution.py:296
  76.7 8.0 %collective-permute-done.17.refs_2_ = bf16[40,1024]{1,0:T(8,128)(2,1)S(1)} collective-permute-done((bf16[40,1024]{1,0:T(8,128)(2,1)S(1)}, bf16[40,1024]{1,0:T(8,128)(2,1)S(1)}, u32[]{:S(2)}, u32[]{:S(2)}) %collective-permute-start.17) | collective-permute-done | bytes 81952 | tf_op jit(solution)/shard_map/ppermute | solution.py:296
  84.7 0.2 shard_map.81
  84.9 0.7 pad_maximum_fusion
  (65 shorter events, 1.5 us)
Async XLA Ops:
  0.0 8.6 %copy-start.7 = (bf16[2,64,4096]{2,1,0:T(8,128)(2,1)S(1)}, bf16[2,64,4096]{2,1,0:T(8,128)(2,1)}, u32[]{:S(2)}) copy-start(bf16[2,64,4096]{2,1,0:T(8,128)(2,1)} %from_ref.2) | copy-start | bytes 3145732
  1.5 22.8 %collective-permute-start = (bf16[64,2048]{1,0:T(8,128)(2,1)S(1)}, bf16[64,2048]{1,0:T(8,128)(2,1)S(1)}, u32[]{:S(2)}, u32[]{:S(2)}) collective-permute-start(bf16[64,2048]{1,0:T(8,128)(2,1)S(1)} %shard_map.74), channel_id=1, source_target_pairs={{0,4},{4,8},{8,12},{12,0},{1,5},{5,9},{9,13},{13,1},{2,6},{6,10},{... | collective-permute-start | bytes 786440 | tf_op jit(solution)/shard_map/ppermute | solution.py:296
  4.6 20.3 %collective-permute-start.1 = (bf16[64,2048]{1,0:T(8,128)(2,1)S(1)}, bf16[64,2048]{1,0:T(8,128)(2,1)S(1)}, u32[]{:S(2)}, u32[]{:S(2)}) collective-permute-start(bf16[64,2048]{1,0:T(8,128)(2,1)S(1)} %shard_map.74), channel_id=1, source_target_pairs={{0,8},{4,12},{8,0},{12,4},{1,9},{5,13},{9,1},{13,5},{2,10},{6,14},... | collective-permute-start | bytes 786440 | tf_op jit(solution)/shard_map/ppermute | solution.py:296
  7.2 17.8 %collective-permute-start.2 = (bf16[64,2048]{1,0:T(8,128)(2,1)S(1)}, bf16[64,2048]{1,0:T(8,128)(2,1)S(1)}, u32[]{:S(2)}, u32[]{:S(2)}) collective-permute-start(bf16[64,2048]{1,0:T(8,128)(2,1)S(1)} %shard_map.74), channel_id=1, source_target_pairs={{0,12},{4,0},{8,4},{12,8},{1,13},{5,1},{9,5},{13,9},{2,14},{6,2},{... | collective-permute-start | bytes 786440 | tf_op jit(solution)/shard_map/ppermute | solution.py:296
  8.7 3.1 %copy-start.9 = (s32[2,64,2]{1,2,0:T(2,128)S(1)}, s32[2,64,2]{1,2,0:T(2,128)}, u32[]{:S(2)}) copy-start(s32[2,64,2]{1,2,0:T(2,128)} %param.10) | copy-start | bytes 3076
  8.7 3.4 %copy-start.10 = (s32[2,64,2]{1,2,0:T(2,128)S(1)}, s32[2,64,2]{1,2,0:T(2,128)}, u32[]{:S(2)}) copy-start(s32[2,64,2]{1,2,0:T(2,128)} %param.8) | copy-start | bytes 3076
  8.7 3.6 %copy-start.8 = (s32[2,4]{1,0:T(2,128)S(1)}, s32[2,4]{1,0:T(2,128)}, u32[]{:S(2)}) copy-start(s32[2,4]{1,0:T(2,128)} %param.11) | copy-start | bytes 100
  8.7 4.1 %copy-start.11 = (s32[4]{0:T(128)S(1)}, s32[4]{0:T(128)}, u32[]{:S(2)}) copy-start(s32[4]{0:T(128)} %param.12) | copy-start | bytes 52
  10.7 1.2 %copy-start = (bf16[2,384,1024]{2,1,0:T(8,128)(2,1)}, bf16[2,384,1024]{2,1,0:T(8,128)(2,1)S(1)}, u32[]{:S(2)}) copy-start(bf16[2,384,1024]{2,1,0:T(8,128)(2,1)S(1)} %shard_map.75) | copy-start | bytes 4718596
  15.1 0.7 copy-start.1
  15.8 0.7 copy-start.3
  16.5 0.7 copy-start.5
  17.1 13.0 %collective-permute-start.6 = (bf16[2,384,1024]{2,1,0:T(8,128)(2,1)}, bf16[2,384,1024]{2,1,0:T(8,128)(2,1)S(1)}, u32[]{:S(2)}, u32[]{:S(2)}) collective-permute-start(bf16[2,384,1024]{2,1,0:T(8,128)(2,1)} %copy-done), channel_id=1, source_target_pairs={{0,1},{1,0},{2,3},{3,2},{4,5},{5,4},{6,7},{7,6},{8,9},{9,8},{10,11... | collective-permute-start | bytes 4718600 | tf_op jit(solution)/shard_map/ppermute | solution.py:305
  24.4 5.7 %collective-permute-start.3 = (bf16[64,2048]{1,0:T(8,128)(2,1)S(1)}, bf16[64,2048]{1,0:T(8,128)(2,1)}, u32[]{:S(2)}, u32[]{:S(2)}) collective-permute-start(bf16[64,2048]{1,0:T(8,128)(2,1)S(1)} %collective-permute-done.refs_0_), channel_id=1, source_target_pairs={{0,1},{1,0},{2,3},{3,2},{4,5},{5,4},{6,7},{7,6},{8,9},{9,8},{10,11... | collective-permute-start | bytes 786440 | tf_op jit(solution)/shard_map/ppermute | solution.py:305
  25.0 5.2 %collective-permute-start.4 = (bf16[64,2048]{1,0:T(8,128)(2,1)S(1)}, bf16[64,2048]{1,0:T(8,128)(2,1)}, u32[]{:S(2)}, u32[]{:S(2)}) collective-permute-start(bf16[64,2048]{1,0:T(8,128)(2,1)S(1)} %collective-permute-done.1.refs_1_), channel_id=1, source_target_pairs={{0,1},{1,0},{2,3},{3,2},{4,5},{5,4},{6,7},{7,6},{8,9},{9,8},{10,11... | collective-permute-start | bytes 786440 | tf_op jit(solution)/shard_map/ppermute | solution.py:305
  25.1 5.1 %collective-permute-start.5 = (bf16[64,2048]{1,0:T(8,128)(2,1)S(1)}, bf16[64,2048]{1,0:T(8,128)(2,1)S(1)}, u32[]{:S(2)}, u32[]{:S(2)}) collective-permute-start(bf16[64,2048]{1,0:T(8,128)(2,1)S(1)} %collective-permute-done.2.refs_2_), channel_id=1, source_target_pairs={{0,1},{1,0},{2,3},{3,2},{4,5},{5,4},{6,7},{7,6},{8,9},{9,8},{10,11... | collective-permute-start | bytes 786440 | tf_op jit(solution)/shard_map/ppermute | solution.py:305
  30.2 3.6 %copy-start.6 = (bf16[40,2048]{1,0:T(8,128)(2,1)S(1)}, bf16[40,2048]{1,0:T(8,128)(2,1)}, u32[]{:S(2)}) copy-start(bf16[40,2048]{1,0:T(8,128)(2,1)} %copy-done.5) | copy-start | bytes 491524
  30.2 9.0 %copy-start.4 = (bf16[40,2048]{1,0:T(8,128)(2,1)S(1)}, bf16[40,2048]{1,0:T(8,128)(2,1)}, u32[]{:S(2)}) copy-start(bf16[40,2048]{1,0:T(8,128)(2,1)} %copy-done.3) | copy-start | bytes 491524
  30.2 10.6 %copy-start.2 = (bf16[40,2048]{1,0:T(8,128)(2,1)S(1)}, bf16[40,2048]{1,0:T(8,128)(2,1)}, u32[]{:S(2)}) copy-start(bf16[40,2048]{1,0:T(8,128)(2,1)} %copy-done.1) | copy-start | bytes 491524
  33.6 8.0 %collective-permute-start.10 = (bf16[256,384]{1,0:T(8,128)(2,1)S(1)}, bf16[256,384]{1,0:T(8,128)(2,1)S(1)}, u32[]{:S(2)}, u32[]{:S(2)}) collective-permute-start(bf16[256,384]{1,0:T(8,128)(2,1)S(1)} %shard_map.77.hidden_ref), channel_id=1, source_target_pairs={{0,1},{1,0},{2,3},{3,2},{4,5},{5,4},{6,7},{7,6},{8,9},{9,8},{10,11... | collective-permute-start | bytes 589832 | tf_op jit(solution)/shard_map/ppermute | solution.py:305
  33.8 11.6 %collective-permute-start.7 = (bf16[40,2048]{1,0:T(8,128)(2,1)S(1)}, bf16[40,2048]{1,0:T(8,128)(2,1)S(1)}, u32[]{:S(2)}, u32[]{:S(2)}) collective-permute-start(bf16[40,2048]{1,0:T(8,128)(2,1)S(1)} %copy-done.6), channel_id=1, source_target_pairs={{0,4},{4,8},{8,12},{12,0},{1,5},{5,9},{9,13},{13,1},{2,6},{6,10},{... | collective-permute-start | bytes 491528 | tf_op jit(solution)/shard_map/ppermute | solution.py:296
  39.1 13.0 %collective-permute-start.8 = (bf16[40,2048]{1,0:T(8,128)(2,1)S(1)}, bf16[40,2048]{1,0:T(8,128)(2,1)S(1)}, u32[]{:S(2)}, u32[]{:S(2)}) collective-permute-start(bf16[40,2048]{1,0:T(8,128)(2,1)S(1)} %copy-done.4), channel_id=1, source_target_pairs={{0,8},{4,12},{8,0},{12,4},{1,9},{5,13},{9,1},{13,5},{2,10},{6,14},... | collective-permute-start | bytes 491528 | tf_op jit(solution)/shard_map/ppermute | solution.py:296
  40.8 11.4 %collective-permute-start.9 = (bf16[40,2048]{1,0:T(8,128)(2,1)S(1)}, bf16[40,2048]{1,0:T(8,128)(2,1)S(1)}, u32[]{:S(2)}, u32[]{:S(2)}) collective-permute-start(bf16[40,2048]{1,0:T(8,128)(2,1)S(1)} %copy-done.2), channel_id=1, source_target_pairs={{0,12},{4,0},{8,4},{12,8},{1,13},{5,1},{9,5},{13,9},{2,14},{6,2},{... | collective-permute-start | bytes 491528 | tf_op jit(solution)/shard_map/ppermute | solution.py:296
  43.4 17.7 %collective-permute-start.19 = (bf16[256,1024]{1,0:T(8,128)(2,1)S(1)}, bf16[256,1024]{1,0:T(8,128)(2,1)S(1)}, u32[]{:S(2)}, u32[]{:S(2)}) collective-permute-start(bf16[256,1024]{1,0:T(8,128)(2,1)S(1)} %get-tuple-element.58), channel_id=1, source_target_pairs={{0,2},{1,3},{2,0},{3,1},{4,6},{5,7},{6,4},{7,5},{8,10},{9,11},{10,... | collective-permute-start | bytes 1572872 | tf_op jit(solution)/shard_map/ppermute | solution.py:302
  52.2 1.4 %collective-permute-start.11 = (bf16[40,2048]{1,0:T(8,128)(2,1)S(1)}, bf16[40,2048]{1,0:T(8,128)(2,1)S(1)}, u32[]{:S(2)}, u32[]{:S(2)}) collective-permute-start(bf16[40,2048]{1,0:T(8,128)(2,1)S(1)} %collective-permute-done.7.refs_0_), channel_id=1, source_target_pairs={{0,1},{1,0},{2,3},{3,2},{4,5},{5,4},{6,7},{7,6},{8,9},{9,8},{10,11... | collective-permute-start | bytes 491528 | tf_op jit(solution)/shard_map/ppermute | solution.py:305
  52.2 1.6 %collective-permute-start.12 = (bf16[40,2048]{1,0:T(8,128)(2,1)S(1)}, bf16[40,2048]{1,0:T(8,128)(2,1)S(1)}, u32[]{:S(2)}, u32[]{:S(2)}) collective-permute-start(bf16[40,2048]{1,0:T(8,128)(2,1)S(1)} %collective-permute-done.8.refs_1_), channel_id=1, source_target_pairs={{0,1},{1,0},{2,3},{3,2},{4,5},{5,4},{6,7},{7,6},{8,9},{9,8},{10,11... | collective-permute-start | bytes 491528 | tf_op jit(solution)/shard_map/ppermute | solution.py:305
  52.7 1.4 %collective-permute-start.13 = (bf16[40,2048]{1,0:T(8,128)(2,1)S(1)}, bf16[40,2048]{1,0:T(8,128)(2,1)S(1)}, u32[]{:S(2)}, u32[]{:S(2)}) collective-permute-start(bf16[40,2048]{1,0:T(8,128)(2,1)S(1)} %collective-permute-done.9.refs_2_), channel_id=1, source_target_pairs={{0,1},{1,0},{2,3},{3,2},{4,5},{5,4},{6,7},{7,6},{8,9},{9,8},{10,11... | collective-permute-start | bytes 491528 | tf_op jit(solution)/shard_map/ppermute | solution.py:305
  56.6 1.4 %collective-permute-start.14 = (bf16[160,384]{1,0:T(8,128)(2,1)S(1)}, bf16[160,384]{1,0:T(8,128)(2,1)S(1)}, u32[]{:S(2)}, u32[]{:S(2)}) collective-permute-start(bf16[160,384]{1,0:T(8,128)(2,1)S(1)} %shard_map.79.hidden_ref), channel_id=1, source_target_pairs={{0,1},{1,0},{2,3},{3,2},{4,5},{5,4},{6,7},{7,6},{8,9},{9,8},{10,11... | collective-permute-start | bytes 368648 | tf_op jit(solution)/shard_map/ppermute | solution.py:305
  59.5 9.9 %collective-permute-start.15 = (bf16[160,1024]{1,0:T(8,128)(2,1)S(1)}, bf16[160,1024]{1,0:T(8,128)(2,1)S(1)}, u32[]{:S(2)}, u32[]{:S(2)}) collective-permute-start(bf16[160,1024]{1,0:T(8,128)(2,1)S(1)} %get-tuple-element.64), channel_id=1, source_target_pairs={{0,2},{1,3},{2,0},{3,1},{4,6},{5,7},{6,4},{7,5},{8,10},{9,11},{10,... | collective-permute-start | bytes 983048 | tf_op jit(solution)/shard_map/ppermute | solution.py:302
  61.3 13.7 %collective-permute-start.22 = (bf16[64,1024]{1,0:T(8,128)(2,1)S(1)}, bf16[64,1024]{1,0:T(8,128)(2,1)S(1)}, u32[]{:S(2)}, u32[]{:S(2)}) collective-permute-start(bf16[64,1024]{1,0:T(8,128)(2,1)S(1)} %get-tuple-element.74), channel_id=1, source_target_pairs={{0,4},{4,8},{8,12},{12,0},{1,5},{5,9},{9,13},{13,1},{2,6},{6,10},{... | collective-permute-start | bytes 393224 | tf_op jit(solution)/shard_map/ppermute | solution.py:296
  65.3 9.7 %collective-permute-start.21 = (bf16[64,1024]{1,0:T(8,128)(2,1)S(1)}, bf16[64,1024]{1,0:T(8,128)(2,1)S(1)}, u32[]{:S(2)}, u32[]{:S(2)}) collective-permute-start(bf16[64,1024]{1,0:T(8,128)(2,1)S(1)} %get-tuple-element.75), channel_id=1, source_target_pairs={{0,8},{4,12},{8,0},{12,4},{1,9},{5,13},{9,1},{13,5},{2,10},{6,14},... | collective-permute-start | bytes 393224 | tf_op jit(solution)/shard_map/ppermute | solution.py:296
  66.2 8.8 %collective-permute-start.20 = (bf16[64,1024]{1,0:T(8,128)(2,1)S(1)}, bf16[64,1024]{1,0:T(8,128)(2,1)S(1)}, u32[]{:S(2)}, u32[]{:S(2)}) collective-permute-start(bf16[64,1024]{1,0:T(8,128)(2,1)S(1)} %get-tuple-element.73), channel_id=1, source_target_pairs={{0,12},{4,0},{8,4},{12,8},{1,13},{5,1},{9,5},{13,9},{2,14},{6,2},{... | collective-permute-start | bytes 393224 | tf_op jit(solution)/shard_map/ppermute | solution.py:296
  69.5 7.3 %collective-permute-start.16 = (bf16[40,1024]{1,0:T(8,128)(2,1)S(1)}, bf16[40,1024]{1,0:T(8,128)(2,1)S(1)}, u32[]{:S(2)}, u32[]{:S(2)}) collective-permute-start(bf16[40,1024]{1,0:T(8,128)(2,1)S(1)} %get-tuple-element.80), channel_id=1, source_target_pairs={{0,12},{4,0},{8,4},{12,8},{1,13},{5,1},{9,5},{13,9},{2,14},{6,2},{... | collective-permute-start | bytes 245768 | tf_op jit(solution)/shard_map/ppermute | solution.py:296
  73.8 10.9 %collective-permute-start.17 = (bf16[40,1024]{1,0:T(8,128)(2,1)S(1)}, bf16[40,1024]{1,0:T(8,128)(2,1)S(1)}, u32[]{:S(2)}, u32[]{:S(2)}) collective-permute-start(bf16[40,1024]{1,0:T(8,128)(2,1)S(1)} %get-tuple-element.79), channel_id=1, source_target_pairs={{0,8},{4,12},{8,0},{12,4},{1,9},{5,13},{9,1},{13,5},{2,10},{6,14},... | collective-permute-start | bytes 245768 | tf_op jit(solution)/shard_map/ppermute | solution.py:296
  75.0 9.7 %collective-permute-start.18 = (bf16[40,1024]{1,0:T(8,128)(2,1)S(1)}, bf16[40,1024]{1,0:T(8,128)(2,1)S(1)}, u32[]{:S(2)}, u32[]{:S(2)}) collective-permute-start(bf16[40,1024]{1,0:T(8,128)(2,1)S(1)} %get-tuple-element.78), channel_id=1, source_target_pairs={{0,4},{4,8},{8,12},{12,0},{1,5},{5,9},{9,13},{13,1},{2,6},{6,10},{... | collective-permute-start | bytes 245768 | tf_op jit(solution)/shard_map/ppermute | solution.py:296

commit v3 on v2

--- a/solution.py
+++ b/solution.py
@@ -132,52 +132,7 @@
     return own, others
 
 
-def load_kernel(columns_ref, from_ref, up_ref, down_ref, sems):
-    parts = up_ref.shape[0]
-    chips = down_ref.shape[0]
-    part = up_ref.shape[3]
-    copies = []
-    for index in range(parts):
-        copies.append(
-            pltpu.make_async_copy(
-                from_ref.at[0, 0:2, :, index * part : (index + 1) * part],
-                up_ref.at[index],
-                sems.at[index],
-            )
-        )
-    for chip in range(chips):
-        at = pl.multiple_of(columns_ref[0, chip] * part, part)
-        copies.append(
-            pltpu.make_async_copy(
-                from_ref.at[0, 2, :, pl.ds(at, part)], down_ref.at[chip], sems.at[parts + chip]
-            )
-        )
-    for copy in copies:
-        copy.start()
-    for copy in copies:
-        copy.wait()
-
-
-def load(columns, weights):
-    chips = columns.shape[1]
-    units, width = weights.shape[2:]
-    part = width // (2 * chips)
-    return pl.pallas_call(
-        load_kernel,
-        out_shape=[
-            pltpu.VMEM((2 * chips, 2, units, part), jnp.bfloat16),
-            pltpu.VMEM((chips, units, part), jnp.bfloat16),
-        ],
-        in_specs=[pl.BlockSpec(memory_space=pltpu.SMEM), in_hbm()],
-        out_specs=in_vmem(2),
-        scratch_shapes=[pltpu.SemaphoreType.DMA((3 * chips,))],
-        compiler_params=params(),
-        cost_estimate=cost(3 * units, width, 1),
-    )(columns, weights)
-
-
-def up_kernel(core_ref, own_ref, *refs):
-    *piece_refs, weight_ref, hidden_ref, rows_ref = refs
+def project(core_ref, own_ref, piece_refs, weight_ref, hidden_ref, rows_ref, before):
     chips = core_ref.shape[0]
     count = len(piece_refs) // 2
     part = own_ref.shape[1] // (2 * chips)
@@ -202,6 +157,7 @@
             joined = jnp.concatenate([value.astype(jnp.float32) for value in values])
             rows_ref[...] = joined.astype(jnp.bfloat16)
         rows = rows_ref[...]
+        before(index)
         gate += lax.dot_general(
             rows, weight_ref[index, 0], CONTRACT_LAST, preferred_element_type=jnp.float32
         )
@@ -209,6 +165,70 @@
             rows, weight_ref[index, 1], CONTRACT_LAST, preferred_element_type=jnp.float32
         )
     hidden_ref[...] = (gate / (1.0 + jnp.exp(-gate)) * upward).astype(jnp.bfloat16)
+
+
+def up_kernel(core_ref, own_ref, *refs):
+    *piece_refs, weight_ref, hidden_ref, rows_ref = refs
+    project(core_ref, own_ref, piece_refs, weight_ref, hidden_ref, rows_ref, lambda index: None)
+
+
+def first_up_kernel(core_ref, columns_ref, own_ref, *refs):
+    *piece_refs, from_ref, hidden_ref, weight_ref, down_ref, rows_ref, sems = refs
+    parts = weight_ref.shape[0]
+    chips = down_ref.shape[0]
+    part = weight_ref.shape[3]
+    copies = [
+        pltpu.make_async_copy(
+            from_ref.at[0, 0:2, :, index * part : (index + 1) * part],
+            weight_ref.at[index],
+            sems.at[index],
+        )
+        for index in range(parts)
+    ]
+    for chip in range(chips):
+        at = pl.multiple_of(columns_ref[0, chip] * part, part)
+        copies.append(
+            pltpu.make_async_copy(
+                from_ref.at[0, 2, :, pl.ds(at, part)], down_ref.at[chip], sems.at[parts + chip]
+            )
+        )
+    ahead = 3
+    for copy in copies[:ahead]:
+        copy.start()
+
+    def before(index):
+        copies[index].wait()
+        if index + ahead < len(copies):
+            copies[index + ahead].start()
+
+    project(core_ref, own_ref, piece_refs, weight_ref, hidden_ref, rows_ref, before)
+    for index in range(parts, len(copies)):
+        before(index)
+
+
+def first_up(core, columns, own, own_pieces, other_pieces, weights):
+    chips = core.shape[0]
+    total = own.shape[0] + sum(piece.shape[0] for piece in own_pieces)
+    units, width = weights.shape[2:]
+    part = width // (2 * chips)
+    return pl.pallas_call(
+        first_up_kernel,
+        out_shape=[
+            jax.ShapeDtypeStruct((total, units), jnp.bfloat16),
+            pltpu.VMEM((2 * chips, 2, units, part), jnp.bfloat16),
+            pltpu.VMEM((chips, units, part), jnp.bfloat16),
+        ],
+        in_specs=[pl.BlockSpec(memory_space=pltpu.SMEM)] * 2
+        + in_vmem(2 * len(own_pieces) + 1)
+        + [in_hbm()],
+        out_specs=in_vmem(3),
+        scratch_shapes=[
+            pltpu.VMEM((total, part), jnp.bfloat16),
+            pltpu.SemaphoreType.DMA((3 * chips,)),
+        ],
+        compiler_params=params(),
+        cost_estimate=cost(total, width, 2 * units),
+    )(core, columns, own, *own_pieces, *other_pieces, weights)
 
 
 def up(core, own, own_pieces, other_pieces, weights):
@@ -330,27 +350,40 @@
     for_other = take(core, weights, (0, 2), 1, True)
     for_other, others = lax.optimization_barrier((for_other, others))
     other_down = along_cores(for_other)
-    last_own, last = arrived[spans - 1]
-    weights, last[0] = lax.optimization_barrier((weights, last[0]))
-    up_weights, down_weights = load(
-        columns, pltpu.with_memory_space_constraint(weights, pltpu.HBM)
-    )
-
     swapped = {}
     for span in range(1, spans):
         own_rows, pieces = arrived[span]
         both = (pieces, [along_cores(piece) for piece in pieces])
-        both, others, other_down = lax.optimization_barrier((both, others, other_down))
+        same = core
+        both, others, other_down, same, weights = lax.optimization_barrier(
+            (both, others, other_down, same, weights)
+        )
         arrived[span], swapped[span] = (own_rows, both[0]), both[1]
+        same = along_chips(same, 1)
     arrived[0] = (own, exchange(others, False))
+
+    kept_weights = []
 
     def finish(span, after):
         own, pieces = arrived[span]
         if after is not None:
             own, pieces, after = lax.optimization_barrier((own, pieces, after))
         others = swapped.get(span) or [along_cores(piece) for piece in pieces]
-        hidden = up(core, own, pieces, others, up_weights)
-        sums = down(columns, hidden, along_cores(hidden), down_weights, other_down)
+        if after is None:
+            hidden, *loaded = first_up(
+                core,
+                columns,
+                own,
+                pieces,
+                others,
+                pltpu.with_memory_space_constraint(weights, pltpu.HBM),
+            )
+            kept_weights.extend(loaded)
+            hidden, core_there = lax.optimization_barrier((hidden, same))
+        else:
+            hidden = up(after[1], own, pieces, others, kept_weights[0])
+            core_there = core
+        sums = down(columns, hidden, along_cores(hidden), kept_weights[1], other_down)
         came = [along_chips(sums[shift], shift) for shift in range(1, chips)]
         totals = []
         count = own.shape[0]
@@ -360,7 +393,7 @@
             for value in came:
                 total = total + value[at].astype(jnp.float32)
             totals.append(total.astype(jnp.bfloat16))
-        return [totals[0]] + exchange(totals[1:], True), sums
+        return [totals[0]] + exchange(totals[1:], True), (sums, core_there)
 
     returned = {}
     hidden = None

time: 86 us -> 81.7 us (0.950)
  starting transfers between devices: 31.9 us -> 29.7 us
  local copies, waits for them, and re-layouts: 8.39 us -> 6.57 us
    ppermute x12, waiting for transfers between devices: 16.7 us -> 7.91 us  [along_ep(): return lax.ppermute(value, 'ep', [(i, (i + shift) % ep) for i in range(ep)])]
    ppermute x2 -> x3, waiting for transfers between devices: 1.63 us -> 8.64 us  [along_chips(): return lax.ppermute(value, 'tp', pairs)]
    pallas_call x2 -> x1, Pallas kernels: 6 us -> 2.59 us  [up(): pl.pallas_call(up_kernel, out_shape=jax.ShapeDtypeStruct((total, units),...]
    ppermute x9, waiting for transfers between devices: 2.5 us -> 4.52 us  [along_cores(): return lax.ppermute(value, 'tp', [(i, i ^ 1) for i in range(tp)])]
    pallas_call x1, Pallas kernels: 3.87 us -> 5.71 us  [first_up(): pl.pallas_call(first_up_kernel, out_shape=[jax.ShapeDtypeStruct((total, u...]
    unnamed x27 -> x21, local copies, waits for them, and re-layouts: 4.16 us -> 2.33 us
    ppermute x12, starting transfers between devices: 26.8 us -> 25 us  [along_ep(): return lax.ppermute(value, 'ep', [(i, (i + shift) % ep) for i in range(ep)])]
    pallas_call x2, Pallas kernels: 3.47 us -> 4.62 us  [take(): pl.pallas_call(functools.partial(take_kernel, lead, side), out_shape=jax....]
  transfers between devices with their start and end apart: 23 -> 24, of which waited for: 9 -> 13; matrix products, arithmetic and copies ran while one was open for 13% -> 12% of each run, Pallas kernels for 15% -> 19%
where the time goes in v3:
time: 81.7 us; the launch traced here: 81.4 us
  starting transfers between devices  29.7 us (36%)
  waiting for transfers between devices  21.1 us (26%)
  Pallas kernels  17.4 us (21%)
  local copies, waits for them, and re-layouts  6.57 us (8%)
  other arithmetic  6.29 us (8%)
    ppermute x12, starting transfers between devices, along_ep(): return lax.ppermute(value, 'ep', [(i, (i + shift) % ep) for i in range(ep)])  25 us
    ppermute x3, waiting for transfers between devices, along_chips(): return lax.ppermute(value, 'tp', pairs)  8.64 us
    ppermute x12, waiting for transfers between devices, along_ep(): return lax.ppermute(value, 'ep', [(i, (i + shift) % ep) for i in range(ep)])  7.91 us
    pallas_call x1, Pallas kernels, first_up(): pl.pallas_call(first_up_kernel, out_shape=[jax.ShapeDtypeStruct((total, u...  5.71 us
    pallas_call x2, Pallas kernels, take(): pl.pallas_call(functools.partial(take_kernel, lead, side), out_shape=jax....  4.62 us
    ppermute x9, waiting for transfers between devices, along_cores(): return lax.ppermute(value, 'tp', [(i, i ^ 1) for i in range(tp)])  4.52 us
    pallas_call x2, Pallas kernels, down(): pl.pallas_call(down_kernel, out_shape=[jax.ShapeDtypeStruct((rows, part),...  3.21 us
    ppermute x3, starting transfers between devices, along_chips(): return lax.ppermute(value, 'tp', pairs)  2.76 us
  transfers between devices with their start and end apart: 24, of which 13 were waited for; matrix products, arithmetic and copies ran while one was open for 12% of the time, Pallas kernels for 19%

profile of v3, /device:TPU:0, one launch (start us, length us, event | category | flops | bytes accessed | tf_op | source)
XLA Modules:
  0.0 81.4 jit_solution(496634713051885380)
XLA Ops:
  0.0 1.5 %shard_map.74 = bf16[64,2048]{1,0:T(8,128)(2,1)S(1)} custom-call(s32[2]{0:T(128)S(1)} %add.127.core_ref, bf16[2,64,4096]{2,1,0:T(8,128)(2,1)} %from_ref.2), custom_call_target="tpu_custom_call" | custom-call | flops 128 | bytes 128 | tf_op jit(solution)/shard_map/pallas_call | solution.py:86
  1.6 3.1 %collective-permute-start = (bf16[64,2048]{1,0:T(8,128)(2,1)S(1)}, bf16[64,2048]{1,0:T(8,128)(2,1)S(1)}, u32[]{:S(2)}, u32[]{:S(2)}) collective-permute-start(bf16[64,2048]{1,0:T(8,128)(2,1)S(1)} %shard_map.74), channel_id=1, source_target_pairs={{0,4},{4,8},{8,12},{12,0},{1,5},{5,9},{9,13},{13,1},{2,6},{6,10},{... | collective-permute-start | bytes 786440 | tf_op jit(solution)/shard_map/ppermute | solution.py:316
  4.7 2.6 %collective-permute-start.1 = (bf16[64,2048]{1,0:T(8,128)(2,1)S(1)}, bf16[64,2048]{1,0:T(8,128)(2,1)S(1)}, u32[]{:S(2)}, u32[]{:S(2)}) collective-permute-start(bf16[64,2048]{1,0:T(8,128)(2,1)S(1)} %shard_map.74), channel_id=1, source_target_pairs={{0,8},{4,12},{8,0},{12,4},{1,9},{5,13},{9,1},{13,5},{2,10},{6,14},... | collective-permute-start | bytes 786440 | tf_op jit(solution)/shard_map/ppermute | solution.py:316
  7.3 1.3 %collective-permute-start.2 = (bf16[64,2048]{1,0:T(8,128)(2,1)S(1)}, bf16[64,2048]{1,0:T(8,128)(2,1)S(1)}, u32[]{:S(2)}, u32[]{:S(2)}) collective-permute-start(bf16[64,2048]{1,0:T(8,128)(2,1)S(1)} %shard_map.74), channel_id=1, source_target_pairs={{0,12},{4,0},{8,4},{12,8},{1,13},{5,1},{9,5},{13,9},{2,14},{6,2},{... | collective-permute-start | bytes 786440 | tf_op jit(solution)/shard_map/ppermute | solution.py:316
  8.9 0.1 eq.135
  9.1 0.1 reshape.163
  9.4 0.2 convert_reduce_fusion.1
  9.6 0.1 and_select_fusion.3
  9.8 0.2 convert_reduce_fusion
  10.0 0.1 sub.25
  10.2 0.1 squeeze.20
  10.5 0.2 squeeze.19
  11.0 3.1 %shard_map.75 = bf16[2,384,1024]{2,1,0:T(8,128)(2,1)} custom-call(s32[2]{0:T(128)S(1)} %add.127.core_ref, bf16[1,3,384,4096]{3,2,1,0:T(8,128)(2,1)} %refs_6_), custom_call_target="tpu_custom_call" | custom-call | flops 768 | bytes 768 | tf_op jit(solution)/shard_map/pallas_call | solution.py:86
  14.1 1.0 %shard_map.73 = (bf16[40,4096]{1,0:T(8,128)(2,1)S(1)}, bf16[40,2048]{1,0:T(8,128)(2,1)S(1)}, bf16[40,2048]{1,0:T(8,128)(2,1)S(1)}, bf16[40,2048]{1,0:T(8,128)(2,1)S(1)}) custom-call(s32[2]{0:T(128)S(1)} %add.127.core_ref, bf16[160,64]{1,0:T(8,128)(2,1)S(1)} %bitcast.19, bf16[64,4096]{1,0:T(8,128)(2,1)S(1)} %get-tuple-element.84.rows_ref), custom_call_target="tpu_custom_call" | custom-call | flops 320 | bytes 320 | tf_op jit(solution)/shard_map/pallas_call | solution.py:124
  15.1 0.7 copy-done
  15.8 0.7 copy-done.1
  16.5 0.7 copy-done.2
  17.1 0.6 slice_bitcast_fusion.3
  17.7 0.8 lt.91
  18.6 0.9 %select_reduce_fusion.4 = s32[4]{0:T(128)S(1)} fusion(s32[4]{0:T(128)} %get-tuple-element.93, s32[4]{0:T(128)} %get-tuple-element.92), kind=kLoop, calls=%fused_computation.34 | loop fusion | flops 44 | bytes 48 | tf_op jit(solution)/shard_map/reduce_min | solution.py:411
  19.5 0.5 and_select_fusion
  20.0 0.7 broadcast_select_fusion
  20.7 0.6 fusion.13
  21.3 0.6 and_select_fusion.1
  21.9 0.1 eq.152
  22.1 0.8 %copy.46 = f32[1,64,2]{1,2,0:T(2,128)S(1)} copy(f32[1,64,2]{2,1,0:T(8,128)} %get-tuple-element.91) | data formatting | bytes 1024 | tf_op jit(solution)/shard_map/slice | solution.py:417
  23.0 0.7 select_reduce_fusion.1
  23.7 0.6 collective-permute-start.3
  24.4 0.5 collective-permute-start.5
  24.9 0.7 pad_add_fusion.columns_ref
  25.6 0.4 collective-permute-done.4.refs_4_
  26.0 0.2 collective-permute-done.5.refs_5_
  26.3 1.5 %collective-permute-start.10 = (s32[2]{0:T(128)S(1)}, s32[2]{0:T(128)S(1)}, u32[]{:S(2)}, u32[]{:S(2)}) collective-permute-start(s32[2]{0:T(128)S(1)} %add.127.core_ref), channel_id=1, source_target_pairs={{0,2},{1,3},{2,0},{3,1},{4,6},{5,7},{6,4},{7,5},{8,10},{9,11},{10,... | collective-permute-start | bytes 32 | tf_op jit(solution)/shard_map/ppermute | solution.py:322
  27.8 5.7 %collective-permute-start.7 = (bf16[40,2048]{1,0:T(8,128)(2,1)}, bf16[40,2048]{1,0:T(8,128)(2,1)S(1)}, u32[]{:S(2)}, u32[]{:S(2)}) collective-permute-start(bf16[40,2048]{1,0:T(8,128)(2,1)} %copy-done.2), channel_id=1, source_target_pairs={{0,4},{4,8},{8,12},{12,0},{1,5},{5,9},{9,13},{13,1},{2,6},{6,10},{... | collective-permute-start | bytes 491528 | tf_op jit(solution)/shard_map/ppermute | solution.py:316
  33.5 2.0 %collective-permute-start.8 = (bf16[40,2048]{1,0:T(8,128)(2,1)}, bf16[40,2048]{1,0:T(8,128)(2,1)S(1)}, u32[]{:S(2)}, u32[]{:S(2)}) collective-permute-start(bf16[40,2048]{1,0:T(8,128)(2,1)} %copy-done.1), channel_id=1, source_target_pairs={{0,8},{4,12},{8,0},{12,4},{1,9},{5,13},{9,1},{13,5},{2,10},{6,14},... | collective-permute-start | bytes 491528 | tf_op jit(solution)/shard_map/ppermute | solution.py:316
  35.5 0.3 collective-permute-start.9
  35.9 5.7 %shard_map.76 = (bf16[256,384]{1,0:T(8,128)(2,1)S(1)}, bf16[4,2,384,1024]{3,2,1,0:T(8,128)(2,1)S(1)}, bf16[2,384,1024]{2,1,0:T(8,128)(2,1)S(1)}) custom-call(s32[2]{0:T(128)S(1)} %add.127.core_ref, s32[2,2]{1,0:T(2,128)S(1)} %pad_add_fusion.columns_ref, bf16[64,4096]{1,0:T(8,128)(2,1)S(1)} %get-tuple-element.85.own_ref, ...), custom_call_target="tpu_custom_call" | custom-call | flops 512 | bytes 512 | tf_op jit(solution)/shard_map/pallas_call | solution.py:214
  41.7 1.4 %collective-permute-done.11.other_hidden_ref = bf16[256,384]{1,0:T(8,128)(2,1)S(1)} collective-permute-done((bf16[256,384]{1,0:T(8,128)(2,1)S(1)}, bf16[256,384]{1,0:T(8,128)(2,1)S(1)}, u32[]{:S(2)}, u32[]{:S(2)}) %collective-permute-start.11) | collective-permute-done | bytes 196640 | tf_op jit(solution)/shard_map/ppermute | solution.py:325
  43.1 1.8 %shard_map.77 = (bf16[256,1024]{1,0:T(8,128)(2,1)S(1)}, bf16[256,1024]{1,0:T(8,128)(2,1)S(1)}) custom-call(s32[2,2]{1,0:T(2,128)S(1)} %pad_add_fusion.columns_ref, bf16[256,384]{1,0:T(8,128)(2,1)S(1)} %get-tuple-element.59.hidden_ref, bf16[256,384]{1,0:T(8,128)(2,1)S(1)} %collective-permute-done.11.other_hidden_ref, ...), custom_call_target="tpu_custom_call" | custom-call | flops 512 | bytes 512 | tf_op jit(solution)/shard_map/pallas_call | solution.py:261
  44.9 0.6 collective-permute-start.20
  45.5 1.0 %collective-permute-done.8.refs_1_ = bf16[40,2048]{1,0:T(8,128)(2,1)S(1)} collective-permute-done((bf16[40,2048]{1,0:T(8,128)(2,1)}, bf16[40,2048]{1,0:T(8,128)(2,1)S(1)}, u32[]{:S(2)}, u32[]{:S(2)}) %collective-permute-start.8) | collective-permute-done | bytes 163872 | tf_op jit(solution)/shard_map/ppermute | solution.py:316
  46.5 0.5 collective-permute-start.13
  47.0 0.9 %collective-permute-done.12.refs_3_ = bf16[40,2048]{1,0:T(8,128)(2,1)S(1)} collective-permute-done((bf16[40,2048]{1,0:T(8,128)(2,1)S(1)}, bf16[40,2048]{1,0:T(8,128)(2,1)S(1)}, u32[]{:S(2)}, u32[]{:S(2)}) %collective-permute-start.12) | collective-permute-done | bytes 163872 | tf_op jit(solution)/shard_map/ppermute | solution.py:325
  47.9 0.2 collective-permute-done.13.refs_4_
  48.1 0.3 collective-permute-done.14.refs_5_
  48.4 2.6 %shard_map.78.hidden_ref = bf16[160,384]{1,0:T(8,128)(2,1)S(1)} custom-call(s32[2]{0:T(128)S(1)} %collective-permute-done.10.core_ref, bf16[40,4096]{1,0:T(8,128)(2,1)S(1)} %get-tuple-element.66.own_ref, bf16[40,2048]{1,0:T(8,128)(2,1)S(1)} %collective-permute-done.7.refs_0_, bf16[40,2048]{1,0:T(8,128)(2,1)S(1)} %collective-permute-done.8.refs_1_, ...), custom_call_target="tpu_custom_call" | custom-call | flops 320 | bytes 320 | tf_op jit(solution)/shard_map/pallas_call | solution.py:237
  51.0 0.3 collective-permute-start.15
  51.3 1.1 %collective-permute-done.15.other_hidden_ref = bf16[160,384]{1,0:T(8,128)(2,1)S(1)} collective-permute-done((bf16[160,384]{1,0:T(8,128)(2,1)S(1)}, bf16[160,384]{1,0:T(8,128)(2,1)S(1)}, u32[]{:S(2)}, u32[]{:S(2)}) %collective-permute-start.15) | collective-permute-done | bytes 122912 | tf_op jit(solution)/shard_map/ppermute | solution.py:325
  52.4 1.4 %shard_map.79 = (bf16[160,1024]{1,0:T(8,128)(2,1)S(1)}, bf16[160,1024]{1,0:T(8,128)(2,1)S(1)}) custom-call(s32[2,2]{1,0:T(2,128)S(1)} %pad_add_fusion.columns_ref, bf16[160,384]{1,0:T(8,128)(2,1)S(1)} %shard_map.78.hidden_ref, bf16[160,384]{1,0:T(8,128)(2,1)S(1)} %collective-permute-done.15.other_hidden_ref, ...), custom_call_target="tpu_custom_call" | custom-call | flops 320 | bytes 320 | tf_op jit(solution)/shard_map/pallas_call | solution.py:261
  53.8 0.7 collective-permute-start.16
  54.6 5.2 %collective-permute-done.20 = bf16[256,1024]{1,0:T(8,128)(2,1)S(1)} collective-permute-done((bf16[256,1024]{1,0:T(8,128)(2,1)S(1)}, bf16[256,1024]{1,0:T(8,128)(2,1)S(1)}, u32[]{:S(2)}, u32[]{:S(2)}) %collective-permute-start.20) | collective-permute-done | bytes 524320 | tf_op jit(solution)/shard_map/ppermute | solution.py:322
  59.7 0.1 add_convert_fusion.3
  59.9 1.3 %collective-permute-start.21 = (bf16[64,1024]{1,0:T(8,128)(2,1)S(1)}, bf16[64,1024]{1,0:T(8,128)(2,1)S(1)}, u32[]{:S(2)}, u32[]{:S(2)}) collective-permute-start(bf16[64,1024]{1,0:T(8,128)(2,1)S(1)} %get-tuple-element.81), channel_id=1, source_target_pairs={{0,12},{4,0},{8,4},{12,8},{1,13},{5,1},{9,5},{13,9},{2,14},{6,2},{... | collective-permute-start | bytes 393224 | tf_op jit(solution)/shard_map/ppermute | solution.py:316
  61.1 1.1 %collective-permute-start.22 = (bf16[64,1024]{1,0:T(8,128)(2,1)S(1)}, bf16[64,1024]{1,0:T(8,128)(2,1)S(1)}, u32[]{:S(2)}, u32[]{:S(2)}) collective-permute-start(bf16[64,1024]{1,0:T(8,128)(2,1)S(1)} %get-tuple-element.83), channel_id=1, source_target_pairs={{0,8},{4,12},{8,0},{12,4},{1,9},{5,13},{9,1},{13,5},{2,10},{6,14},... | collective-permute-start | bytes 393224 | tf_op jit(solution)/shard_map/ppermute | solution.py:316
  62.3 0.2 collective-permute-start.23
  62.5 3.5 %collective-permute-done.16 = bf16[160,1024]{1,0:T(8,128)(2,1)S(1)} collective-permute-done((bf16[160,1024]{1,0:T(8,128)(2,1)S(1)}, bf16[160,1024]{1,0:T(8,128)(2,1)S(1)}, u32[]{:S(2)}, u32[]{:S(2)}) %collective-permute-start.16) | collective-permute-done | bytes 327712 | tf_op jit(solution)/shard_map/ppermute | solution.py:322
  66.1 2.1 %collective-permute-start.17 = (bf16[40,1024]{1,0:T(8,128)(2,1)S(1)}, bf16[40,1024]{1,0:T(8,128)(2,1)S(1)}, u32[]{:S(2)}, u32[]{:S(2)}) collective-permute-start(bf16[40,1024]{1,0:T(8,128)(2,1)S(1)} %get-tuple-element.88), channel_id=1, source_target_pairs={{0,12},{4,0},{8,4},{12,8},{1,13},{5,1},{9,5},{13,9},{2,14},{6,2},{... | collective-permute-start | bytes 245768 | tf_op jit(solution)/shard_map/ppermute | solution.py:316
  68.2 1.1 %collective-permute-start.18 = (bf16[40,1024]{1,0:T(8,128)(2,1)S(1)}, bf16[40,1024]{1,0:T(8,128)(2,1)S(1)}, u32[]{:S(2)}, u32[]{:S(2)}) collective-permute-start(bf16[40,1024]{1,0:T(8,128)(2,1)S(1)} %get-tuple-element.87), channel_id=1, source_target_pairs={{0,8},{4,12},{8,0},{12,4},{1,9},{5,13},{9,1},{13,5},{2,10},{6,14},... | collective-permute-start | bytes 245768 | tf_op jit(solution)/shard_map/ppermute | solution.py:316
  69.3 4.0 %collective-permute-start.19 = (bf16[40,1024]{1,0:T(8,128)(2,1)S(1)}, bf16[40,1024]{1,0:T(8,128)(2,1)S(1)}, u32[]{:S(2)}, u32[]{:S(2)}) collective-permute-start(bf16[40,1024]{1,0:T(8,128)(2,1)S(1)} %get-tuple-element.86), channel_id=1, source_target_pairs={{0,4},{4,8},{8,12},{12,0},{1,5},{5,9},{9,13},{13,1},{2,6},{6,10},{... | collective-permute-start | bytes 245768 | tf_op jit(solution)/shard_map/ppermute | solution.py:316
  73.3 4.8 %collective-permute-done.22 = bf16[64,1024]{1,0:T(8,128)(2,1)S(1)} collective-permute-done((bf16[64,1024]{1,0:T(8,128)(2,1)S(1)}, bf16[64,1024]{1,0:T(8,128)(2,1)S(1)}, u32[]{:S(2)}, u32[]{:S(2)}) %collective-permute-start.22) | collective-permute-done | bytes 131104 | tf_op jit(solution)/shard_map/ppermute | solution.py:316
  78.1 0.2 fusion.1
  78.4 2.0 %collective-permute-done.18.refs_2_ = bf16[40,1024]{1,0:T(8,128)(2,1)S(1)} collective-permute-done((bf16[40,1024]{1,0:T(8,128)(2,1)S(1)}, bf16[40,1024]{1,0:T(8,128)(2,1)S(1)}, u32[]{:S(2)}, u32[]{:S(2)}) %collective-permute-start.18) | collective-permute-done | bytes 81952 | tf_op jit(solution)/shard_map/ppermute | solution.py:316
  80.4 0.2 shard_map.80
  80.6 0.7 pad_maximum_fusion
  (60 shorter events, 1.7 us)
Async XLA Ops:
  0.0 8.6 %copy-start.3 = (bf16[2,64,4096]{2,1,0:T(8,128)(2,1)S(1)}, bf16[2,64,4096]{2,1,0:T(8,128)(2,1)}, u32[]{:S(2)}) copy-start(bf16[2,64,4096]{2,1,0:T(8,128)(2,1)} %from_ref.2) | copy-start | bytes 3145732
  0.0 8.7 %copy-start.5 = (s32[2,64,2]{1,2,0:T(2,128)S(1)}, s32[2,64,2]{1,2,0:T(2,128)}, u32[]{:S(2)}) copy-start(s32[2,64,2]{1,2,0:T(2,128)} %param.8) | copy-start | bytes 3076
  0.0 9.0 %copy-start.6 = (s32[2,64,2]{1,2,0:T(2,128)S(1)}, s32[2,64,2]{1,2,0:T(2,128)}, u32[]{:S(2)}) copy-start(s32[2,64,2]{1,2,0:T(2,128)} %param.10) | copy-start | bytes 3076
  0.0 9.3 %copy-start.4 = (s32[2,4]{1,0:T(2,128)S(1)}, s32[2,4]{1,0:T(2,128)}, u32[]{:S(2)}) copy-start(s32[2,4]{1,0:T(2,128)} %param.11) | copy-start | bytes 100
  0.0 9.7 %copy-start.8 = (s32[4]{0:T(128)S(1)}, s32[4]{0:T(128)}, u32[]{:S(2)}) copy-start(s32[4]{0:T(128)} %param.12) | copy-start | bytes 52
  1.6 22.2 %collective-permute-start = (bf16[64,2048]{1,0:T(8,128)(2,1)S(1)}, bf16[64,2048]{1,0:T(8,128)(2,1)S(1)}, u32[]{:S(2)}, u32[]{:S(2)}) collective-permute-start(bf16[64,2048]{1,0:T(8,128)(2,1)S(1)} %shard_map.74), channel_id=1, source_target_pairs={{0,4},{4,8},{8,12},{12,0},{1,5},{5,9},{9,13},{13,1},{2,6},{6,10},{... | collective-permute-start | bytes 786440 | tf_op jit(solution)/shard_map/ppermute | solution.py:316
  4.7 19.7 %collective-permute-start.1 = (bf16[64,2048]{1,0:T(8,128)(2,1)S(1)}, bf16[64,2048]{1,0:T(8,128)(2,1)S(1)}, u32[]{:S(2)}, u32[]{:S(2)}) collective-permute-start(bf16[64,2048]{1,0:T(8,128)(2,1)S(1)} %shard_map.74), channel_id=1, source_target_pairs={{0,8},{4,12},{8,0},{12,4},{1,9},{5,13},{9,1},{13,5},{2,10},{6,14},... | collective-permute-start | bytes 786440 | tf_op jit(solution)/shard_map/ppermute | solution.py:316
  7.3 17.1 %collective-permute-start.2 = (bf16[64,2048]{1,0:T(8,128)(2,1)S(1)}, bf16[64,2048]{1,0:T(8,128)(2,1)S(1)}, u32[]{:S(2)}, u32[]{:S(2)}) collective-permute-start(bf16[64,2048]{1,0:T(8,128)(2,1)S(1)} %shard_map.74), channel_id=1, source_target_pairs={{0,12},{4,0},{8,4},{12,8},{1,13},{5,1},{9,5},{13,9},{2,14},{6,2},{... | collective-permute-start | bytes 786440 | tf_op jit(solution)/shard_map/ppermute | solution.py:316
  11.0 7.5 %copy-start.7 = (f32[2,64,2]{1,2,0:T(2,128)S(1)}, f32[2,64,2]{1,2,0:T(2,128)}, u32[]{:S(2)}) copy-start(f32[2,64,2]{1,2,0:T(2,128)} %param.9) | copy-start | bytes 3076
  15.1 0.7 copy-start
  15.8 0.7 copy-start.1
  16.5 0.7 copy-start.2
  17.1 9.1 %collective-permute-start.6 = (bf16[2,384,1024]{2,1,0:T(8,128)(2,1)}, bf16[2,384,1024]{2,1,0:T(8,128)(2,1)S(1)}, u32[]{:S(2)}, u32[]{:S(2)}) collective-permute-start(bf16[2,384,1024]{2,1,0:T(8,128)(2,1)} %shard_map.75), channel_id=1, source_target_pairs={{0,1},{1,0},{2,3},{3,2},{4,5},{5,4},{6,7},{7,6},{8,9},{9,8},{10,11... | collective-permute-start | bytes 4718600 | tf_op jit(solution)/shard_map/ppermute | solution.py:325
  23.7 1.9 %collective-permute-start.3 = (bf16[64,2048]{1,0:T(8,128)(2,1)S(1)}, bf16[64,2048]{1,0:T(8,128)(2,1)}, u32[]{:S(2)}, u32[]{:S(2)}) collective-permute-start(bf16[64,2048]{1,0:T(8,128)(2,1)S(1)} %collective-permute-done.refs_0_), channel_id=1, source_target_pairs={{0,1},{1,0},{2,3},{3,2},{4,5},{5,4},{6,7},{7,6},{8,9},{9,8},{10,11... | collective-permute-start | bytes 786440 | tf_op jit(solution)/shard_map/ppermute | solution.py:325
  24.4 1.7 %collective-permute-start.4 = (bf16[64,2048]{1,0:T(8,128)(2,1)S(1)}, bf16[64,2048]{1,0:T(8,128)(2,1)}, u32[]{:S(2)}, u32[]{:S(2)}) collective-permute-start(bf16[64,2048]{1,0:T(8,128)(2,1)S(1)} %collective-permute-done.1.refs_1_), channel_id=1, source_target_pairs={{0,1},{1,0},{2,3},{3,2},{4,5},{5,4},{6,7},{7,6},{8,9},{9,8},{10,11... | collective-permute-start | bytes 786440 | tf_op jit(solution)/shard_map/ppermute | solution.py:325
  24.4 1.9 %collective-permute-start.5 = (bf16[64,2048]{1,0:T(8,128)(2,1)S(1)}, bf16[64,2048]{1,0:T(8,128)(2,1)S(1)}, u32[]{:S(2)}, u32[]{:S(2)}) collective-permute-start(bf16[64,2048]{1,0:T(8,128)(2,1)S(1)} %collective-permute-done.2.refs_2_), channel_id=1, source_target_pairs={{0,1},{1,0},{2,3},{3,2},{4,5},{5,4},{6,7},{7,6},{8,9},{9,8},{10,11... | collective-permute-start | bytes 786440 | tf_op jit(solution)/shard_map/ppermute | solution.py:325
  26.3 15.3 %collective-permute-start.10 = (s32[2]{0:T(128)S(1)}, s32[2]{0:T(128)S(1)}, u32[]{:S(2)}, u32[]{:S(2)}) collective-permute-start(s32[2]{0:T(128)S(1)} %add.127.core_ref), channel_id=1, source_target_pairs={{0,2},{1,3},{2,0},{3,1},{4,6},{5,7},{6,4},{7,5},{8,10},{9,11},{10,... | collective-permute-start | bytes 32 | tf_op jit(solution)/shard_map/ppermute | solution.py:322
  27.8 17.7 %collective-permute-start.7 = (bf16[40,2048]{1,0:T(8,128)(2,1)}, bf16[40,2048]{1,0:T(8,128)(2,1)S(1)}, u32[]{:S(2)}, u32[]{:S(2)}) collective-permute-start(bf16[40,2048]{1,0:T(8,128)(2,1)} %copy-done.2), channel_id=1, source_target_pairs={{0,4},{4,8},{8,12},{12,0},{1,5},{5,9},{9,13},{13,1},{2,6},{6,10},{... | collective-permute-start | bytes 491528 | tf_op jit(solution)/shard_map/ppermute | solution.py:316
  33.5 13.0 %collective-permute-start.8 = (bf16[40,2048]{1,0:T(8,128)(2,1)}, bf16[40,2048]{1,0:T(8,128)(2,1)S(1)}, u32[]{:S(2)}, u32[]{:S(2)}) collective-permute-start(bf16[40,2048]{1,0:T(8,128)(2,1)} %copy-done.1), channel_id=1, source_target_pairs={{0,8},{4,12},{8,0},{12,4},{1,9},{5,13},{9,1},{13,5},{2,10},{6,14},... | collective-permute-start | bytes 491528 | tf_op jit(solution)/shard_map/ppermute | solution.py:316
  35.5 11.0 %collective-permute-start.9 = (bf16[40,2048]{1,0:T(8,128)(2,1)}, bf16[40,2048]{1,0:T(8,128)(2,1)S(1)}, u32[]{:S(2)}, u32[]{:S(2)}) collective-permute-start(bf16[40,2048]{1,0:T(8,128)(2,1)} %copy-done), channel_id=1, source_target_pairs={{0,12},{4,0},{8,4},{12,8},{1,13},{5,1},{9,5},{13,9},{2,14},{6,2},{... | collective-permute-start | bytes 491528 | tf_op jit(solution)/shard_map/ppermute | solution.py:316
  41.6 1.5 %collective-permute-start.11 = (bf16[256,384]{1,0:T(8,128)(2,1)S(1)}, bf16[256,384]{1,0:T(8,128)(2,1)S(1)}, u32[]{:S(2)}, u32[]{:S(2)}) collective-permute-start(bf16[256,384]{1,0:T(8,128)(2,1)S(1)} %get-tuple-element.59.hidden_ref), channel_id=1, source_target_pairs={{0,1},{1,0},{2,3},{3,2},{4,5},{5,4},{6,7},{7,6},{8,9},{9,8},{10,11... | collective-permute-start | bytes 589832 | tf_op jit(solution)/shard_map/ppermute | solution.py:325
  44.9 14.8 %collective-permute-start.20 = (bf16[256,1024]{1,0:T(8,128)(2,1)S(1)}, bf16[256,1024]{1,0:T(8,128)(2,1)S(1)}, u32[]{:S(2)}, u32[]{:S(2)}) collective-permute-start(bf16[256,1024]{1,0:T(8,128)(2,1)S(1)} %get-tuple-element.63), channel_id=1, source_target_pairs={{0,2},{1,3},{2,0},{3,1},{4,6},{5,7},{6,4},{7,5},{8,10},{9,11},{10,... | collective-permute-start | bytes 1572872 | tf_op jit(solution)/shard_map/ppermute | solution.py:322
  46.5 1.4 %collective-permute-start.12 = (bf16[40,2048]{1,0:T(8,128)(2,1)S(1)}, bf16[40,2048]{1,0:T(8,128)(2,1)S(1)}, u32[]{:S(2)}, u32[]{:S(2)}) collective-permute-start(bf16[40,2048]{1,0:T(8,128)(2,1)S(1)} %collective-permute-done.7.refs_0_), channel_id=1, source_target_pairs={{0,1},{1,0},{2,3},{3,2},{4,5},{5,4},{6,7},{7,6},{8,9},{9,8},{10,11... | collective-permute-start | bytes 491528 | tf_op jit(solution)/shard_map/ppermute | solution.py:325
  46.5 1.6 %collective-permute-start.13 = (bf16[40,2048]{1,0:T(8,128)(2,1)S(1)}, bf16[40,2048]{1,0:T(8,128)(2,1)S(1)}, u32[]{:S(2)}, u32[]{:S(2)}) collective-permute-start(bf16[40,2048]{1,0:T(8,128)(2,1)S(1)} %collective-permute-done.8.refs_1_), channel_id=1, source_target_pairs={{0,1},{1,0},{2,3},{3,2},{4,5},{5,4},{6,7},{7,6},{8,9},{9,8},{10,11... | collective-permute-start | bytes 491528 | tf_op jit(solution)/shard_map/ppermute | solution.py:325
  47.0 1.4 %collective-permute-start.14 = (bf16[40,2048]{1,0:T(8,128)(2,1)S(1)}, bf16[40,2048]{1,0:T(8,128)(2,1)S(1)}, u32[]{:S(2)}, u32[]{:S(2)}) collective-permute-start(bf16[40,2048]{1,0:T(8,128)(2,1)S(1)} %collective-permute-done.9.refs_2_), channel_id=1, source_target_pairs={{0,1},{1,0},{2,3},{3,2},{4,5},{5,4},{6,7},{7,6},{8,9},{9,8},{10,11... | collective-permute-start | bytes 491528 | tf_op jit(solution)/shard_map/ppermute | solution.py:325
  51.0 1.4 %collective-permute-start.15 = (bf16[160,384]{1,0:T(8,128)(2,1)S(1)}, bf16[160,384]{1,0:T(8,128)(2,1)S(1)}, u32[]{:S(2)}, u32[]{:S(2)}) collective-permute-start(bf16[160,384]{1,0:T(8,128)(2,1)S(1)} %shard_map.78.hidden_ref), channel_id=1, source_target_pairs={{0,1},{1,0},{2,3},{3,2},{4,5},{5,4},{6,7},{7,6},{8,9},{9,8},{10,11... | collective-permute-start | bytes 368648 | tf_op jit(solution)/shard_map/ppermute | solution.py:325
  53.8 12.2 %collective-permute-start.16 = (bf16[160,1024]{1,0:T(8,128)(2,1)S(1)}, bf16[160,1024]{1,0:T(8,128)(2,1)S(1)}, u32[]{:S(2)}, u32[]{:S(2)}) collective-permute-start(bf16[160,1024]{1,0:T(8,128)(2,1)S(1)} %get-tuple-element.72), channel_id=1, source_target_pairs={{0,2},{1,3},{2,0},{3,1},{4,6},{5,7},{6,4},{7,5},{8,10},{9,11},{10,... | collective-permute-start | bytes 983048 | tf_op jit(solution)/shard_map/ppermute | solution.py:322
  59.9 9.4 %collective-permute-start.21 = (bf16[64,1024]{1,0:T(8,128)(2,1)S(1)}, bf16[64,1024]{1,0:T(8,128)(2,1)S(1)}, u32[]{:S(2)}, u32[]{:S(2)}) collective-permute-start(bf16[64,1024]{1,0:T(8,128)(2,1)S(1)} %get-tuple-element.81), channel_id=1, source_target_pairs={{0,12},{4,0},{8,4},{12,8},{1,13},{5,1},{9,5},{13,9},{2,14},{6,2},{... | collective-permute-start | bytes 393224 | tf_op jit(solution)/shard_map/ppermute | solution.py:316
  61.1 17.0 %collective-permute-start.22 = (bf16[64,1024]{1,0:T(8,128)(2,1)S(1)}, bf16[64,1024]{1,0:T(8,128)(2,1)S(1)}, u32[]{:S(2)}, u32[]{:S(2)}) collective-permute-start(bf16[64,1024]{1,0:T(8,128)(2,1)S(1)} %get-tuple-element.83), channel_id=1, source_target_pairs={{0,8},{4,12},{8,0},{12,4},{1,9},{5,13},{9,1},{13,5},{2,10},{6,14},... | collective-permute-start | bytes 393224 | tf_op jit(solution)/shard_map/ppermute | solution.py:316
  62.3 15.9 %collective-permute-start.23 = (bf16[64,1024]{1,0:T(8,128)(2,1)S(1)}, bf16[64,1024]{1,0:T(8,128)(2,1)S(1)}, u32[]{:S(2)}, u32[]{:S(2)}) collective-permute-start(bf16[64,1024]{1,0:T(8,128)(2,1)S(1)} %get-tuple-element.82), channel_id=1, source_target_pairs={{0,4},{4,8},{8,12},{12,0},{1,5},{5,9},{9,13},{13,1},{2,6},{6,10},{... | collective-permute-start | bytes 393224 | tf_op jit(solution)/shard_map/ppermute | solution.py:316
  66.1 12.3 %collective-permute-start.17 = (bf16[40,1024]{1,0:T(8,128)(2,1)S(1)}, bf16[40,1024]{1,0:T(8,128)(2,1)S(1)}, u32[]{:S(2)}, u32[]{:S(2)}) collective-permute-start(bf16[40,1024]{1,0:T(8,128)(2,1)S(1)} %get-tuple-element.88), channel_id=1, source_target_pairs={{0,12},{4,0},{8,4},{12,8},{1,13},{5,1},{9,5},{13,9},{2,14},{6,2},{... | collective-permute-start | bytes 245768 | tf_op jit(solution)/shard_map/ppermute | solution.py:316
  68.2 12.2 %collective-permute-start.18 = (bf16[40,1024]{1,0:T(8,128)(2,1)S(1)}, bf16[40,1024]{1,0:T(8,128)(2,1)S(1)}, u32[]{:S(2)}, u32[]{:S(2)}) collective-permute-start(bf16[40,1024]{1,0:T(8,128)(2,1)S(1)} %get-tuple-element.87), channel_id=1, source_target_pairs={{0,8},{4,12},{8,0},{12,4},{1,9},{5,13},{9,1},{13,5},{2,10},{6,14},... | collective-permute-start | bytes 245768 | tf_op jit(solution)/shard_map/ppermute | solution.py:316
  69.3 11.1 %collective-permute-start.19 = (bf16[40,1024]{1,0:T(8,128)(2,1)S(1)}, bf16[40,1024]{1,0:T(8,128)(2,1)S(1)}, u32[]{:S(2)}, u32[]{:S(2)}) collective-permute-start(bf16[40,1024]{1,0:T(8,128)(2,1)S(1)} %get-tuple-element.86), channel_id=1, source_target_pairs={{0,4},{4,8},{8,12},{12,0},{1,5},{5,9},{9,13},{13,1},{2,6},{6,10},{... | collective-permute-start | bytes 245768 | tf_op jit(solution)/shard_map/ppermute | solution.py:316

commit v4 on v3

--- a/solution.py
+++ b/solution.py
@@ -354,12 +354,12 @@
     for span in range(1, spans):
         own_rows, pieces = arrived[span]
         both = (pieces, [along_cores(piece) for piece in pieces])
-        same = core
+        same = 1 - core
         both, others, other_down, same, weights = lax.optimization_barrier(
             (both, others, other_down, same, weights)
         )
         arrived[span], swapped[span] = (own_rows, both[0]), both[1]
-        same = along_chips(same, 1)
+        same = along_cores(same)
     arrived[0] = (own, exchange(others, False))
 
     kept_weights = []

time: 81.7 us -> 80.4 us (0.984)
  waiting for transfers between devices: 21.1 us -> 19.4 us
    ppermute x3 -> x2, waiting for transfers between devices: 8.64 us -> 7.31 us  [along_chips(): return lax.ppermute(value, 'tp', pairs)]
    ppermute x3 -> x2, starting transfers between devices: 2.76 us -> 3.13 us  [along_chips(): return lax.ppermute(value, 'tp', pairs)]
    ppermute x9 -> x10, starting transfers between devices: 1.98 us -> 2.29 us  [along_cores(): return lax.ppermute(value, 'tp', [(i, i ^ 1) for i in range(tp)])]
    ppermute x9 -> x10, waiting for transfers between devices: 4.52 us -> 4.53 us  [along_cores(): return lax.ppermute(value, 'tp', [(i, i ^ 1) for i in range(tp)])]
  transfers between devices with their start and end apart: 24 -> 24, of which waited for: 13 -> 13; matrix products, arithmetic and copies ran while one was open for 12% -> 13% of each run, Pallas kernels for 19% -> 19%
where the time goes in v4:
time: 80.4 us; the launch traced here: 80.1 us
  starting transfers between devices  30.2 us (38%)
  waiting for transfers between devices  19.4 us (24%)
  Pallas kernels  17.4 us (22%)
  local copies, waits for them, and re-layouts  6.57 us (8%)
  other arithmetic  6.28 us (8%)
    ppermute x12, starting transfers between devices, along_ep(): return lax.ppermute(value, 'ep', [(i, (i + shift) % ep) for i in range(ep)])  24.7 us
    ppermute x12, waiting for transfers between devices, along_ep(): return lax.ppermute(value, 'ep', [(i, (i + shift) % ep) for i in range(ep)])  7.51 us
    ppermute x2, waiting for transfers between devices, along_chips(): return lax.ppermute(value, 'tp', pairs)  7.31 us
    pallas_call x1, Pallas kernels, first_up(): pl.pallas_call(first_up_kernel, out_shape=[jax.ShapeDtypeStruct((total, u...  5.71 us
    pallas_call x2, Pallas kernels, take(): pl.pallas_call(functools.partial(take_kernel, lead, side), out_shape=jax....  4.62 us
    ppermute x10, waiting for transfers between devices, along_cores(): return lax.ppermute(value, 'tp', [(i, i ^ 1) for i in range(tp)])  4.53 us
    pallas_call x2, Pallas kernels, down(): pl.pallas_call(down_kernel, out_shape=[jax.ShapeDtypeStruct((rows, part),...  3.2 us
    ppermute x2, starting transfers between devices, along_chips(): return lax.ppermute(value, 'tp', pairs)  3.13 us
  transfers between devices with their start and end apart: 24, of which 13 were waited for; matrix products, arithmetic and copies ran while one was open for 13% of the time, Pallas kernels for 19%

profile of v4, /device:TPU:0, one launch (start us, length us, event | category | flops | bytes accessed | tf_op | source)
XLA Modules:
  0.0 80.1 jit_solution(15200202104823520256)
XLA Ops:
  0.0 1.5 %shard_map.74 = bf16[64,2048]{1,0:T(8,128)(2,1)S(1)} custom-call(s32[2]{0:T(128)S(1)} %add.129.core_ref, bf16[2,64,4096]{2,1,0:T(8,128)(2,1)} %from_ref.2), custom_call_target="tpu_custom_call" | custom-call | flops 128 | bytes 128 | tf_op jit(solution)/shard_map/pallas_call | solution.py:86
  1.6 3.1 %collective-permute-start = (bf16[64,2048]{1,0:T(8,128)(2,1)S(1)}, bf16[64,2048]{1,0:T(8,128)(2,1)S(1)}, u32[]{:S(2)}, u32[]{:S(2)}) collective-permute-start(bf16[64,2048]{1,0:T(8,128)(2,1)S(1)} %shard_map.74), channel_id=1, source_target_pairs={{0,4},{4,8},{8,12},{12,0},{1,5},{5,9},{9,13},{13,1},{2,6},{6,10},{... | collective-permute-start | bytes 786440 | tf_op jit(solution)/shard_map/ppermute | solution.py:316
  4.7 2.6 %collective-permute-start.1 = (bf16[64,2048]{1,0:T(8,128)(2,1)S(1)}, bf16[64,2048]{1,0:T(8,128)(2,1)S(1)}, u32[]{:S(2)}, u32[]{:S(2)}) collective-permute-start(bf16[64,2048]{1,0:T(8,128)(2,1)S(1)} %shard_map.74), channel_id=1, source_target_pairs={{0,8},{4,12},{8,0},{12,4},{1,9},{5,13},{9,1},{13,5},{2,10},{6,14},... | collective-permute-start | bytes 786440 | tf_op jit(solution)/shard_map/ppermute | solution.py:316
  7.3 1.3 %collective-permute-start.2 = (bf16[64,2048]{1,0:T(8,128)(2,1)S(1)}, bf16[64,2048]{1,0:T(8,128)(2,1)S(1)}, u32[]{:S(2)}, u32[]{:S(2)}) collective-permute-start(bf16[64,2048]{1,0:T(8,128)(2,1)S(1)} %shard_map.74), channel_id=1, source_target_pairs={{0,12},{4,0},{8,4},{12,8},{1,13},{5,1},{9,5},{13,9},{2,14},{6,2},{... | collective-permute-start | bytes 786440 | tf_op jit(solution)/shard_map/ppermute | solution.py:316
  8.9 0.1 eq.135
  9.1 0.1 reshape.163
  9.4 0.2 convert_reduce_fusion.1
  9.6 0.1 and_select_fusion.3
  9.8 0.2 convert_reduce_fusion
  10.0 0.1 sub.29
  10.2 0.1 squeeze.20
  10.5 0.2 squeeze.19
  10.9 0.1 copy.44
  11.0 3.1 %shard_map.75 = bf16[2,384,1024]{2,1,0:T(8,128)(2,1)} custom-call(s32[2]{0:T(128)S(1)} %add.129.core_ref, bf16[1,3,384,4096]{3,2,1,0:T(8,128)(2,1)} %refs_6_), custom_call_target="tpu_custom_call" | custom-call | flops 768 | bytes 768 | tf_op jit(solution)/shard_map/pallas_call | solution.py:86
  14.1 1.0 %shard_map.73 = (bf16[40,4096]{1,0:T(8,128)(2,1)S(1)}, bf16[40,2048]{1,0:T(8,128)(2,1)S(1)}, bf16[40,2048]{1,0:T(8,128)(2,1)S(1)}, bf16[40,2048]{1,0:T(8,128)(2,1)S(1)}) custom-call(s32[2]{0:T(128)S(1)} %add.129.core_ref, bf16[160,64]{1,0:T(8,128)(2,1)S(1)} %bitcast.19, bf16[64,4096]{1,0:T(8,128)(2,1)S(1)} %get-tuple-element.84.rows_ref), custom_call_target="tpu_custom_call" | custom-call | flops 320 | bytes 320 | tf_op jit(solution)/shard_map/pallas_call | solution.py:124
  15.1 0.7 copy-done
  15.8 0.7 copy-done.1
  16.5 0.7 copy-done.2
  17.1 0.6 slice_bitcast_fusion.3
  17.7 0.8 lt.91
  18.6 0.9 %select_reduce_fusion.4 = s32[4]{0:T(128)S(1)} fusion(s32[4]{0:T(128)} %get-tuple-element.93, s32[4]{0:T(128)} %get-tuple-element.92), kind=kLoop, calls=%fused_computation.34 | loop fusion | flops 44 | bytes 48 | tf_op jit(solution)/shard_map/reduce_min | solution.py:411
  19.5 0.5 and_select_fusion
  20.0 0.7 broadcast_select_fusion
  20.7 0.6 fusion.13
  21.3 0.6 and_select_fusion.1
  21.9 0.1 eq.152
  22.1 0.8 %copy.46 = f32[1,64,2]{1,2,0:T(2,128)S(1)} copy(f32[1,64,2]{2,1,0:T(8,128)} %get-tuple-element.91) | data formatting | bytes 1024 | tf_op jit(solution)/shard_map/slice | solution.py:417
  23.0 0.7 select_reduce_fusion.1
  23.7 0.6 collective-permute-start.3
  24.4 0.5 collective-permute-start.5
  24.9 0.7 pad_add_fusion.columns_ref
  25.6 0.4 collective-permute-done.4.refs_4_
  26.0 0.2 collective-permute-done.5.refs_5_
  26.3 0.3 collective-permute-start.10
  26.6 5.5 %collective-permute-start.7 = (bf16[40,2048]{1,0:T(8,128)(2,1)}, bf16[40,2048]{1,0:T(8,128)(2,1)S(1)}, u32[]{:S(2)}, u32[]{:S(2)}) collective-permute-start(bf16[40,2048]{1,0:T(8,128)(2,1)} %copy-done.2), channel_id=1, source_target_pairs={{0,4},{4,8},{8,12},{12,0},{1,5},{5,9},{9,13},{13,1},{2,6},{6,10},{... | collective-permute-start | bytes 491528 | tf_op jit(solution)/shard_map/ppermute | solution.py:316
  32.1 2.1 %collective-permute-start.8 = (bf16[40,2048]{1,0:T(8,128)(2,1)}, bf16[40,2048]{1,0:T(8,128)(2,1)S(1)}, u32[]{:S(2)}, u32[]{:S(2)}) collective-permute-start(bf16[40,2048]{1,0:T(8,128)(2,1)} %copy-done.1), channel_id=1, source_target_pairs={{0,8},{4,12},{8,0},{12,4},{1,9},{5,13},{9,1},{13,5},{2,10},{6,14},... | collective-permute-start | bytes 491528 | tf_op jit(solution)/shard_map/ppermute | solution.py:316
  34.2 0.3 collective-permute-start.9
  34.5 5.7 %shard_map.76 = (bf16[256,384]{1,0:T(8,128)(2,1)S(1)}, bf16[4,2,384,1024]{3,2,1,0:T(8,128)(2,1)S(1)}, bf16[2,384,1024]{2,1,0:T(8,128)(2,1)S(1)}) custom-call(s32[2]{0:T(128)S(1)} %add.129.core_ref, s32[2,2]{1,0:T(2,128)S(1)} %pad_add_fusion.columns_ref, bf16[64,4096]{1,0:T(8,128)(2,1)S(1)} %get-tuple-element.85.own_ref, ...), custom_call_target="tpu_custom_call" | custom-call | flops 512 | bytes 512 | tf_op jit(solution)/shard_map/pallas_call | solution.py:214
  40.3 1.4 %collective-permute-done.11.other_hidden_ref = bf16[256,384]{1,0:T(8,128)(2,1)S(1)} collective-permute-done((bf16[256,384]{1,0:T(8,128)(2,1)S(1)}, bf16[256,384]{1,0:T(8,128)(2,1)S(1)}, u32[]{:S(2)}, u32[]{:S(2)}) %collective-permute-start.11) | collective-permute-done | bytes 196640 | tf_op jit(solution)/shard_map/ppermute | solution.py:325
  41.7 1.8 %shard_map.77 = (bf16[256,1024]{1,0:T(8,128)(2,1)S(1)}, bf16[256,1024]{1,0:T(8,128)(2,1)S(1)}) custom-call(s32[2,2]{1,0:T(2,128)S(1)} %pad_add_fusion.columns_ref, bf16[256,384]{1,0:T(8,128)(2,1)S(1)} %get-tuple-element.59.hidden_ref, bf16[256,384]{1,0:T(8,128)(2,1)S(1)} %collective-permute-done.11.other_hidden_ref, ...), custom_call_target="tpu_custom_call" | custom-call | flops 512 | bytes 512 | tf_op jit(solution)/shard_map/pallas_call | solution.py:261
  43.6 1.6 %collective-permute-start.20 = (bf16[256,1024]{1,0:T(8,128)(2,1)S(1)}, bf16[256,1024]{1,0:T(8,128)(2,1)S(1)}, u32[]{:S(2)}, u32[]{:S(2)}) collective-permute-start(bf16[256,1024]{1,0:T(8,128)(2,1)S(1)} %get-tuple-element.63), channel_id=1, source_target_pairs={{0,2},{1,3},{2,0},{3,1},{4,6},{5,7},{6,4},{7,5},{8,10},{9,11},{10,... | collective-permute-start | bytes 1572872 | tf_op jit(solution)/shard_map/ppermute | solution.py:322
  45.1 0.6 collective-permute-done.8.refs_1_
  45.7 0.5 collective-permute-start.13
  46.2 0.9 %collective-permute-done.12.refs_3_ = bf16[40,2048]{1,0:T(8,128)(2,1)S(1)} collective-permute-done((bf16[40,2048]{1,0:T(8,128)(2,1)S(1)}, bf16[40,2048]{1,0:T(8,128)(2,1)S(1)}, u32[]{:S(2)}, u32[]{:S(2)}) %collective-permute-start.12) | collective-permute-done | bytes 163872 | tf_op jit(solution)/shard_map/ppermute | solution.py:325
  47.1 0.2 collective-permute-done.13.refs_4_
  47.3 0.3 collective-permute-done.14.refs_5_
  47.6 2.6 %shard_map.78.hidden_ref = bf16[160,384]{1,0:T(8,128)(2,1)S(1)} custom-call(s32[2]{0:T(128)S(1)} %collective-permute-done.10.core_ref, bf16[40,4096]{1,0:T(8,128)(2,1)S(1)} %get-tuple-element.66.own_ref, bf16[40,2048]{1,0:T(8,128)(2,1)S(1)} %collective-permute-done.7.refs_0_, bf16[40,2048]{1,0:T(8,128)(2,1)S(1)} %collective-permute-done.8.refs_1_, ...), custom_call_target="tpu_custom_call" | custom-call | flops 320 | bytes 320 | tf_op jit(solution)/shard_map/pallas_call | solution.py:237
  50.2 0.3 collective-permute-start.15
  50.5 1.1 %collective-permute-done.15.other_hidden_ref = bf16[160,384]{1,0:T(8,128)(2,1)S(1)} collective-permute-done((bf16[160,384]{1,0:T(8,128)(2,1)S(1)}, bf16[160,384]{1,0:T(8,128)(2,1)S(1)}, u32[]{:S(2)}, u32[]{:S(2)}) %collective-permute-start.15) | collective-permute-done | bytes 122912 | tf_op jit(solution)/shard_map/ppermute | solution.py:325
  51.6 1.4 %shard_map.79 = (bf16[160,1024]{1,0:T(8,128)(2,1)S(1)}, bf16[160,1024]{1,0:T(8,128)(2,1)S(1)}) custom-call(s32[2,2]{1,0:T(2,128)S(1)} %pad_add_fusion.columns_ref, bf16[160,384]{1,0:T(8,128)(2,1)S(1)} %shard_map.78.hidden_ref, bf16[160,384]{1,0:T(8,128)(2,1)S(1)} %collective-permute-done.15.other_hidden_ref, ...), custom_call_target="tpu_custom_call" | custom-call | flops 320 | bytes 320 | tf_op jit(solution)/shard_map/pallas_call | solution.py:261
  53.0 1.6 %collective-permute-start.16 = (bf16[160,1024]{1,0:T(8,128)(2,1)S(1)}, bf16[160,1024]{1,0:T(8,128)(2,1)S(1)}, u32[]{:S(2)}, u32[]{:S(2)}) collective-permute-start(bf16[160,1024]{1,0:T(8,128)(2,1)S(1)} %get-tuple-element.72), channel_id=1, source_target_pairs={{0,2},{1,3},{2,0},{3,1},{4,6},{5,7},{6,4},{7,5},{8,10},{9,11},{10,... | collective-permute-start | bytes 983048 | tf_op jit(solution)/shard_map/ppermute | solution.py:322
  54.7 3.7 %collective-permute-done.20 = bf16[256,1024]{1,0:T(8,128)(2,1)S(1)} collective-permute-done((bf16[256,1024]{1,0:T(8,128)(2,1)S(1)}, bf16[256,1024]{1,0:T(8,128)(2,1)S(1)}, u32[]{:S(2)}, u32[]{:S(2)}) %collective-permute-start.20) | collective-permute-done | bytes 524320 | tf_op jit(solution)/shard_map/ppermute | solution.py:322
  58.4 0.1 add_convert_fusion.3
  58.5 1.3 %collective-permute-start.21 = (bf16[64,1024]{1,0:T(8,128)(2,1)S(1)}, bf16[64,1024]{1,0:T(8,128)(2,1)S(1)}, u32[]{:S(2)}, u32[]{:S(2)}) collective-permute-start(bf16[64,1024]{1,0:T(8,128)(2,1)S(1)} %get-tuple-element.81), channel_id=1, source_target_pairs={{0,12},{4,0},{8,4},{12,8},{1,13},{5,1},{9,5},{13,9},{2,14},{6,2},{... | collective-permute-start | bytes 393224 | tf_op jit(solution)/shard_map/ppermute | solution.py:316
  59.8 1.2 %collective-permute-start.22 = (bf16[64,1024]{1,0:T(8,128)(2,1)S(1)}, bf16[64,1024]{1,0:T(8,128)(2,1)S(1)}, u32[]{:S(2)}, u32[]{:S(2)}) collective-permute-start(bf16[64,1024]{1,0:T(8,128)(2,1)S(1)} %get-tuple-element.83), channel_id=1, source_target_pairs={{0,8},{4,12},{8,0},{12,4},{1,9},{5,13},{9,1},{13,5},{2,10},{6,14},... | collective-permute-start | bytes 393224 | tf_op jit(solution)/shard_map/ppermute | solution.py:316
  61.0 3.6 %collective-permute-done.16 = bf16[160,1024]{1,0:T(8,128)(2,1)S(1)} collective-permute-done((bf16[160,1024]{1,0:T(8,128)(2,1)S(1)}, bf16[160,1024]{1,0:T(8,128)(2,1)S(1)}, u32[]{:S(2)}, u32[]{:S(2)}) %collective-permute-start.16) | collective-permute-done | bytes 327712 | tf_op jit(solution)/shard_map/ppermute | solution.py:322
  64.7 2.6 %collective-permute-start.17 = (bf16[40,1024]{1,0:T(8,128)(2,1)S(1)}, bf16[40,1024]{1,0:T(8,128)(2,1)S(1)}, u32[]{:S(2)}, u32[]{:S(2)}) collective-permute-start(bf16[40,1024]{1,0:T(8,128)(2,1)S(1)} %get-tuple-element.88), channel_id=1, source_target_pairs={{0,12},{4,0},{8,4},{12,8},{1,13},{5,1},{9,5},{13,9},{2,14},{6,2},{... | collective-permute-start | bytes 245768 | tf_op jit(solution)/shard_map/ppermute | solution.py:316
  67.4 1.2 %collective-permute-start.18 = (bf16[40,1024]{1,0:T(8,128)(2,1)S(1)}, bf16[40,1024]{1,0:T(8,128)(2,1)S(1)}, u32[]{:S(2)}, u32[]{:S(2)}) collective-permute-start(bf16[40,1024]{1,0:T(8,128)(2,1)S(1)} %get-tuple-element.87), channel_id=1, source_target_pairs={{0,8},{4,12},{8,0},{12,4},{1,9},{5,13},{9,1},{13,5},{2,10},{6,14},... | collective-permute-start | bytes 245768 | tf_op jit(solution)/shard_map/ppermute | solution.py:316
  68.5 3.5 %collective-permute-start.19 = (bf16[40,1024]{1,0:T(8,128)(2,1)S(1)}, bf16[40,1024]{1,0:T(8,128)(2,1)S(1)}, u32[]{:S(2)}, u32[]{:S(2)}) collective-permute-start(bf16[40,1024]{1,0:T(8,128)(2,1)S(1)} %get-tuple-element.86), channel_id=1, source_target_pairs={{0,4},{4,8},{8,12},{12,0},{1,5},{5,9},{9,13},{13,1},{2,6},{6,10},{... | collective-permute-start | bytes 245768 | tf_op jit(solution)/shard_map/ppermute | solution.py:316
  72.1 4.9 %collective-permute-done.22 = bf16[64,1024]{1,0:T(8,128)(2,1)S(1)} collective-permute-done((bf16[64,1024]{1,0:T(8,128)(2,1)S(1)}, bf16[64,1024]{1,0:T(8,128)(2,1)S(1)}, u32[]{:S(2)}, u32[]{:S(2)}) %collective-permute-start.22) | collective-permute-done | bytes 131104 | tf_op jit(solution)/shard_map/ppermute | solution.py:316
  76.9 0.2 fusion.1
  77.2 2.0 %collective-permute-done.18.refs_2_ = bf16[40,1024]{1,0:T(8,128)(2,1)S(1)} collective-permute-done((bf16[40,1024]{1,0:T(8,128)(2,1)S(1)}, bf16[40,1024]{1,0:T(8,128)(2,1)S(1)}, u32[]{:S(2)}, u32[]{:S(2)}) %collective-permute-start.18) | collective-permute-done | bytes 81952 | tf_op jit(solution)/shard_map/ppermute | solution.py:316
  79.1 0.2 shard_map.80
  79.4 0.7 pad_maximum_fusion
  (61 shorter events, 1.6 us)
Async XLA Ops:
  0.0 8.6 %copy-start.3 = (bf16[2,64,4096]{2,1,0:T(8,128)(2,1)S(1)}, bf16[2,64,4096]{2,1,0:T(8,128)(2,1)}, u32[]{:S(2)}) copy-start(bf16[2,64,4096]{2,1,0:T(8,128)(2,1)} %from_ref.2) | copy-start | bytes 3145732
  0.0 8.7 %copy-start.5 = (s32[2,64,2]{1,2,0:T(2,128)S(1)}, s32[2,64,2]{1,2,0:T(2,128)}, u32[]{:S(2)}) copy-start(s32[2,64,2]{1,2,0:T(2,128)} %param.8) | copy-start | bytes 3076
  0.0 9.0 %copy-start.6 = (s32[2,64,2]{1,2,0:T(2,128)S(1)}, s32[2,64,2]{1,2,0:T(2,128)}, u32[]{:S(2)}) copy-start(s32[2,64,2]{1,2,0:T(2,128)} %param.10) | copy-start | bytes 3076
  0.0 9.3 %copy-start.4 = (s32[2,4]{1,0:T(2,128)S(1)}, s32[2,4]{1,0:T(2,128)}, u32[]{:S(2)}) copy-start(s32[2,4]{1,0:T(2,128)} %param.11) | copy-start | bytes 100
  0.0 9.7 %copy-start.8 = (s32[4]{0:T(128)S(1)}, s32[4]{0:T(128)}, u32[]{:S(2)}) copy-start(s32[4]{0:T(128)} %param.12) | copy-start | bytes 52
  1.6 22.2 %collective-permute-start = (bf16[64,2048]{1,0:T(8,128)(2,1)S(1)}, bf16[64,2048]{1,0:T(8,128)(2,1)S(1)}, u32[]{:S(2)}, u32[]{:S(2)}) collective-permute-start(bf16[64,2048]{1,0:T(8,128)(2,1)S(1)} %shard_map.74), channel_id=1, source_target_pairs={{0,4},{4,8},{8,12},{12,0},{1,5},{5,9},{9,13},{13,1},{2,6},{6,10},{... | collective-permute-start | bytes 786440 | tf_op jit(solution)/shard_map/ppermute | solution.py:316
  4.7 19.7 %collective-permute-start.1 = (bf16[64,2048]{1,0:T(8,128)(2,1)S(1)}, bf16[64,2048]{1,0:T(8,128)(2,1)S(1)}, u32[]{:S(2)}, u32[]{:S(2)}) collective-permute-start(bf16[64,2048]{1,0:T(8,128)(2,1)S(1)} %shard_map.74), channel_id=1, source_target_pairs={{0,8},{4,12},{8,0},{12,4},{1,9},{5,13},{9,1},{13,5},{2,10},{6,14},... | collective-permute-start | bytes 786440 | tf_op jit(solution)/shard_map/ppermute | solution.py:316
  7.3 17.1 %collective-permute-start.2 = (bf16[64,2048]{1,0:T(8,128)(2,1)S(1)}, bf16[64,2048]{1,0:T(8,128)(2,1)S(1)}, u32[]{:S(2)}, u32[]{:S(2)}) collective-permute-start(bf16[64,2048]{1,0:T(8,128)(2,1)S(1)} %shard_map.74), channel_id=1, source_target_pairs={{0,12},{4,0},{8,4},{12,8},{1,13},{5,1},{9,5},{13,9},{2,14},{6,2},{... | collective-permute-start | bytes 786440 | tf_op jit(solution)/shard_map/ppermute | solution.py:316
  11.0 7.5 %copy-start.7 = (f32[2,64,2]{1,2,0:T(2,128)S(1)}, f32[2,64,2]{1,2,0:T(2,128)}, u32[]{:S(2)}) copy-start(f32[2,64,2]{1,2,0:T(2,128)} %param.9) | copy-start | bytes 3076
  15.1 0.7 copy-start
  15.8 0.7 copy-start.1
  16.5 0.7 copy-start.2
  17.1 9.1 %collective-permute-start.6 = (bf16[2,384,1024]{2,1,0:T(8,128)(2,1)}, bf16[2,384,1024]{2,1,0:T(8,128)(2,1)S(1)}, u32[]{:S(2)}, u32[]{:S(2)}) collective-permute-start(bf16[2,384,1024]{2,1,0:T(8,128)(2,1)} %shard_map.75), channel_id=1, source_target_pairs={{0,1},{1,0},{2,3},{3,2},{4,5},{5,4},{6,7},{7,6},{8,9},{9,8},{10,11... | collective-permute-start | bytes 4718600 | tf_op jit(solution)/shard_map/ppermute | solution.py:325
  23.7 1.9 %collective-permute-start.3 = (bf16[64,2048]{1,0:T(8,128)(2,1)S(1)}, bf16[64,2048]{1,0:T(8,128)(2,1)}, u32[]{:S(2)}, u32[]{:S(2)}) collective-permute-start(bf16[64,2048]{1,0:T(8,128)(2,1)S(1)} %collective-permute-done.refs_0_), channel_id=1, source_target_pairs={{0,1},{1,0},{2,3},{3,2},{4,5},{5,4},{6,7},{7,6},{8,9},{9,8},{10,11... | collective-permute-start | bytes 786440 | tf_op jit(solution)/shard_map/ppermute | solution.py:325
  24.4 1.7 %collective-permute-start.4 = (bf16[64,2048]{1,0:T(8,128)(2,1)S(1)}, bf16[64,2048]{1,0:T(8,128)(2,1)}, u32[]{:S(2)}, u32[]{:S(2)}) collective-permute-start(bf16[64,2048]{1,0:T(8,128)(2,1)S(1)} %collective-permute-done.1.refs_1_), channel_id=1, source_target_pairs={{0,1},{1,0},{2,3},{3,2},{4,5},{5,4},{6,7},{7,6},{8,9},{9,8},{10,11... | collective-permute-start | bytes 786440 | tf_op jit(solution)/shard_map/ppermute | solution.py:325
  24.4 1.9 %collective-permute-start.5 = (bf16[64,2048]{1,0:T(8,128)(2,1)S(1)}, bf16[64,2048]{1,0:T(8,128)(2,1)S(1)}, u32[]{:S(2)}, u32[]{:S(2)}) collective-permute-start(bf16[64,2048]{1,0:T(8,128)(2,1)S(1)} %collective-permute-done.2.refs_2_), channel_id=1, source_target_pairs={{0,1},{1,0},{2,3},{3,2},{4,5},{5,4},{6,7},{7,6},{8,9},{9,8},{10,11... | collective-permute-start | bytes 786440 | tf_op jit(solution)/shard_map/ppermute | solution.py:325
  26.3 14.0 %collective-permute-start.10 = (s32[2]{0:T(128)S(1)}, s32[2]{0:T(128)S(1)}, u32[]{:S(2)}, u32[]{:S(2)}) collective-permute-start(s32[2]{0:T(128)S(1)} %add.130), channel_id=1, source_target_pairs={{0,1},{1,0},{2,3},{3,2},{4,5},{5,4},{6,7},{7,6},{8,9},{9,8},{10,11... | collective-permute-start | bytes 32 | tf_op jit(solution)/shard_map/ppermute | solution.py:325
  26.6 18.5 %collective-permute-start.7 = (bf16[40,2048]{1,0:T(8,128)(2,1)}, bf16[40,2048]{1,0:T(8,128)(2,1)S(1)}, u32[]{:S(2)}, u32[]{:S(2)}) collective-permute-start(bf16[40,2048]{1,0:T(8,128)(2,1)} %copy-done.2), channel_id=1, source_target_pairs={{0,4},{4,8},{8,12},{12,0},{1,5},{5,9},{9,13},{13,1},{2,6},{6,10},{... | collective-permute-start | bytes 491528 | tf_op jit(solution)/shard_map/ppermute | solution.py:316
  32.1 13.6 %collective-permute-start.8 = (bf16[40,2048]{1,0:T(8,128)(2,1)}, bf16[40,2048]{1,0:T(8,128)(2,1)S(1)}, u32[]{:S(2)}, u32[]{:S(2)}) collective-permute-start(bf16[40,2048]{1,0:T(8,128)(2,1)} %copy-done.1), channel_id=1, source_target_pairs={{0,8},{4,12},{8,0},{12,4},{1,9},{5,13},{9,1},{13,5},{2,10},{6,14},... | collective-permute-start | bytes 491528 | tf_op jit(solution)/shard_map/ppermute | solution.py:316
  34.2 11.5 %collective-permute-start.9 = (bf16[40,2048]{1,0:T(8,128)(2,1)}, bf16[40,2048]{1,0:T(8,128)(2,1)S(1)}, u32[]{:S(2)}, u32[]{:S(2)}) collective-permute-start(bf16[40,2048]{1,0:T(8,128)(2,1)} %copy-done), channel_id=1, source_target_pairs={{0,12},{4,0},{8,4},{12,8},{1,13},{5,1},{9,5},{13,9},{2,14},{6,2},{... | collective-permute-start | bytes 491528 | tf_op jit(solution)/shard_map/ppermute | solution.py:316
  40.2 1.5 %collective-permute-start.11 = (bf16[256,384]{1,0:T(8,128)(2,1)S(1)}, bf16[256,384]{1,0:T(8,128)(2,1)S(1)}, u32[]{:S(2)}, u32[]{:S(2)}) collective-permute-start(bf16[256,384]{1,0:T(8,128)(2,1)S(1)} %get-tuple-element.59.hidden_ref), channel_id=1, source_target_pairs={{0,1},{1,0},{2,3},{3,2},{4,5},{5,4},{6,7},{7,6},{8,9},{9,8},{10,11... | collective-permute-start | bytes 589832 | tf_op jit(solution)/shard_map/ppermute | solution.py:325
  43.6 14.8 %collective-permute-start.20 = (bf16[256,1024]{1,0:T(8,128)(2,1)S(1)}, bf16[256,1024]{1,0:T(8,128)(2,1)S(1)}, u32[]{:S(2)}, u32[]{:S(2)}) collective-permute-start(bf16[256,1024]{1,0:T(8,128)(2,1)S(1)} %get-tuple-element.63), channel_id=1, source_target_pairs={{0,2},{1,3},{2,0},{3,1},{4,6},{5,7},{6,4},{7,5},{8,10},{9,11},{10,... | collective-permute-start | bytes 1572872 | tf_op jit(solution)/shard_map/ppermute | solution.py:322
  45.7 1.4 %collective-permute-start.12 = (bf16[40,2048]{1,0:T(8,128)(2,1)S(1)}, bf16[40,2048]{1,0:T(8,128)(2,1)S(1)}, u32[]{:S(2)}, u32[]{:S(2)}) collective-permute-start(bf16[40,2048]{1,0:T(8,128)(2,1)S(1)} %collective-permute-done.7.refs_0_), channel_id=1, source_target_pairs={{0,1},{1,0},{2,3},{3,2},{4,5},{5,4},{6,7},{7,6},{8,9},{9,8},{10,11... | collective-permute-start | bytes 491528 | tf_op jit(solution)/shard_map/ppermute | solution.py:325
  45.7 1.6 %collective-permute-start.13 = (bf16[40,2048]{1,0:T(8,128)(2,1)S(1)}, bf16[40,2048]{1,0:T(8,128)(2,1)S(1)}, u32[]{:S(2)}, u32[]{:S(2)}) collective-permute-start(bf16[40,2048]{1,0:T(8,128)(2,1)S(1)} %collective-permute-done.8.refs_1_), channel_id=1, source_target_pairs={{0,1},{1,0},{2,3},{3,2},{4,5},{5,4},{6,7},{7,6},{8,9},{9,8},{10,11... | collective-permute-start | bytes 491528 | tf_op jit(solution)/shard_map/ppermute | solution.py:325
  46.2 1.4 %collective-permute-start.14 = (bf16[40,2048]{1,0:T(8,128)(2,1)S(1)}, bf16[40,2048]{1,0:T(8,128)(2,1)S(1)}, u32[]{:S(2)}, u32[]{:S(2)}) collective-permute-start(bf16[40,2048]{1,0:T(8,128)(2,1)S(1)} %collective-permute-done.9.refs_2_), channel_id=1, source_target_pairs={{0,1},{1,0},{2,3},{3,2},{4,5},{5,4},{6,7},{7,6},{8,9},{9,8},{10,11... | collective-permute-start | bytes 491528 | tf_op jit(solution)/shard_map/ppermute | solution.py:325
  50.2 1.4 %collective-permute-start.15 = (bf16[160,384]{1,0:T(8,128)(2,1)S(1)}, bf16[160,384]{1,0:T(8,128)(2,1)S(1)}, u32[]{:S(2)}, u32[]{:S(2)}) collective-permute-start(bf16[160,384]{1,0:T(8,128)(2,1)S(1)} %shard_map.78.hidden_ref), channel_id=1, source_target_pairs={{0,1},{1,0},{2,3},{3,2},{4,5},{5,4},{6,7},{7,6},{8,9},{9,8},{10,11... | collective-permute-start | bytes 368648 | tf_op jit(solution)/shard_map/ppermute | solution.py:325
  53.0 11.6 %collective-permute-start.16 = (bf16[160,1024]{1,0:T(8,128)(2,1)S(1)}, bf16[160,1024]{1,0:T(8,128)(2,1)S(1)}, u32[]{:S(2)}, u32[]{:S(2)}) collective-permute-start(bf16[160,1024]{1,0:T(8,128)(2,1)S(1)} %get-tuple-element.72), channel_id=1, source_target_pairs={{0,2},{1,3},{2,0},{3,1},{4,6},{5,7},{6,4},{7,5},{8,10},{9,11},{10,... | collective-permute-start | bytes 983048 | tf_op jit(solution)/shard_map/ppermute | solution.py:322
  58.5 10.0 %collective-permute-start.21 = (bf16[64,1024]{1,0:T(8,128)(2,1)S(1)}, bf16[64,1024]{1,0:T(8,128)(2,1)S(1)}, u32[]{:S(2)}, u32[]{:S(2)}) collective-permute-start(bf16[64,1024]{1,0:T(8,128)(2,1)S(1)} %get-tuple-element.81), channel_id=1, source_target_pairs={{0,12},{4,0},{8,4},{12,8},{1,13},{5,1},{9,5},{13,9},{2,14},{6,2},{... | collective-permute-start | bytes 393224 | tf_op jit(solution)/shard_map/ppermute | solution.py:316
  59.8 17.1 %collective-permute-start.22 = (bf16[64,1024]{1,0:T(8,128)(2,1)S(1)}, bf16[64,1024]{1,0:T(8,128)(2,1)S(1)}, u32[]{:S(2)}, u32[]{:S(2)}) collective-permute-start(bf16[64,1024]{1,0:T(8,128)(2,1)S(1)} %get-tuple-element.83), channel_id=1, source_target_pairs={{0,8},{4,12},{8,0},{12,4},{1,9},{5,13},{9,1},{13,5},{2,10},{6,14},... | collective-permute-start | bytes 393224 | tf_op jit(solution)/shard_map/ppermute | solution.py:316
  61.0 15.9 %collective-permute-start.23 = (bf16[64,1024]{1,0:T(8,128)(2,1)S(1)}, bf16[64,1024]{1,0:T(8,128)(2,1)S(1)}, u32[]{:S(2)}, u32[]{:S(2)}) collective-permute-start(bf16[64,1024]{1,0:T(8,128)(2,1)S(1)} %get-tuple-element.82), channel_id=1, source_target_pairs={{0,4},{4,8},{8,12},{12,0},{1,5},{5,9},{9,13},{13,1},{2,6},{6,10},{... | collective-permute-start | bytes 393224 | tf_op jit(solution)/shard_map/ppermute | solution.py:316
  64.7 12.4 %collective-permute-start.17 = (bf16[40,1024]{1,0:T(8,128)(2,1)S(1)}, bf16[40,1024]{1,0:T(8,128)(2,1)S(1)}, u32[]{:S(2)}, u32[]{:S(2)}) collective-permute-start(bf16[40,1024]{1,0:T(8,128)(2,1)S(1)} %get-tuple-element.88), channel_id=1, source_target_pairs={{0,12},{4,0},{8,4},{12,8},{1,13},{5,1},{9,5},{13,9},{2,14},{6,2},{... | collective-permute-start | bytes 245768 | tf_op jit(solution)/shard_map/ppermute | solution.py:316
  67.4 11.8 %collective-permute-start.18 = (bf16[40,1024]{1,0:T(8,128)(2,1)S(1)}, bf16[40,1024]{1,0:T(8,128)(2,1)S(1)}, u32[]{:S(2)}, u32[]{:S(2)}) collective-permute-start(bf16[40,1024]{1,0:T(8,128)(2,1)S(1)} %get-tuple-element.87), channel_id=1, source_target_pairs={{0,8},{4,12},{8,0},{12,4},{1,9},{5,13},{9,1},{13,5},{2,10},{6,14},... | collective-permute-start | bytes 245768 | tf_op jit(solution)/shard_map/ppermute | solution.py:316
  68.5 10.6 %collective-permute-start.19 = (bf16[40,1024]{1,0:T(8,128)(2,1)S(1)}, bf16[40,1024]{1,0:T(8,128)(2,1)S(1)}, u32[]{:S(2)}, u32[]{:S(2)}) collective-permute-start(bf16[40,1024]{1,0:T(8,128)(2,1)S(1)} %get-tuple-element.86), channel_id=1, source_target_pairs={{0,4},{4,8},{8,12},{12,0},{1,5},{5,9},{9,13},{13,1},{2,6},{6,10},{... | collective-permute-start | bytes 245768 | tf_op jit(solution)/shard_map/ppermute | solution.py:316

commit v5 on v4

--- a/solution.py
+++ b/solution.py
@@ -269,7 +269,7 @@
 
 
 def unpack_kernel(weight_ref, *refs):
-    *piece_refs, out_ref = refs
+    *piece_refs, rest_ref, out_ref = refs
     rows = jnp.concatenate([ref[...].astype(jnp.float32) for ref in piece_refs])
     rows = rows.astype(jnp.bfloat16)
     weight = weight_ref[...]
@@ -277,19 +277,20 @@
     low = (weight - high.astype(jnp.float32)).astype(jnp.bfloat16)
     total = jnp.dot(high, rows, preferred_element_type=jnp.float32)
     total += jnp.dot(low, rows, preferred_element_type=jnp.float32)
-    out_ref[...] = total.astype(jnp.bfloat16)
-
-
-def unpack(weight, pieces):
+    out_ref[0] = total.astype(jnp.bfloat16)
+    out_ref[1:] = rest_ref[...]
+
+
+def unpack(weight, pieces, rest):
     rows, part = weight.shape[0], pieces[0].shape[1]
     return pl.pallas_call(
         unpack_kernel,
-        out_shape=jax.ShapeDtypeStruct((rows, part), jnp.bfloat16),
-        in_specs=in_vmem(1 + len(pieces)),
+        out_shape=jax.ShapeDtypeStruct((rest.shape[0] + 1, rows, part), jnp.bfloat16),
+        in_specs=in_vmem(2 + len(pieces)),
         out_specs=in_vmem(1)[0],
         compiler_params=params(),
         cost_estimate=cost(rows, weight.shape[1], part),
-    )(weight, *pieces)
+    )(weight, *pieces, rest)
 
 
 def per_device(
@@ -402,11 +403,7 @@
 
     old_table = placement[0]
     outs = []
-    for span in range(spans):
-        if span == 0:
-            weight = jnp.sum(jnp.where(hits, kept_gates[0][:, :, None], 0.0), axis=1)
-            outs.append(unpack(weight, returned[0]))
-            continue
+    for span in range(1, spans):
         serves = placement[span][:, None] == old_table[None, :]
         serving = jnp.min(jnp.where(serves, slot_range, ep), axis=1)
         served = jnp.sum(
@@ -418,7 +415,8 @@
             value = share * returned[span][at].astype(jnp.float32)
             combined = combined + jnp.where(share != 0, value, 0.0)
         outs.append(combined.astype(jnp.bfloat16))
-    return jnp.stack(outs)
+    weight = jnp.sum(jnp.where(hits, kept_gates[0][:, :, None], 0.0), axis=1)
+    return unpack(weight, returned[0], jnp.stack(outs))
 
 
 def solution(mesh):

time: 80.4 us -> 80.4 us (level)
  no operation moved by 1% of the time
where the time goes in v5:
time: 80.4 us; the launch traced here: 80.1 us
  starting transfers between devices  30.1 us (37%)
  waiting for transfers between devices  19.4 us (24%)
  Pallas kernels  18.1 us (23%)
  local copies, waits for them, and re-layouts  6.57 us (8%)
  other arithmetic  5.56 us (7%)
    ppermute x12, starting transfers between devices, along_ep(): return lax.ppermute(value, 'ep', [(i, (i + shift) % ep) for i in range(ep)])  24.7 us
    ppermute x12, waiting for transfers between devices, along_ep(): return lax.ppermute(value, 'ep', [(i, (i + shift) % ep) for i in range(ep)])  7.51 us
    ppermute x2, waiting for transfers between devices, along_chips(): return lax.ppermute(value, 'tp', pairs)  7.32 us
    pallas_call x1, Pallas kernels, first_up(): pl.pallas_call(first_up_kernel, out_shape=[jax.ShapeDtypeStruct((total, u...  5.71 us
    pallas_call x2, Pallas kernels, take(): pl.pallas_call(functools.partial(take_kernel, lead, side), out_shape=jax....  4.62 us
    ppermute x10, waiting for transfers between devices, along_cores(): return lax.ppermute(value, 'tp', [(i, i ^ 1) for i in range(tp)])  4.53 us
    pallas_call x2, Pallas kernels, down(): pl.pallas_call(down_kernel, out_shape=[jax.ShapeDtypeStruct((rows, part),...  3.2 us
    ppermute x2, starting transfers between devices, along_chips(): return lax.ppermute(value, 'tp', pairs)  3.11 us
  transfers between devices with their start and end apart: 24, of which 13 were waited for; matrix products, arithmetic and copies ran while one was open for 13% of the time, Pallas kernels for 19%

profile of v5, /device:TPU:0, one launch (start us, length us, event | category | flops | bytes accessed | tf_op | source)
XLA Modules:
  0.0 80.1 jit_solution(17624125231481079118)
XLA Ops:
  0.0 1.5 %shard_map.74 = bf16[64,2048]{1,0:T(8,128)(2,1)S(1)} custom-call(s32[2]{0:T(128)S(1)} %add.129.core_ref, bf16[2,64,4096]{2,1,0:T(8,128)(2,1)} %from_ref.2), custom_call_target="tpu_custom_call" | custom-call | flops 128 | bytes 128 | tf_op jit(solution)/shard_map/pallas_call | solution.py:86
  1.6 3.1 %collective-permute-start = (bf16[64,2048]{1,0:T(8,128)(2,1)S(1)}, bf16[64,2048]{1,0:T(8,128)(2,1)S(1)}, u32[]{:S(2)}, u32[]{:S(2)}) collective-permute-start(bf16[64,2048]{1,0:T(8,128)(2,1)S(1)} %shard_map.74), channel_id=1, source_target_pairs={{0,4},{4,8},{8,12},{12,0},{1,5},{5,9},{9,13},{13,1},{2,6},{6,10},{... | collective-permute-start | bytes 786440 | tf_op jit(solution)/shard_map/ppermute | solution.py:317
  4.7 2.6 %collective-permute-start.1 = (bf16[64,2048]{1,0:T(8,128)(2,1)S(1)}, bf16[64,2048]{1,0:T(8,128)(2,1)S(1)}, u32[]{:S(2)}, u32[]{:S(2)}) collective-permute-start(bf16[64,2048]{1,0:T(8,128)(2,1)S(1)} %shard_map.74), channel_id=1, source_target_pairs={{0,8},{4,12},{8,0},{12,4},{1,9},{5,13},{9,1},{13,5},{2,10},{6,14},... | collective-permute-start | bytes 786440 | tf_op jit(solution)/shard_map/ppermute | solution.py:317
  7.3 1.3 %collective-permute-start.2 = (bf16[64,2048]{1,0:T(8,128)(2,1)S(1)}, bf16[64,2048]{1,0:T(8,128)(2,1)S(1)}, u32[]{:S(2)}, u32[]{:S(2)}) collective-permute-start(bf16[64,2048]{1,0:T(8,128)(2,1)S(1)} %shard_map.74), channel_id=1, source_target_pairs={{0,12},{4,0},{8,4},{12,8},{1,13},{5,1},{9,5},{13,9},{2,14},{6,2},{... | collective-permute-start | bytes 786440 | tf_op jit(solution)/shard_map/ppermute | solution.py:317
  8.7 0.1 copy.35
  8.9 0.1 eq.135
  9.1 0.1 reshape.163
  9.4 0.2 convert_reduce_fusion.1
  9.6 0.1 and_select_fusion.3
  9.8 0.2 convert_reduce_fusion
  10.0 0.1 sub.29
  10.2 0.1 squeeze.20
  10.5 0.2 squeeze.19
  10.9 0.1 copy.44
  11.0 3.1 %shard_map.75 = bf16[2,384,1024]{2,1,0:T(8,128)(2,1)} custom-call(s32[2]{0:T(128)S(1)} %add.129.core_ref, bf16[1,3,384,4096]{3,2,1,0:T(8,128)(2,1)} %refs_6_), custom_call_target="tpu_custom_call" | custom-call | flops 768 | bytes 768 | tf_op jit(solution)/shard_map/pallas_call | solution.py:86
  14.1 1.0 %shard_map.73 = (bf16[40,4096]{1,0:T(8,128)(2,1)S(1)}, bf16[40,2048]{1,0:T(8,128)(2,1)S(1)}, bf16[40,2048]{1,0:T(8,128)(2,1)S(1)}, bf16[40,2048]{1,0:T(8,128)(2,1)S(1)}) custom-call(s32[2]{0:T(128)S(1)} %add.129.core_ref, bf16[160,64]{1,0:T(8,128)(2,1)S(1)} %bitcast.17, bf16[64,4096]{1,0:T(8,128)(2,1)S(1)} %get-tuple-element.85.rows_ref), custom_call_target="tpu_custom_call" | custom-call | flops 320 | bytes 320 | tf_op jit(solution)/shard_map/pallas_call | solution.py:124
  15.1 0.7 copy-done
  15.8 0.7 copy-done.1
  16.5 0.7 copy-done.2
  17.1 0.6 slice_bitcast_fusion.3
  17.7 0.8 lt.91
  18.6 0.9 %select_reduce_fusion.4 = s32[4]{0:T(128)S(1)} fusion(s32[4]{0:T(128)} %get-tuple-element.93, s32[4]{0:T(128)} %get-tuple-element.92), kind=kLoop, calls=%fused_computation.33 | loop fusion | flops 44 | bytes 48 | tf_op jit(solution)/shard_map/reduce_min | solution.py:408
  19.5 0.5 and_select_fusion
  20.0 0.7 broadcast_select_fusion
  20.7 0.6 fusion.13
  21.3 0.6 and_select_fusion.1
  21.9 0.1 eq.152
  22.1 0.8 %copy.46 = f32[1,64,2]{1,2,0:T(2,128)S(1)} copy(f32[1,64,2]{2,1,0:T(8,128)} %get-tuple-element.90) | data formatting | bytes 1024 | tf_op jit(solution)/shard_map/slice | solution.py:414
  23.0 0.7 select_reduce_fusion.1
  23.7 0.6 collective-permute-start.3
  24.4 0.5 collective-permute-start.5
  24.9 0.7 pad_add_fusion.columns_ref
  25.6 0.4 collective-permute-done.4.refs_4_
  26.0 0.2 collective-permute-done.5.refs_5_
  26.3 0.3 collective-permute-start.10
  26.6 5.5 %collective-permute-start.7 = (bf16[40,2048]{1,0:T(8,128)(2,1)}, bf16[40,2048]{1,0:T(8,128)(2,1)S(1)}, u32[]{:S(2)}, u32[]{:S(2)}) collective-permute-start(bf16[40,2048]{1,0:T(8,128)(2,1)} %copy-done.2), channel_id=1, source_target_pairs={{0,4},{4,8},{8,12},{12,0},{1,5},{5,9},{9,13},{13,1},{2,6},{6,10},{... | collective-permute-start | bytes 491528 | tf_op jit(solution)/shard_map/ppermute | solution.py:317
  32.1 2.1 %collective-permute-start.8 = (bf16[40,2048]{1,0:T(8,128)(2,1)}, bf16[40,2048]{1,0:T(8,128)(2,1)S(1)}, u32[]{:S(2)}, u32[]{:S(2)}) collective-permute-start(bf16[40,2048]{1,0:T(8,128)(2,1)} %copy-done.1), channel_id=1, source_target_pairs={{0,8},{4,12},{8,0},{12,4},{1,9},{5,13},{9,1},{13,5},{2,10},{6,14},... | collective-permute-start | bytes 491528 | tf_op jit(solution)/shard_map/ppermute | solution.py:317
  34.2 0.3 collective-permute-start.9
  34.5 5.7 %shard_map.76 = (bf16[256,384]{1,0:T(8,128)(2,1)S(1)}, bf16[4,2,384,1024]{3,2,1,0:T(8,128)(2,1)S(1)}, bf16[2,384,1024]{2,1,0:T(8,128)(2,1)S(1)}) custom-call(s32[2]{0:T(128)S(1)} %add.129.core_ref, s32[2,2]{1,0:T(2,128)S(1)} %pad_add_fusion.columns_ref, bf16[64,4096]{1,0:T(8,128)(2,1)S(1)} %get-tuple-element.84.own_ref, ...), custom_call_target="tpu_custom_call" | custom-call | flops 512 | bytes 512 | tf_op jit(solution)/shard_map/pallas_call | solution.py:214
  40.3 1.4 %collective-permute-done.11.other_hidden_ref = bf16[256,384]{1,0:T(8,128)(2,1)S(1)} collective-permute-done((bf16[256,384]{1,0:T(8,128)(2,1)S(1)}, bf16[256,384]{1,0:T(8,128)(2,1)S(1)}, u32[]{:S(2)}, u32[]{:S(2)}) %collective-permute-start.11) | collective-permute-done | bytes 196640 | tf_op jit(solution)/shard_map/ppermute | solution.py:326
  41.7 1.8 %shard_map.77 = (bf16[256,1024]{1,0:T(8,128)(2,1)S(1)}, bf16[256,1024]{1,0:T(8,128)(2,1)S(1)}) custom-call(s32[2,2]{1,0:T(2,128)S(1)} %pad_add_fusion.columns_ref, bf16[256,384]{1,0:T(8,128)(2,1)S(1)} %get-tuple-element.59.hidden_ref, bf16[256,384]{1,0:T(8,128)(2,1)S(1)} %collective-permute-done.11.other_hidden_ref, ...), custom_call_target="tpu_custom_call" | custom-call | flops 512 | bytes 512 | tf_op jit(solution)/shard_map/pallas_call | solution.py:261
  43.6 1.6 %collective-permute-start.20 = (bf16[256,1024]{1,0:T(8,128)(2,1)S(1)}, bf16[256,1024]{1,0:T(8,128)(2,1)S(1)}, u32[]{:S(2)}, u32[]{:S(2)}) collective-permute-start(bf16[256,1024]{1,0:T(8,128)(2,1)S(1)} %get-tuple-element.63), channel_id=1, source_target_pairs={{0,2},{1,3},{2,0},{3,1},{4,6},{5,7},{6,4},{7,5},{8,10},{9,11},{10,... | collective-permute-start | bytes 1572872 | tf_op jit(solution)/shard_map/ppermute | solution.py:323
  45.1 0.6 collective-permute-done.8.refs_1_
  45.7 0.5 collective-permute-start.13
  46.2 0.9 %collective-permute-done.12.refs_3_ = bf16[40,2048]{1,0:T(8,128)(2,1)S(1)} collective-permute-done((bf16[40,2048]{1,0:T(8,128)(2,1)S(1)}, bf16[40,2048]{1,0:T(8,128)(2,1)S(1)}, u32[]{:S(2)}, u32[]{:S(2)}) %collective-permute-start.12) | collective-permute-done | bytes 163872 | tf_op jit(solution)/shard_map/ppermute | solution.py:326
  47.1 0.2 collective-permute-done.13.refs_4_
  47.3 0.3 collective-permute-done.14.refs_5_
  47.6 2.6 %shard_map.78.hidden_ref = bf16[160,384]{1,0:T(8,128)(2,1)S(1)} custom-call(s32[2]{0:T(128)S(1)} %collective-permute-done.10.core_ref, bf16[40,4096]{1,0:T(8,128)(2,1)S(1)} %get-tuple-element.66.own_ref, bf16[40,2048]{1,0:T(8,128)(2,1)S(1)} %collective-permute-done.7.refs_0_, bf16[40,2048]{1,0:T(8,128)(2,1)S(1)} %collective-permute-done.8.refs_1_, ...), custom_call_target="tpu_custom_call" | custom-call | flops 320 | bytes 320 | tf_op jit(solution)/shard_map/pallas_call | solution.py:237
  50.2 0.3 collective-permute-start.15
  50.5 1.1 %collective-permute-done.15.other_hidden_ref = bf16[160,384]{1,0:T(8,128)(2,1)S(1)} collective-permute-done((bf16[160,384]{1,0:T(8,128)(2,1)S(1)}, bf16[160,384]{1,0:T(8,128)(2,1)S(1)}, u32[]{:S(2)}, u32[]{:S(2)}) %collective-permute-start.15) | collective-permute-done | bytes 122912 | tf_op jit(solution)/shard_map/ppermute | solution.py:326
  51.6 1.4 %shard_map.79 = (bf16[160,1024]{1,0:T(8,128)(2,1)S(1)}, bf16[160,1024]{1,0:T(8,128)(2,1)S(1)}) custom-call(s32[2,2]{1,0:T(2,128)S(1)} %pad_add_fusion.columns_ref, bf16[160,384]{1,0:T(8,128)(2,1)S(1)} %shard_map.78.hidden_ref, bf16[160,384]{1,0:T(8,128)(2,1)S(1)} %collective-permute-done.15.other_hidden_ref, ...), custom_call_target="tpu_custom_call" | custom-call | flops 320 | bytes 320 | tf_op jit(solution)/shard_map/pallas_call | solution.py:261
  53.0 1.6 %collective-permute-start.16 = (bf16[160,1024]{1,0:T(8,128)(2,1)S(1)}, bf16[160,1024]{1,0:T(8,128)(2,1)S(1)}, u32[]{:S(2)}, u32[]{:S(2)}) collective-permute-start(bf16[160,1024]{1,0:T(8,128)(2,1)S(1)} %get-tuple-element.72), channel_id=1, source_target_pairs={{0,2},{1,3},{2,0},{3,1},{4,6},{5,7},{6,4},{7,5},{8,10},{9,11},{10,... | collective-permute-start | bytes 983048 | tf_op jit(solution)/shard_map/ppermute | solution.py:323
  54.7 3.7 %collective-permute-done.20 = bf16[256,1024]{1,0:T(8,128)(2,1)S(1)} collective-permute-done((bf16[256,1024]{1,0:T(8,128)(2,1)S(1)}, bf16[256,1024]{1,0:T(8,128)(2,1)S(1)}, u32[]{:S(2)}, u32[]{:S(2)}) %collective-permute-start.20) | collective-permute-done | bytes 524320 | tf_op jit(solution)/shard_map/ppermute | solution.py:323
  58.4 0.1 add_convert_fusion.3
  58.5 1.3 %collective-permute-start.21 = (bf16[64,1024]{1,0:T(8,128)(2,1)S(1)}, bf16[64,1024]{1,0:T(8,128)(2,1)S(1)}, u32[]{:S(2)}, u32[]{:S(2)}) collective-permute-start(bf16[64,1024]{1,0:T(8,128)(2,1)S(1)} %get-tuple-element.81), channel_id=1, source_target_pairs={{0,12},{4,0},{8,4},{12,8},{1,13},{5,1},{9,5},{13,9},{2,14},{6,2},{... | collective-permute-start | bytes 393224 | tf_op jit(solution)/shard_map/ppermute | solution.py:317
  59.8 1.2 %collective-permute-start.22 = (bf16[64,1024]{1,0:T(8,128)(2,1)S(1)}, bf16[64,1024]{1,0:T(8,128)(2,1)S(1)}, u32[]{:S(2)}, u32[]{:S(2)}) collective-permute-start(bf16[64,1024]{1,0:T(8,128)(2,1)S(1)} %get-tuple-element.83), channel_id=1, source_target_pairs={{0,8},{4,12},{8,0},{12,4},{1,9},{5,13},{9,1},{13,5},{2,10},{6,14},... | collective-permute-start | bytes 393224 | tf_op jit(solution)/shard_map/ppermute | solution.py:317
  61.0 3.6 %collective-permute-done.16 = bf16[160,1024]{1,0:T(8,128)(2,1)S(1)} collective-permute-done((bf16[160,1024]{1,0:T(8,128)(2,1)S(1)}, bf16[160,1024]{1,0:T(8,128)(2,1)S(1)}, u32[]{:S(2)}, u32[]{:S(2)}) %collective-permute-start.16) | collective-permute-done | bytes 327712 | tf_op jit(solution)/shard_map/ppermute | solution.py:323
  64.7 2.6 %collective-permute-start.17 = (bf16[40,1024]{1,0:T(8,128)(2,1)S(1)}, bf16[40,1024]{1,0:T(8,128)(2,1)S(1)}, u32[]{:S(2)}, u32[]{:S(2)}) collective-permute-start(bf16[40,1024]{1,0:T(8,128)(2,1)S(1)} %get-tuple-element.88), channel_id=1, source_target_pairs={{0,12},{4,0},{8,4},{12,8},{1,13},{5,1},{9,5},{13,9},{2,14},{6,2},{... | collective-permute-start | bytes 245768 | tf_op jit(solution)/shard_map/ppermute | solution.py:317
  67.4 1.2 %collective-permute-start.18 = (bf16[40,1024]{1,0:T(8,128)(2,1)S(1)}, bf16[40,1024]{1,0:T(8,128)(2,1)S(1)}, u32[]{:S(2)}, u32[]{:S(2)}) collective-permute-start(bf16[40,1024]{1,0:T(8,128)(2,1)S(1)} %get-tuple-element.87), channel_id=1, source_target_pairs={{0,8},{4,12},{8,0},{12,4},{1,9},{5,13},{9,1},{13,5},{2,10},{6,14},... | collective-permute-start | bytes 245768 | tf_op jit(solution)/shard_map/ppermute | solution.py:317
  68.5 3.5 %collective-permute-start.19 = (bf16[40,1024]{1,0:T(8,128)(2,1)S(1)}, bf16[40,1024]{1,0:T(8,128)(2,1)S(1)}, u32[]{:S(2)}, u32[]{:S(2)}) collective-permute-start(bf16[40,1024]{1,0:T(8,128)(2,1)S(1)} %get-tuple-element.86), channel_id=1, source_target_pairs={{0,4},{4,8},{8,12},{12,0},{1,5},{5,9},{9,13},{13,1},{2,6},{6,10},{... | collective-permute-start | bytes 245768 | tf_op jit(solution)/shard_map/ppermute | solution.py:317
  72.1 4.9 %collective-permute-done.22 = bf16[64,1024]{1,0:T(8,128)(2,1)S(1)} collective-permute-done((bf16[64,1024]{1,0:T(8,128)(2,1)S(1)}, bf16[64,1024]{1,0:T(8,128)(2,1)S(1)}, u32[]{:S(2)}, u32[]{:S(2)}) %collective-permute-start.22) | collective-permute-done | bytes 131104 | tf_op jit(solution)/shard_map/ppermute | solution.py:317
  77.0 0.2 fusion.1.refs_4_
  77.2 2.0 %collective-permute-done.18.refs_2_ = bf16[40,1024]{1,0:T(8,128)(2,1)S(1)} collective-permute-done((bf16[40,1024]{1,0:T(8,128)(2,1)S(1)}, bf16[40,1024]{1,0:T(8,128)(2,1)S(1)}, u32[]{:S(2)}, u32[]{:S(2)}) %collective-permute-start.18) | collective-permute-done | bytes 81952 | tf_op jit(solution)/shard_map/ppermute | solution.py:317
  79.1 0.9 %shard_map.80 = bf16[2,64,1024]{2,1,0:T(8,128)(2,1)} custom-call(f32[64,160]{1,0:T(8,128)S(1)} %select_reduce_fusion.weight_ref, bf16[40,1024]{1,0:T(8,128)(2,1)S(1)} %get-tuple-element.89.refs_0_, bf16[40,1024]{1,0:T(8,128)(2,1)S(1)} %collective-permute-done.17.refs_1_, bf16[40,1024]{1,0:T(8,128)(2,1)S(1)} %collective-permute-done.18.refs_2_, ...), custom_call_target="tpu_custom_call" | custom-call | flops 128 | bytes 128 | tf_op jit(solution)/shard_map/pallas_call | solution.py:286
  (60 shorter events, 1.5 us)
Async XLA Ops:
  0.0 8.6 %copy-start.3 = (bf16[2,64,4096]{2,1,0:T(8,128)(2,1)S(1)}, bf16[2,64,4096]{2,1,0:T(8,128)(2,1)}, u32[]{:S(2)}) copy-start(bf16[2,64,4096]{2,1,0:T(8,128)(2,1)} %from_ref.2) | copy-start | bytes 3145732
  0.0 8.7 %copy-start.5 = (s32[2,64,2]{1,2,0:T(2,128)S(1)}, s32[2,64,2]{1,2,0:T(2,128)}, u32[]{:S(2)}) copy-start(s32[2,64,2]{1,2,0:T(2,128)} %param.8) | copy-start | bytes 3076
  0.0 9.0 %copy-start.6 = (s32[2,64,2]{1,2,0:T(2,128)S(1)}, s32[2,64,2]{1,2,0:T(2,128)}, u32[]{:S(2)}) copy-start(s32[2,64,2]{1,2,0:T(2,128)} %param.10) | copy-start | bytes 3076
  0.0 9.3 %copy-start.4 = (s32[2,4]{1,0:T(2,128)S(1)}, s32[2,4]{1,0:T(2,128)}, u32[]{:S(2)}) copy-start(s32[2,4]{1,0:T(2,128)} %param.11) | copy-start | bytes 100
  0.0 9.7 %copy-start.8 = (s32[4]{0:T(128)S(1)}, s32[4]{0:T(128)}, u32[]{:S(2)}) copy-start(s32[4]{0:T(128)} %param.12) | copy-start | bytes 52
  1.6 22.2 %collective-permute-start = (bf16[64,2048]{1,0:T(8,128)(2,1)S(1)}, bf16[64,2048]{1,0:T(8,128)(2,1)S(1)}, u32[]{:S(2)}, u32[]{:S(2)}) collective-permute-start(bf16[64,2048]{1,0:T(8,128)(2,1)S(1)} %shard_map.74), channel_id=1, source_target_pairs={{0,4},{4,8},{8,12},{12,0},{1,5},{5,9},{9,13},{13,1},{2,6},{6,10},{... | collective-permute-start | bytes 786440 | tf_op jit(solution)/shard_map/ppermute | solution.py:317
  4.7 19.7 %collective-permute-start.1 = (bf16[64,2048]{1,0:T(8,128)(2,1)S(1)}, bf16[64,2048]{1,0:T(8,128)(2,1)S(1)}, u32[]{:S(2)}, u32[]{:S(2)}) collective-permute-start(bf16[64,2048]{1,0:T(8,128)(2,1)S(1)} %shard_map.74), channel_id=1, source_target_pairs={{0,8},{4,12},{8,0},{12,4},{1,9},{5,13},{9,1},{13,5},{2,10},{6,14},... | collective-permute-start | bytes 786440 | tf_op jit(solution)/shard_map/ppermute | solution.py:317
  7.3 17.1 %collective-permute-start.2 = (bf16[64,2048]{1,0:T(8,128)(2,1)S(1)}, bf16[64,2048]{1,0:T(8,128)(2,1)S(1)}, u32[]{:S(2)}, u32[]{:S(2)}) collective-permute-start(bf16[64,2048]{1,0:T(8,128)(2,1)S(1)} %shard_map.74), channel_id=1, source_target_pairs={{0,12},{4,0},{8,4},{12,8},{1,13},{5,1},{9,5},{13,9},{2,14},{6,2},{... | collective-permute-start | bytes 786440 | tf_op jit(solution)/shard_map/ppermute | solution.py:317
  11.0 7.5 %copy-start.7 = (f32[2,64,2]{1,2,0:T(2,128)S(1)}, f32[2,64,2]{1,2,0:T(2,128)}, u32[]{:S(2)}) copy-start(f32[2,64,2]{1,2,0:T(2,128)} %param.9) | copy-start | bytes 3076
  15.1 0.7 copy-start
  15.8 0.7 copy-start.1
  16.5 0.7 copy-start.2
  17.1 9.1 %collective-permute-start.6 = (bf16[2,384,1024]{2,1,0:T(8,128)(2,1)}, bf16[2,384,1024]{2,1,0:T(8,128)(2,1)S(1)}, u32[]{:S(2)}, u32[]{:S(2)}) collective-permute-start(bf16[2,384,1024]{2,1,0:T(8,128)(2,1)} %shard_map.75), channel_id=1, source_target_pairs={{0,1},{1,0},{2,3},{3,2},{4,5},{5,4},{6,7},{7,6},{8,9},{9,8},{10,11... | collective-permute-start | bytes 4718600 | tf_op jit(solution)/shard_map/ppermute | solution.py:326
  23.7 1.9 %collective-permute-start.3 = (bf16[64,2048]{1,0:T(8,128)(2,1)S(1)}, bf16[64,2048]{1,0:T(8,128)(2,1)}, u32[]{:S(2)}, u32[]{:S(2)}) collective-permute-start(bf16[64,2048]{1,0:T(8,128)(2,1)S(1)} %collective-permute-done.refs_0_), channel_id=1, source_target_pairs={{0,1},{1,0},{2,3},{3,2},{4,5},{5,4},{6,7},{7,6},{8,9},{9,8},{10,11... | collective-permute-start | bytes 786440 | tf_op jit(solution)/shard_map/ppermute | solution.py:326
  24.4 1.7 %collective-permute-start.4 = (bf16[64,2048]{1,0:T(8,128)(2,1)S(1)}, bf16[64,2048]{1,0:T(8,128)(2,1)}, u32[]{:S(2)}, u32[]{:S(2)}) collective-permute-start(bf16[64,2048]{1,0:T(8,128)(2,1)S(1)} %collective-permute-done.1.refs_1_), channel_id=1, source_target_pairs={{0,1},{1,0},{2,3},{3,2},{4,5},{5,4},{6,7},{7,6},{8,9},{9,8},{10,11... | collective-permute-start | bytes 786440 | tf_op jit(solution)/shard_map/ppermute | solution.py:326
  24.4 1.9 %collective-permute-start.5 = (bf16[64,2048]{1,0:T(8,128)(2,1)S(1)}, bf16[64,2048]{1,0:T(8,128)(2,1)S(1)}, u32[]{:S(2)}, u32[]{:S(2)}) collective-permute-start(bf16[64,2048]{1,0:T(8,128)(2,1)S(1)} %collective-permute-done.2.refs_2_), channel_id=1, source_target_pairs={{0,1},{1,0},{2,3},{3,2},{4,5},{5,4},{6,7},{7,6},{8,9},{9,8},{10,11... | collective-permute-start | bytes 786440 | tf_op jit(solution)/shard_map/ppermute | solution.py:326
  26.3 14.0 %collective-permute-start.10 = (s32[2]{0:T(128)S(1)}, s32[2]{0:T(128)S(1)}, u32[]{:S(2)}, u32[]{:S(2)}) collective-permute-start(s32[2]{0:T(128)S(1)} %add.130), channel_id=1, source_target_pairs={{0,1},{1,0},{2,3},{3,2},{4,5},{5,4},{6,7},{7,6},{8,9},{9,8},{10,11... | collective-permute-start | bytes 32 | tf_op jit(solution)/shard_map/ppermute | solution.py:326
  26.6 18.5 %collective-permute-start.7 = (bf16[40,2048]{1,0:T(8,128)(2,1)}, bf16[40,2048]{1,0:T(8,128)(2,1)S(1)}, u32[]{:S(2)}, u32[]{:S(2)}) collective-permute-start(bf16[40,2048]{1,0:T(8,128)(2,1)} %copy-done.2), channel_id=1, source_target_pairs={{0,4},{4,8},{8,12},{12,0},{1,5},{5,9},{9,13},{13,1},{2,6},{6,10},{... | collective-permute-start | bytes 491528 | tf_op jit(solution)/shard_map/ppermute | solution.py:317
  32.1 13.6 %collective-permute-start.8 = (bf16[40,2048]{1,0:T(8,128)(2,1)}, bf16[40,2048]{1,0:T(8,128)(2,1)S(1)}, u32[]{:S(2)}, u32[]{:S(2)}) collective-permute-start(bf16[40,2048]{1,0:T(8,128)(2,1)} %copy-done.1), channel_id=1, source_target_pairs={{0,8},{4,12},{8,0},{12,4},{1,9},{5,13},{9,1},{13,5},{2,10},{6,14},... | collective-permute-start | bytes 491528 | tf_op jit(solution)/shard_map/ppermute | solution.py:317
  34.2 11.5 %collective-permute-start.9 = (bf16[40,2048]{1,0:T(8,128)(2,1)}, bf16[40,2048]{1,0:T(8,128)(2,1)S(1)}, u32[]{:S(2)}, u32[]{:S(2)}) collective-permute-start(bf16[40,2048]{1,0:T(8,128)(2,1)} %copy-done), channel_id=1, source_target_pairs={{0,12},{4,0},{8,4},{12,8},{1,13},{5,1},{9,5},{13,9},{2,14},{6,2},{... | collective-permute-start | bytes 491528 | tf_op jit(solution)/shard_map/ppermute | solution.py:317
  40.2 1.5 %collective-permute-start.11 = (bf16[256,384]{1,0:T(8,128)(2,1)S(1)}, bf16[256,384]{1,0:T(8,128)(2,1)S(1)}, u32[]{:S(2)}, u32[]{:S(2)}) collective-permute-start(bf16[256,384]{1,0:T(8,128)(2,1)S(1)} %get-tuple-element.59.hidden_ref), channel_id=1, source_target_pairs={{0,1},{1,0},{2,3},{3,2},{4,5},{5,4},{6,7},{7,6},{8,9},{9,8},{10,11... | collective-permute-start | bytes 589832 | tf_op jit(solution)/shard_map/ppermute | solution.py:326
  43.6 14.8 %collective-permute-start.20 = (bf16[256,1024]{1,0:T(8,128)(2,1)S(1)}, bf16[256,1024]{1,0:T(8,128)(2,1)S(1)}, u32[]{:S(2)}, u32[]{:S(2)}) collective-permute-start(bf16[256,1024]{1,0:T(8,128)(2,1)S(1)} %get-tuple-element.63), channel_id=1, source_target_pairs={{0,2},{1,3},{2,0},{3,1},{4,6},{5,7},{6,4},{7,5},{8,10},{9,11},{10,... | collective-permute-start | bytes 1572872 | tf_op jit(solution)/shard_map/ppermute | solution.py:323
  45.7 1.4 %collective-permute-start.12 = (bf16[40,2048]{1,0:T(8,128)(2,1)S(1)}, bf16[40,2048]{1,0:T(8,128)(2,1)S(1)}, u32[]{:S(2)}, u32[]{:S(2)}) collective-permute-start(bf16[40,2048]{1,0:T(8,128)(2,1)S(1)} %collective-permute-done.7.refs_0_), channel_id=1, source_target_pairs={{0,1},{1,0},{2,3},{3,2},{4,5},{5,4},{6,7},{7,6},{8,9},{9,8},{10,11... | collective-permute-start | bytes 491528 | tf_op jit(solution)/shard_map/ppermute | solution.py:326
  45.7 1.6 %collective-permute-start.13 = (bf16[40,2048]{1,0:T(8,128)(2,1)S(1)}, bf16[40,2048]{1,0:T(8,128)(2,1)S(1)}, u32[]{:S(2)}, u32[]{:S(2)}) collective-permute-start(bf16[40,2048]{1,0:T(8,128)(2,1)S(1)} %collective-permute-done.8.refs_1_), channel_id=1, source_target_pairs={{0,1},{1,0},{2,3},{3,2},{4,5},{5,4},{6,7},{7,6},{8,9},{9,8},{10,11... | collective-permute-start | bytes 491528 | tf_op jit(solution)/shard_map/ppermute | solution.py:326
  46.2 1.4 %collective-permute-start.14 = (bf16[40,2048]{1,0:T(8,128)(2,1)S(1)}, bf16[40,2048]{1,0:T(8,128)(2,1)S(1)}, u32[]{:S(2)}, u32[]{:S(2)}) collective-permute-start(bf16[40,2048]{1,0:T(8,128)(2,1)S(1)} %collective-permute-done.9.refs_2_), channel_id=1, source_target_pairs={{0,1},{1,0},{2,3},{3,2},{4,5},{5,4},{6,7},{7,6},{8,9},{9,8},{10,11... | collective-permute-start | bytes 491528 | tf_op jit(solution)/shard_map/ppermute | solution.py:326
  50.2 1.4 %collective-permute-start.15 = (bf16[160,384]{1,0:T(8,128)(2,1)S(1)}, bf16[160,384]{1,0:T(8,128)(2,1)S(1)}, u32[]{:S(2)}, u32[]{:S(2)}) collective-permute-start(bf16[160,384]{1,0:T(8,128)(2,1)S(1)} %shard_map.78.hidden_ref), channel_id=1, source_target_pairs={{0,1},{1,0},{2,3},{3,2},{4,5},{5,4},{6,7},{7,6},{8,9},{9,8},{10,11... | collective-permute-start | bytes 368648 | tf_op jit(solution)/shard_map/ppermute | solution.py:326
  53.0 11.6 %collective-permute-start.16 = (bf16[160,1024]{1,0:T(8,128)(2,1)S(1)}, bf16[160,1024]{1,0:T(8,128)(2,1)S(1)}, u32[]{:S(2)}, u32[]{:S(2)}) collective-permute-start(bf16[160,1024]{1,0:T(8,128)(2,1)S(1)} %get-tuple-element.72), channel_id=1, source_target_pairs={{0,2},{1,3},{2,0},{3,1},{4,6},{5,7},{6,4},{7,5},{8,10},{9,11},{10,... | collective-permute-start | bytes 983048 | tf_op jit(solution)/shard_map/ppermute | solution.py:323
  58.5 10.0 %collective-permute-start.21 = (bf16[64,1024]{1,0:T(8,128)(2,1)S(1)}, bf16[64,1024]{1,0:T(8,128)(2,1)S(1)}, u32[]{:S(2)}, u32[]{:S(2)}) collective-permute-start(bf16[64,1024]{1,0:T(8,128)(2,1)S(1)} %get-tuple-element.81), channel_id=1, source_target_pairs={{0,12},{4,0},{8,4},{12,8},{1,13},{5,1},{9,5},{13,9},{2,14},{6,2},{... | collective-permute-start | bytes 393224 | tf_op jit(solution)/shard_map/ppermute | solution.py:317
  59.8 17.1 %collective-permute-start.22 = (bf16[64,1024]{1,0:T(8,128)(2,1)S(1)}, bf16[64,1024]{1,0:T(8,128)(2,1)S(1)}, u32[]{:S(2)}, u32[]{:S(2)}) collective-permute-start(bf16[64,1024]{1,0:T(8,128)(2,1)S(1)} %get-tuple-element.83), channel_id=1, source_target_pairs={{0,8},{4,12},{8,0},{12,4},{1,9},{5,13},{9,1},{13,5},{2,10},{6,14},... | collective-permute-start | bytes 393224 | tf_op jit(solution)/shard_map/ppermute | solution.py:317
  61.0 16.0 %collective-permute-start.23 = (bf16[64,1024]{1,0:T(8,128)(2,1)S(1)}, bf16[64,1024]{1,0:T(8,128)(2,1)S(1)}, u32[]{:S(2)}, u32[]{:S(2)}) collective-permute-start(bf16[64,1024]{1,0:T(8,128)(2,1)S(1)} %get-tuple-element.82), channel_id=1, source_target_pairs={{0,4},{4,8},{8,12},{12,0},{1,5},{5,9},{9,13},{13,1},{2,6},{6,10},{... | collective-permute-start | bytes 393224 | tf_op jit(solution)/shard_map/ppermute | solution.py:317
  64.7 12.4 %collective-permute-start.17 = (bf16[40,1024]{1,0:T(8,128)(2,1)S(1)}, bf16[40,1024]{1,0:T(8,128)(2,1)S(1)}, u32[]{:S(2)}, u32[]{:S(2)}) collective-permute-start(bf16[40,1024]{1,0:T(8,128)(2,1)S(1)} %get-tuple-element.88), channel_id=1, source_target_pairs={{0,12},{4,0},{8,4},{12,8},{1,13},{5,1},{9,5},{13,9},{2,14},{6,2},{... | collective-permute-start | bytes 245768 | tf_op jit(solution)/shard_map/ppermute | solution.py:317
  67.4 11.8 %collective-permute-start.18 = (bf16[40,1024]{1,0:T(8,128)(2,1)S(1)}, bf16[40,1024]{1,0:T(8,128)(2,1)S(1)}, u32[]{:S(2)}, u32[]{:S(2)}) collective-permute-start(bf16[40,1024]{1,0:T(8,128)(2,1)S(1)} %get-tuple-element.87), channel_id=1, source_target_pairs={{0,8},{4,12},{8,0},{12,4},{1,9},{5,13},{9,1},{13,5},{2,10},{6,14},... | collective-permute-start | bytes 245768 | tf_op jit(solution)/shard_map/ppermute | solution.py:317
  68.5 10.6 %collective-permute-start.19 = (bf16[40,1024]{1,0:T(8,128)(2,1)S(1)}, bf16[40,1024]{1,0:T(8,128)(2,1)S(1)}, u32[]{:S(2)}, u32[]{:S(2)}) collective-permute-start(bf16[40,1024]{1,0:T(8,128)(2,1)S(1)} %get-tuple-element.86), channel_id=1, source_target_pairs={{0,4},{4,8},{8,12},{12,0},{1,5},{5,9},{9,13},{13,1},{2,6},{6,10},{... | collective-permute-start | bytes 245768 | tf_op jit(solution)/shard_map/ppermute | solution.py:317
